TPU v7x, 32 devices: a whole 2x2x4 slice. The times are simulated.
32 devices in a mesh: seq: 8 (over z, x), tp: 4 (over y, core).
Axes of the slice: x: 2, y: 2, z: 4, core: 2. Of those that a mesh axis runs over, the one named last changes fastest.
Arguments:
- tokens: bfloat16 [1024, 2048], P('seq'), may hold values from -6 to 6
- out_grad: bfloat16 [1024, 2048], P('seq', 'tp'), may hold values from -6 to 6
- modality: int32 [1024], P('seq'), may hold values from 0 to 2
- segment: int32 [1024], replicated, may hold values from 0 to 2, as said below
- w_in: float32 [3, 2048, 2, 4096], P(None, 'seq', None, 'tp'), may hold values from -0.125 to 0.125
- w_x: float32 [3, 4096, 160], P(None, ('tp', 'seq')), may hold values from -0.09375 to 0.09375
- w_dt: float32 [3, 128, 4096], P(None, 'seq', 'tp'), may hold values from -0.5 to 0.5
- w_out: float32 [3, 4096, 2048], P(None, 'tp', 'seq'), may hold values from -0.09375 to 0.09375
- channel: float32 [25, 4096], P(None, ('tp', 'seq'))
- norm_gain: float32 [2048], P('seq'), may hold values from 0.3 to 3.2
- moment_in: float32 [3, 2048, 2, 4096], P(None, 'seq', None, 'tp')
- moment_x: float32 [3, 4096, 160], P(None, ('tp', 'seq'))
- moment_dt: float32 [3, 128, 4096], P(None, 'seq', 'tp')
- moment_out: float32 [3, 4096, 2048], P(None, 'tp', 'seq')
- moment_channel: float32 [25, 4096], P(None, ('tp', 'seq'))
- moment_gain: float32 [2048], P('seq')
- square_in: float32 [3, 2048, 2, 4096], P(None, 'seq', None, 'tp')
- square_x: float32 [3, 4096, 160], P(None, ('tp', 'seq'))
- square_dt: float32 [3, 128, 4096], P(None, 'seq', 'tp')
- square_out: float32 [3, 4096, 2048], P(None, 'tp', 'seq')
- square_channel: float32 [25, 4096], P(None, ('tp', 'seq'))
- square_gain: float32 [2048], P('seq')
- average_in: float32 [3, 2048, 2, 4096], P(None, 'seq', None, 'tp'), may hold values from -0.125 to 0.125
- average_x: float32 [3, 4096, 160], P(None, ('tp', 'seq')), may hold values from -0.09375 to 0.09375
- average_dt: float32 [3, 128, 4096], P(None, 'seq', 'tp'), may hold values from -0.5 to 0.5
- average_out: float32 [3, 4096, 2048], P(None, 'tp', 'seq'), may hold values from -0.09375 to 0.09375
- average_channel: float32 [25, 4096], P(None, ('tp', 'seq')), may hold values from -6 to 6
- average_gain: float32 [2048], P('seq'), may hold values from 0.5 to 1.5
Outputs:
- layer_out: float32 [1024, 2048], P('seq', 'tp')
- tokens_grad: float32 [1024, 2048], P('seq', 'tp')
- new_w_in: float32 [3, 2048, 2, 4096], P(None, 'seq', None, 'tp')
- new_w_x: float32 [3, 4096, 160], P(None, ('tp', 'seq'))
- new_w_dt: float32 [3, 128, 4096], P(None, 'seq', 'tp')
- new_w_out: float32 [3, 4096, 2048], P(None, 'tp', 'seq')
- new_channel: float32 [25, 4096], P(None, ('tp', 'seq'))
- new_norm_gain: float32 [2048], P('seq')
- new_moment_in: float32 [3, 2048, 2, 4096], P(None, 'seq', None, 'tp')
- new_moment_x: float32 [3, 4096, 160], P(None, ('tp', 'seq'))
- new_moment_dt: float32 [3, 128, 4096], P(None, 'seq', 'tp')
- new_moment_out: float32 [3, 4096, 2048], P(None, 'tp', 'seq')
- new_moment_channel: float32 [25, 4096], P(None, ('tp', 'seq'))
- new_moment_gain: float32 [2048], P('seq')
- new_square_in: float32 [3, 2048, 2, 4096], P(None, 'seq', None, 'tp')
- new_square_x: float32 [3, 4096, 160], P(None, ('tp', 'seq'))
- new_square_dt: float32 [3, 128, 4096], P(None, 'seq', 'tp')
- new_square_out: float32 [3, 4096, 2048], P(None, 'tp', 'seq')
- new_square_channel: float32 [25, 4096], P(None, ('tp', 'seq'))
- new_square_gain: float32 [2048], P('seq')
- new_average_in: float32 [3, 2048, 2, 4096], P(None, 'seq', None, 'tp')
- new_average_x: float32 [3, 4096, 160], P(None, ('tp', 'seq'))
- new_average_dt: float32 [3, 128, 4096], P(None, 'seq', 'tp')
- new_average_out: float32 [3, 4096, 2048], P(None, 'tp', 'seq')
- new_average_channel: float32 [25, 4096], P(None, ('tp', 'seq'))
- new_average_gain: float32 [2048], P('seq')
Inputs may be any that keep to these rules, and one draw needn't show every extreme that they name: segment never falls along the stream and starts at 0; document 1 begins within the first 128 tokens and document 2 within the last 128.
All inputs are finite; a program needn't handle non-finite values.
Results may differ from a plain program's by a relative error of at most 0.0075.
The roundings to bfloat16 on the way count: a program that leaves them out, or rounds other values in their place, can miss the bound.
Values may be sent and summed in bfloat16 or wider, within the bound.
A program may use at most 384 MiB of HBM per device.

v0:
```python
import jax
import jax.numpy as jnp
from jax import lax
from jax.sharding import PartitionSpec as P

D = 2048
R = 128
N = 16
K = 4
M = 3
STEP = 10


EPSILON = 1e-05
BETA_ONE = 0.9
BETA_TWO = 0.999
ADAM_EPSILON = 1e-06
WEIGHT_DECAY = 0.01
MATRIX_RATE = 0.25
CHANNEL_RATE = 0.7
GAIN_RATE = 0.35
AVERAGE_KEEP = 0.8
PRECISE = lax.Precision.HIGHEST


def passed_along(value, axis, steps):
    count = lax.axis_size(axis)
    leading, last = (max(0, -steps), min(count, count - steps))
    return lax.ppermute(value, axis, [(source, source + steps) for source in range(leading, last)])


def prefix(x, axis, combine, identity, reverse):
    devices, place = (lax.axis_size(axis), lax.axis_index(axis))
    everything = jax.tree.map(lambda part: lax.all_gather(part, axis), x)
    start = jax.tree.map(
        lambda part, zero: jnp.broadcast_to(jnp.asarray(zero, part.dtype), part.shape), x, identity
    )

    def lap(k, before):
        at = devices - 1 - k if reverse else k
        reached = at > place if reverse else at < place
        new = combine(before, jax.tree.map(lambda part: part[at], everything))
        return jax.tree.map(lambda a, b: jnp.where(reached, a, b), new, before)

    return lax.fori_loop(0, devices, lap, start)


def silu_grad(operand):
    sigmoid_of = jax.nn.sigmoid(operand)
    return sigmoid_of * (1.0 + operand * (1.0 - sigmoid_of))


def combine(earlier, following):
    return (earlier[0] * following[0], following[0] * earlier[1] + following[1])


def masked_dot(mask_cols, operand, stacked):
    running = mask_cols[:, 0:1] * jnp.dot(operand, stacked[0], preferred_element_type=jnp.float32)
    for modal_index in range(1, M):
        running = running + mask_cols[:, modal_index : modal_index + 1] * jnp.dot(
            operand, stacked[modal_index], preferred_element_type=jnp.float32
        )
    return running


def masked_back(mask_cols, operand, stacked):
    contract = (((1,), (1,)), ((), ()))
    running = mask_cols[:, 0:1] * lax.dot_general(
        operand, stacked[0], contract, preferred_element_type=jnp.float32
    )
    for modal_index in range(1, M):
        running = running + mask_cols[:, modal_index : modal_index + 1] * lax.dot_general(
            operand, stacked[modal_index], contract, preferred_element_type=jnp.float32
        )
    return running


def masked_outer(mask_low, operand, cotangent):
    contract = (((0,), (0,)), ((), ()))
    return jnp.stack(
        [
            lax.dot_general(
                operand * mask_low[:, modal_index : modal_index + 1],
                cotangent,
                contract,
                preferred_element_type=jnp.float32,
            )
            for modal_index in range(M)
        ]
    )


def adam_parts(gradient, moment, square):
    moment_new = BETA_ONE * moment + (1.0 - BETA_ONE) * gradient
    square_new = BETA_TWO * square + (1.0 - BETA_TWO) * gradient * gradient
    adam_ratio = (
        moment_new
        / (1.0 - BETA_ONE**STEP)
        / (jnp.sqrt(square_new / (1.0 - BETA_TWO**STEP)) + ADAM_EPSILON)
    )
    return (moment_new, square_new, adam_ratio)


def local(
    tokens,
    out_grad,
    modality,
    segment,
    w_in,
    w_x,
    w_dt,
    w_out,
    channel,
    norm_gain,
    moment_in,
    moment_x,
    moment_dt,
    moment_out,
    moment_channel,
    moment_gain,
    square_in,
    square_x,
    square_dt,
    square_out,
    square_channel,
    square_gain,
    average_in,
    average_x,
    average_dt,
    average_out,
    average_channel,
    average_gain,
):
    tok_local = tokens.shape[0]
    width_tp = out_grad.shape[1]
    lowered = (
        w_in.astype(jnp.bfloat16),
        w_x.astype(jnp.bfloat16),
        w_dt.astype(jnp.bfloat16),
        w_out.astype(jnp.bfloat16),
    )
    stack_in, stack_x, stack_dt, stack_out = (
        lax.all_gather(lowered[0], "seq", axis=1, tiled=True),
        lax.all_gather(lowered[1], "seq", axis=1, tiled=True),
        lax.all_gather(lowered[2], "seq", axis=1, tiled=True),
        lax.all_gather(lowered[3], "seq", axis=2, tiled=True),
    )
    chan_full, gain_full = (
        lax.all_gather(channel, "seq", axis=1, tiled=True),
        lax.all_gather(norm_gain, "seq", axis=0, tiled=True),
    )
    inner_width = stack_out.shape[1]
    in_flat = stack_in.reshape(M, D, 2 * inner_width)
    seq_index = lax.axis_index("seq")
    tp_index = lax.axis_index("tp")
    start_row = seq_index * tok_local
    seg_local = lax.dynamic_slice(segment, (start_row,), (tok_local,))
    seg_before = lax.dynamic_slice(
        jnp.concatenate([jnp.full((K - 1,), -1, jnp.int32), segment]),
        (start_row,),
        (tok_local + K - 1,),
    )
    seg_after = lax.dynamic_slice(
        jnp.concatenate([segment, jnp.full((K - 1,), -2, jnp.int32)]),
        (start_row,),
        (tok_local + K - 1,),
    )
    mask_cols = (modality[:, None] == jnp.arange(M, dtype=jnp.int32)[None, :]).astype(jnp.float32)
    mask_low = mask_cols.astype(jnp.bfloat16)
    tokens_wide = tokens.astype(jnp.float32)
    inv_root = lax.rsqrt(jnp.mean(tokens_wide * tokens_wide, axis=-1, keepdims=True) + EPSILON)
    scaled = tokens_wide * inv_root
    normed = (scaled * gain_full[None, :]).astype(jnp.bfloat16)
    projected = masked_dot(mask_cols, normed, in_flat)
    inner_act = projected[:, :inner_width].astype(jnp.bfloat16)
    gate_pre = projected[:, inner_width:]
    rim_rows = passed_along(inner_act[tok_local - (K - 1) :], "seq", 1)
    extended = jnp.concatenate([rim_rows, inner_act], axis=0).astype(jnp.float32)
    conv_pre = jnp.broadcast_to(chan_full[K][None, :], (tok_local, inner_width))
    same_docs = []
    for tap_index in range(K):
        same_doc = (seg_before[tap_index : tap_index + tok_local] == seg_local).astype(jnp.float32)[
            :, None
        ]
        same_docs.append(same_doc)
        conv_pre = (
            conv_pre
            + chan_full[tap_index][None, :] * extended[tap_index : tap_index + tok_local] * same_doc
        )
    activated = jax.nn.silu(conv_pre).astype(jnp.bfloat16)
    act_wide = activated.astype(jnp.float32)
    params_x = lax.psum(masked_dot(mask_cols, activated, stack_x), "tp")
    low_rank = params_x[:, :R].astype(jnp.bfloat16)
    input_b = params_x[:, R : R + N]
    output_c = params_x[:, R + N :]
    step_pre = masked_dot(mask_cols, low_rank, stack_dt) + jnp.dot(
        mask_cols, chan_full[K + 2 : K + 2 + M], precision=PRECISE
    )
    step_size = jax.nn.softplus(step_pre)
    decay_base = -jnp.exp(chan_full[K + 2 + M :])
    keep_flag = (seg_before[K - 2 : K - 2 + tok_local] == seg_local).astype(jnp.float32)
    decay_rate = jnp.exp(step_size[:, None, :] * decay_base[None]) * keep_flag[:, None, None]
    drive_term = (step_size * act_wide)[:, None, :] * input_b[:, :, None]
    decay_cum, local_state = lax.associative_scan(combine, (decay_rate, drive_term), axis=0)
    unit_pair = (jnp.ones_like(decay_base), jnp.zeros_like(decay_base))
    carry_in = prefix((decay_cum[-1], local_state[-1]), "seq", combine, unit_pair, False)[1]
    hidden_state = local_state + decay_cum * carry_in[None]
    mixed_out = (
        jnp.einsum("tn,tne->te", output_c, hidden_state, precision=PRECISE)
        + chan_full[K + 1][None, :] * act_wide
    )
    gate_act = jax.nn.silu(gate_pre)
    gated_out = (mixed_out * gate_act).astype(jnp.bfloat16)
    out_share = lax.psum_scatter(
        masked_dot(mask_cols, gated_out, stack_out), "tp", scatter_dimension=1, tiled=True
    )
    layer_out = lax.dynamic_slice_in_dim(tokens_wide, tp_index * width_tp, width_tp, 1) + out_share
    grad_full = lax.all_gather(out_grad, "tp", axis=1, tiled=True)
    d_gated = masked_back(mask_cols, grad_full, stack_out)
    grad_out = masked_outer(mask_low, gated_out, grad_full)
    d_mixed = d_gated * gate_act
    d_gate = d_gated * mixed_out * silu_grad(gate_pre)
    grad_skip = jnp.sum(d_mixed * act_wide, axis=0)
    d_out_c = jnp.einsum("te,tne->tn", d_mixed, hidden_state, precision=PRECISE)
    d_hidden = output_c[:, :, None] * d_mixed[:, None, :]
    decay_next = jnp.concatenate([decay_rate[1:], jnp.ones_like(decay_rate[:1])], axis=0)
    suffix_cum, local_back = lax.associative_scan(
        combine, (decay_next, d_hidden), reverse=True, axis=0
    )
    device_pair = (decay_rate[0] * suffix_cum[0], decay_rate[0] * local_back[0])
    carry_back = prefix(device_pair, "seq", combine, unit_pair, True)[1]
    back_state = local_back + suffix_cum * carry_back[None]
    state_prev = jnp.concatenate([carry_in[None], hidden_state[:-1]], axis=0)
    d_log = back_state * state_prev * decay_rate
    d_drive_sum = jnp.einsum("tne,tn->te", back_state, input_b, precision=PRECISE)
    d_step_size = jnp.sum(d_log * decay_base[None], axis=1) + act_wide * d_drive_sum
    grad_decay = decay_base * jnp.einsum("tne,te->ne", d_log, step_size, precision=PRECISE)
    d_in_b = jnp.einsum("tne,te->tn", back_state, step_size * act_wide, precision=PRECISE)
    d_step = (d_step_size * jax.nn.sigmoid(step_pre)).astype(jnp.bfloat16)
    d_step_wide = d_step.astype(jnp.float32)
    grad_bias = jnp.dot(mask_cols.T, d_step_wide, precision=PRECISE)
    grad_dt = masked_outer(mask_low, low_rank, d_step)
    d_low = masked_back(mask_cols, d_step, stack_dt)
    d_params = lax.psum(jnp.concatenate([d_low, d_in_b, d_out_c], axis=1), "tp").astype(
        jnp.bfloat16
    )
    grad_x = masked_outer(mask_low, activated, d_params)
    d_activ = (
        d_mixed * chan_full[K + 1][None, :]
        + step_size * d_drive_sum
        + masked_back(mask_cols, d_params, stack_x)
    )
    d_conv = (d_activ * silu_grad(conv_pre)).astype(jnp.bfloat16)
    rim_back = passed_along(d_conv[: K - 1], "seq", -1)
    d_conv_wide = d_conv.astype(jnp.float32)
    conv_after = jnp.concatenate([d_conv, rim_back], axis=0).astype(jnp.float32)
    d_inner = jnp.zeros((tok_local, inner_width), jnp.float32)
    grad_taps = []
    for tap_index in range(K):
        grad_taps.append(
            jnp.sum(
                d_conv_wide * extended[tap_index : tap_index + tok_local] * same_docs[tap_index],
                axis=0,
            )
        )
        offset = K - 1 - tap_index
        same_after = (seg_after[offset : offset + tok_local] == seg_local).astype(jnp.float32)[
            :, None
        ]
        d_inner = (
            d_inner
            + chan_full[tap_index][None, :] * conv_after[offset : offset + tok_local] * same_after
        )
    grad_conv_b = jnp.sum(d_conv_wide, axis=0)
    d_proj = jnp.concatenate([d_inner, d_gate], axis=1).astype(jnp.bfloat16)
    grad_in = masked_outer(mask_low, normed, d_proj).reshape(M, D, 2, inner_width)
    d_normed = lax.psum(masked_back(mask_cols, d_proj, in_flat), "tp")
    grad_gain = jnp.sum(d_normed * scaled, axis=0)
    d_scaled = d_normed * gain_full[None, :]
    d_tokens = inv_root * (d_scaled - scaled * jnp.mean(d_scaled * scaled, axis=-1, keepdims=True))
    tokens_grad = out_grad.astype(jnp.float32) + lax.dynamic_slice_in_dim(
        d_tokens, tp_index * width_tp, width_tp, 1
    )
    grad_channel = jnp.concatenate(
        [jnp.stack(grad_taps), grad_conv_b[None], grad_skip[None], grad_bias, grad_decay], axis=0
    )
    reduced = (
        lax.psum_scatter(grad_in, "seq", scatter_dimension=1, tiled=True),
        lax.psum_scatter(grad_x, "seq", scatter_dimension=1, tiled=True),
        lax.psum_scatter(grad_dt, "seq", scatter_dimension=1, tiled=True),
        lax.psum_scatter(grad_out, "seq", scatter_dimension=2, tiled=True),
        lax.psum_scatter(grad_channel, "seq", scatter_dimension=1, tiled=True),
        lax.psum_scatter(grad_gain, "seq", scatter_dimension=0, tiled=True),
    )
    weights = (w_in, w_x, w_dt, w_out, channel, norm_gain)
    moments = (moment_in, moment_x, moment_dt, moment_out, moment_channel, moment_gain)
    squares = (square_in, square_x, square_dt, square_out, square_channel, square_gain)
    averages = (average_in, average_x, average_dt, average_out, average_channel, average_gain)
    adam_all = [
        adam_parts(reduced[position], moments[position], squares[position]) for position in range(6)
    ]
    directions = [adam_all[position][2] + WEIGHT_DECAY * weights[position] for position in range(4)]
    weight_sums = jnp.stack(
        [
            jnp.sum(
                weights[position] * weights[position], axis=tuple(range(1, weights[position].ndim))
            )
            for position in range(4)
        ]
    )
    direction_sums = jnp.stack(
        [
            jnp.sum(
                directions[position] * directions[position],
                axis=tuple(range(1, directions[position].ndim)),
            )
            for position in range(4)
        ]
    )
    totals = lax.psum(jnp.stack([weight_sums, direction_sums]), ("seq", "tp"))
    trust_ratio = jnp.sqrt(totals[0]) / jnp.sqrt(totals[1])
    new_weights = []
    new_averages = []
    for position in range(6):
        weight = weights[position]
        if position < 4:
            updated = (
                weight
                - MATRIX_RATE
                * trust_ratio[position].reshape((M,) + (1,) * (weight.ndim - 1))
                * directions[position]
            )
        elif position == 4:
            updated = weight - CHANNEL_RATE * adam_all[position][2]
        else:
            updated = weight - GAIN_RATE * adam_all[position][2]
        new_weights.append(updated)
        new_averages.append(AVERAGE_KEEP * averages[position] + (1.0 - AVERAGE_KEEP) * updated)
    return (
        layer_out,
        tokens_grad,
        new_weights[0],
        new_weights[1],
        new_weights[2],
        new_weights[3],
        new_weights[4],
        new_weights[5],
        adam_all[0][0],
        adam_all[1][0],
        adam_all[2][0],
        adam_all[3][0],
        adam_all[4][0],
        adam_all[5][0],
        adam_all[0][1],
        adam_all[1][1],
        adam_all[2][1],
        adam_all[3][1],
        adam_all[4][1],
        adam_all[5][1],
        new_averages[0],
        new_averages[1],
        new_averages[2],
        new_averages[3],
        new_averages[4],
        new_averages[5],
    )


def solution(mesh):
    placed = (
        P("seq", None),
        P("seq", "tp"),
        P("seq"),
        P(),
        P(None, "seq", None, "tp"),
        P(None, ("tp", "seq"), None),
        P(None, "seq", "tp"),
        P(None, "tp", "seq"),
        P(None, ("tp", "seq")),
        P("seq"),
        P(None, "seq", None, "tp"),
        P(None, ("tp", "seq"), None),
        P(None, "seq", "tp"),
        P(None, "tp", "seq"),
        P(None, ("tp", "seq")),
        P("seq"),
        P(None, "seq", None, "tp"),
        P(None, ("tp", "seq"), None),
        P(None, "seq", "tp"),
        P(None, "tp", "seq"),
        P(None, ("tp", "seq")),
        P("seq"),
        P(None, "seq", None, "tp"),
        P(None, ("tp", "seq"), None),
        P(None, "seq", "tp"),
        P(None, "tp", "seq"),
        P(None, ("tp", "seq")),
        P("seq"),
    )
    return jax.shard_map(
        local,
        mesh=mesh,
        in_specs=placed,
        out_specs=(
            P("seq", "tp"),
            P("seq", "tp"),
            P(None, "seq", None, "tp"),
            P(None, ("tp", "seq"), None),
            P(None, "seq", "tp"),
            P(None, "tp", "seq"),
            P(None, ("tp", "seq")),
            P("seq"),
            P(None, "seq", None, "tp"),
            P(None, ("tp", "seq"), None),
            P(None, "seq", "tp"),
            P(None, "tp", "seq"),
            P(None, ("tp", "seq")),
            P("seq"),
            P(None, "seq", None, "tp"),
            P(None, ("tp", "seq"), None),
            P(None, "seq", "tp"),
            P(None, "tp", "seq"),
            P(None, ("tp", "seq")),
            P("seq"),
            P(None, "seq", None, "tp"),
            P(None, ("tp", "seq"), None),
            P(None, "seq", "tp"),
            P(None, "tp", "seq"),
            P(None, ("tp", "seq")),
            P("seq"),
        ),
        check_vma=False,
    )
```

profile of v0, /device:TPU:0, one launch (start us, length us, event | category | flops | bytes accessed | tf_op | source)
XLA Modules:
  0.0 3326.5 jit_solution(12276884144016850486)
XLA Ops:
  10.6 12.0 multiply_reduce_fusion.3
  22.7 22.5 all-gather
  45.2 31.5 all_gather.35
  87.2 46.2 %all_gather.39 = bf16[3,128,1024]{2,1,0:T(8,128)(2,1)S(1)} all-gather(bf16[3,16,1024]{2,1,0:T(8,128)(2,1)S(1)} %convert_element_type.94), channel_id=1, replica_groups=mesh['seq'=8,'tp'=4] {'seq'}, dimensions={1}, use_global_device_ids=true | all-gather | bytes 884736 | tf_op jit(solution)/shard_map/all_gather | solution.py:145
  133.3 47.9 %all_gather.38 = bf16[3,1024,160]{1,2,0:T(8,128)(2,1)S(1)} all-gather(bf16[3,128,160]{1,2,0:T(8,128)(2,1)S(1)} %convert_element_type.93), channel_id=1, replica_groups=mesh['seq'=8,'tp'=4] {'seq'}, dimensions={1}, use_global_device_ids=true | all-gather | bytes 1105920 | tf_op jit(solution)/shard_map/all_gather | solution.py:144
  181.2 43.3 %all-gather.6.cloned.1.call-done = bf16[3,1024,2048]{2,1,0:T(8,128)(2,1)} async-done(((bf16[3,1024,256]{2,1,0:T(8,128)(2,1)}), bf16[3,1024,2048]{2,1,0:T(8,128)(2,1)}) %all-gather.6.cloned.1.call-update) | async-done | bytes 12582928 | tf_op jit(solution)/shard_map/all_gather | solution.py:146
  229.0 476.3 %all-gather.4.cloned.1.call-done = bf16[3,2048,2,1024]{3,2,1,0:T(2,128)(2,1)} async-done(((bf16[3,256,2,1024]{3,2,1,0:T(2,128)(2,1)}), bf16[3,2048,2,1024]{3,2,1,0:T(2,128)(2,1)}) %all-gather.4.cloned.1.call-update) | async-done | bytes 25165840 | tf_op jit(solution)/shard_map/all_gather | solution.py:143
  705.3 20.3 fusion.135
  776.4 31.8 all-reduce.64.cloned.1.call-done
  833.2 10.5 reverse_add_fusion
  949.8 12.1 pad.228
  963.6 12.1 pad.214
  975.7 18.7 pad.215
  994.4 12.1 pad.229
  1031.1 35.6 %pad.216 = f32[128,16,1024]{2,1,0:T(8,128)} pad(f32[64,16,1024]{2,1,0:T(8,128)} %pad_maximum_fusion.4, f32[]{:T(128)} %constant.79.clone.1), padding=0_1_1x0_0_0x0_0_0 | pad | bytes 12582916 | tf_op jit(solution)/shard_map/pad | solution.py:227
  1066.7 35.6 %pad.217 = f32[128,16,1024]{2,1,0:T(8,128)} pad(f32[64,16,1024]{2,1,0:T(8,128)} %add.686, f32[]{:T(128)} %constant.79.clone.1), padding=1_0_1x0_0_0x0_0_0 | pad | bytes 12582916 | tf_op jit(solution)/shard_map/pad | solution.py:227
  1102.3 35.6 %pad.231 = f32[128,16,1024]{2,1,0:T(8,128)} pad(f32[64,16,1024]{2,1,0:T(8,128)} %add.694, f32[]{:T(128)} %constant.79.clone.1), padding=1_0_1x0_0_0x0_0_0 | pad | bytes 12582916 | tf_op jit(solution)/shard_map/pad | solution.py:227
  1142.7 35.7 %pad.230 = f32[128,16,1024]{2,1,0:T(8,128)} pad(f32[64,16,1024]{2,1,0:T(8,128)} %concatenate.127, f32[]{:T(128)} %constant.79.clone.1), padding=0_1_1x0_0_0x0_0_0 | pad | bytes 12582916 | tf_op jit(solution)/shard_map/pad | solution.py:227
  1178.4 12.1 add.695
  1192.2 12.3 add.688
  1208.6 10.4 slice_add_fusion
  1325.3 12.1 pad.200
  1339.1 12.1 pad.186
  1351.3 18.7 pad.187
  1370.0 12.1 pad.201
  1402.1 31.6 all_gather.45
  1433.7 31.2 all_gather.44
  1470.0 35.6 %pad.202 = f32[128,16,1024]{2,1,0:T(8,128)} pad(f32[64,16,1024]{2,1,0:T(8,128)} %pad_maximum_fusion.3, f32[]{:T(128)} %constant.79.clone.1), padding=0_1_1x0_0_0x0_0_0 | pad | bytes 12582916 | tf_op jit(solution)/shard_map/pad | solution.py:204
  1510.4 35.6 %pad.188 = f32[128,16,1024]{2,1,0:T(8,128)} pad(f32[64,16,1024]{2,1,0:T(8,128)} %pad_maximum_fusion.2, f32[]{:T(128)} %constant.79.clone.1), padding=0_1_1x0_0_0x0_0_0 | pad | bytes 12582916 | tf_op jit(solution)/shard_map/pad | solution.py:204
  1546.0 35.5 %pad.189 = f32[128,16,1024]{2,1,0:T(8,128)} pad(f32[64,16,1024]{2,1,0:T(8,128)} %add.651, f32[]{:T(128)} %constant.79.clone.1), padding=1_0_1x0_0_0x0_0_0 | pad | bytes 12582916 | tf_op jit(solution)/shard_map/pad | solution.py:204
  1582.4 31.4 all_gather.41
  1613.8 35.6 %pad.203 = f32[128,16,1024]{2,1,0:T(8,128)} pad(f32[64,16,1024]{2,1,0:T(8,128)} %add.659, f32[]{:T(128)} %constant.79.clone.1), padding=1_0_1x0_0_0x0_0_0 | pad | bytes 12582916 | tf_op jit(solution)/shard_map/pad | solution.py:204
  1650.3 31.2 all_gather.40
  1682.0 12.7 multiply_add_fusion.1
  1704.8 11.1 multiply_reduce_fusion
  1743.8 11.9 fusion.67
  1757.5 10.9 psum.29
  1826.5 25.4 copy.61
  1860.2 25.4 copy.62
  1893.8 25.4 copy.63
  1919.2 36.1 %copy_bitcast_fusion = f32[2048,3,2,1024]{3,2,1,0:T(2,128)} fusion(f32[1,2048,2,1024]{3,2,1,0:T(2,128)} %copy.63, f32[1,2048,2,1024]{3,2,1,0:T(2,128)} %copy.62, f32[1,2048,2,1024]{3,2,1,0:T(2,128)} %copy.61), kind=kLoop, calls=%fused_computation.7 | loop fusion | flops 25165824 | bytes 100663296
  1955.2 61.8 %reshape.164 = f32[2048,6144]{1,0:T(8,128)} reshape(f32[2048,3,2,1024]{3,2,1,0:T(2,128)} %copy_bitcast_fusion) | data formatting | bytes 100663296
  2034.6 23.1 all-reduce.60
  2065.8 362.4 %reduce-scatter.16.cloned.1.call-done = f32[3,1024,256]{2,1,0:T(8,128)} async-done(((f32[3,1024,2048]{2,1,0:T(8,128)}), f32[3,1024,256]{2,1,0:T(8,128)}) %reduce-scatter.16.cloned.1.call-update) | async-done | bytes 3145744 | tf_op jit(solution)/shard_map/reduce_scatter | solution.py:291
  2435.7 785.8 %reduce-scatter.20.cloned.1.call-done = f32[256,6144]{1,0:T(8,128)} async-done(((f32[2048,6144]{1,0:T(8,128)}), f32[256,6144]{1,0:T(8,128)}) %reduce-scatter.20.cloned.1.call-update) | async-done | bytes 6291472
  3230.4 24.5 multiply_reduce_fusion.2
  3256.7 39.7 %psum.31 = f32[2,4,3]{2,1,0:T(4,128)S(1)} all-reduce(f32[2,4,3]{2,1,0:T(4,128)S(1)} %pad_maximum_fusion.29), channel_id=1, replica_groups=mesh['seq'=8,'tp'=4] {'seq','tp'}, use_global_device_ids=true, to_apply=%region_23.24 | all-reduce | flops 24 | bytes 192 | tf_op jit(solution)/shard_map/psum | solution.py:320
  3296.6 16.1 multiply_add_fusion.2
  (625 shorter events, 539.9 us)
Async XLA Ops:
  7.2 217.3 %all-gather.6.cloned.1.call-start = ((), (), s32[]{:S(2)}) async-start(), calls=%async_computation.8 | async-start | bytes 14155776 | tf_op jit(solution)/shard_map/all_gather | solution.py:146
  10.5 34.7 %copy-start.114 = (f32[25,128]{1,0:T(8,128)S(1)}, f32[25,128]{1,0:T(8,128)}, u32[]{:S(2)}) copy-start(f32[25,128]{1,0:T(8,128)} %param.40) | copy-start | bytes 38404
  10.5 66.2 %copy-start.146 = (s32[1024]{0:T(1024)S(1)}, s32[1024]{0:T(1024)}, u32[]{:S(2)}) copy-start(s32[1024]{0:T(1024)} %param.35) | copy-start | bytes 12292
  10.5 694.8 %all-gather.4.cloned.1.call-start = ((), (), s32[]{:S(2)}) async-start(), calls=%async_computation.6 | async-start | bytes 28311552 | tf_op jit(solution)/shard_map/all_gather | solution.py:143
  22.6 54.3 %copy-start.4 = (bf16[128,2048]{1,0:T(8,128)(2,1)S(1)}, bf16[128,2048]{1,0:T(8,128)(2,1)}, u32[]{:S(2)}) copy-start(bf16[128,2048]{1,0:T(8,128)(2,1)} %param.32) | copy-start | bytes 1572868
  22.6 54.5 %copy-start.92 = (bf16[128,512]{1,0:T(8,128)(2,1)S(1)}, bf16[128,512]{1,0:T(8,128)(2,1)}, u32[]{:S(2)}) copy-start(bf16[128,512]{1,0:T(8,128)(2,1)} %param.33) | copy-start | bytes 393220
  22.6 62.0 %copy-start.147 = (s32[128]{0:T(128)S(1)}, s32[128]{0:T(128)}, u32[]{:S(2)}) copy-start(s32[128]{0:T(128)} %param.34) | copy-start | bytes 1540
  22.6 785.6 %all-reduce.64.cloned.1.call-start = ((), (), s32[]{:S(2)}) async-start(), calls=%async_computation.7 | async-start | bytes 163840 | tf_op jit(solution)/shard_map/psum | solution.py:192
  45.2 718.5 %copy-start.61 = (f32[8,1,256]{2,1,0:T(1,128)}, f32[8,1,256]{2,1,0:T(1,128)S(1)}, u32[]{:S(2)}) copy-start(f32[8,1,256]{2,1,0:T(1,128)S(1)} %all-gather) | copy-start | bytes 24580
  76.8 152.2 %copy-start.88 = (f32[25,1024]{1,0:T(8,128)}, f32[25,1024]{1,0:T(8,128)S(1)}, u32[]{:S(2)}) copy-start(f32[25,1024]{1,0:T(8,128)S(1)} %all_gather.35) | copy-start | bytes 307204
  83.9 686.9 %copy-start.36 = (bf16[128,2048]{1,0:T(8,128)(2,1)}, bf16[128,2048]{1,0:T(8,128)(2,1)S(1)}, u32[]{:S(2)}) copy-start(bf16[128,2048]{1,0:T(8,128)(2,1)S(1)} %all_gather.43) | copy-start | bytes 1572868
  83.9 679.8 %copy-start.112 = (f32[128]{0:T(128)}, f32[128]{0:T(128)S(1)}, u32[]{:S(2)}) copy-start(f32[128]{0:T(128)S(1)} %add_rsqrt_fusion) | copy-start | bytes 1540
  84.6 732.8 %copy-start.121 = (f32[128]{0:T(128)}, f32[128]{0:T(128)S(1)}, u32[]{:S(2)}) copy-start(f32[128]{0:T(128)S(1)} %get-tuple-element.455) | copy-start | bytes 1540
  84.6 733.0 %copy-start.128 = (f32[128]{0:T(128)}, f32[128]{0:T(128)S(1)}, u32[]{:S(2)}) copy-start(f32[128]{0:T(128)S(1)} %get-tuple-element.454) | copy-start | bytes 1540
  84.6 733.3 %copy-start.125 = (f32[128]{0:T(128)}, f32[128]{0:T(128)S(1)}, u32[]{:S(2)}) copy-start(f32[128]{0:T(128)S(1)} %get-tuple-element.453) | copy-start | bytes 1540
  85.3 685.5 %copy-start.159 = (f32[128]{0:T(128)}, f32[128]{0:T(128)S(1)}, u32[]{:S(2)}) copy-start(f32[128]{0:T(128)S(1)} %get-tuple-element.468) | copy-start | bytes 1540
  85.3 685.5 %copy-start.160 = (f32[128]{0:T(128)}, f32[128]{0:T(128)S(1)}, u32[]{:S(2)}) copy-start(f32[128]{0:T(128)S(1)} %get-tuple-element.470) | copy-start | bytes 1540
  85.3 685.5 %copy-start.161 = (f32[128]{0:T(128)}, f32[128]{0:T(128)S(1)}, u32[]{:S(2)}) copy-start(f32[128]{0:T(128)S(1)} %get-tuple-element.471) | copy-start | bytes 1540
  85.3 734.2 %copy-start.144 = (f32[128]{0:T(128)}, f32[128]{0:T(128)S(1)}, u32[]{:S(2)}) copy-start(f32[128]{0:T(128)S(1)} %get-tuple-element.469) | copy-start | bytes 1540
  85.9 684.9 %copy-start.132 = (f32[1,1024]{1,0:T(1,128)}, f32[1,1024]{1,0:T(1,128)S(1)}, u32[]{:S(2)}) copy-start(f32[1,1024]{1,0:T(1,128)S(1)} %get-tuple-element.434) | copy-start | bytes 12292
  85.9 684.9 %copy-start.134 = (f32[1,1024]{1,0:T(1,128)}, f32[1,1024]{1,0:T(1,128)S(1)}, u32[]{:S(2)}) copy-start(f32[1,1024]{1,0:T(1,128)S(1)} %get-tuple-element.435) | copy-start | bytes 12292
  85.9 684.9 %copy-start.136 = (f32[1,1024]{1,0:T(1,128)}, f32[1,1024]{1,0:T(1,128)S(1)}, u32[]{:S(2)}) copy-start(f32[1,1024]{1,0:T(1,128)S(1)} %get-tuple-element.436) | copy-start | bytes 12292
  85.9 684.9 %copy-start.138 = (f32[1,1024]{1,0:T(1,128)}, f32[1,1024]{1,0:T(1,128)S(1)}, u32[]{:S(2)}) copy-start(f32[1,1024]{1,0:T(1,128)S(1)} %get-tuple-element.437) | copy-start | bytes 12292
  85.9 733.6 %copy-start.82 = (f32[16,1024]{1,0:T(8,128)}, f32[16,1024]{1,0:T(8,128)S(1)}, u32[]{:S(2)}) copy-start(f32[16,1024]{1,0:T(8,128)S(1)} %fusion.109) | copy-start | bytes 196612
  133.3 684.6 %copy-start.40 = (bf16[3,128,1024]{2,1,0:T(8,128)(2,1)}, bf16[3,128,1024]{2,1,0:T(8,128)(2,1)S(1)}, u32[]{:S(2)}) copy-start(bf16[3,128,1024]{2,1,0:T(8,128)(2,1)S(1)} %all_gather.39) | copy-start | bytes 2359300
  181.2 593.6 %copy-start.42 = (bf16[3,1024,160]{1,2,0:T(8,128)(2,1)}, bf16[3,1024,160]{1,2,0:T(8,128)(2,1)S(1)}, u32[]{:S(2)}) copy-start(bf16[3,1024,160]{1,2,0:T(8,128)(2,1)S(1)} %all_gather.38) | copy-start | bytes 2949124
  766.5 4.1 collective-permute-start
  774.3 35.9 %copy-start.70 = (f32[128,1024]{1,0:T(8,128)}, f32[128,1024]{1,0:T(8,128)S(1)}, u32[]{:S(2)}) copy-start(f32[128,1024]{1,0:T(8,128)S(1)} %get-tuple-element.342) | copy-start | bytes 1572868
  774.3 43.9 %copy-start.23 = (bf16[128,1024]{1,0:T(8,128)(2,1)}, bf16[128,1024]{1,0:T(8,128)(2,1)S(1)}, u32[]{:S(2)}) copy-start(bf16[128,1024]{1,0:T(8,128)(2,1)S(1)} %get-tuple-element.343) | copy-start | bytes 786436
  775.8 1253.8 %reduce-scatter.18.cloned.1.call-start = ((), (), s32[]{:S(2)}) async-start(), calls=%async_computation.14 | async-start | bytes 147456 | tf_op jit(solution)/shard_map/reduce_scatter | solution.py:292
  1398.8 34.8 %copy-start.108 = (f32[1,16,1024]{2,1,0:T(8,128)S(1)}, f32[1,16,1024]{2,1,0:T(8,128)}, u32[]{:S(2)}) copy-start(f32[1,16,1024]{2,1,0:T(8,128)} %get-tuple-element.362) | copy-start | bytes 196612
  1398.8 66.0 %copy-start.64 = (f32[16,1024]{1,0:T(8,128)S(1)}, f32[16,1024]{1,0:T(8,128)}, u32[]{:S(2)}) copy-start(f32[16,1024]{1,0:T(8,128)} %custom-call.1) | copy-start | bytes 196612
  1398.8 66.4 %copy-start.99 = (f32[1,16,1024]{2,1,0:T(8,128)S(1)}, f32[1,16,1024]{2,1,0:T(8,128)}, u32[]{:S(2)}) copy-start(f32[1,16,1024]{2,1,0:T(8,128)} %get-tuple-element.363) | copy-start | bytes 196612
  1470.0 35.7 %slice-start.4 = ((f32[128,16,1024]{2,1,0:T(8,128)}), f32[1,16,1024]{2,1,0:T(8,128)S(1)}, s32[]{:S(2)}) async-start(f32[128,16,1024]{2,1,0:T(8,128)} %copy-done.6), calls=%async_computation.20 | async-start | bytes 131072 | tf_op jit(solution)/shard_map/slice | solution.py:204
  1613.8 67.7 %copy-start.58 = (f32[16,1024]{1,0:T(8,128)S(1)}, f32[16,1024]{1,0:T(8,128)}, u32[]{:S(2)}) copy-start(f32[16,1024]{1,0:T(8,128)} %custom-call) | copy-start | bytes 196612
  1773.7 5.5 collective-permute-start.1
  1778.7 252.5 %all-reduce.66.cloned.1.call-start = ((), (), s32[]{:S(2)}) async-start(), calls=%async_computation.10 | async-start | bytes 2097152 | tf_op jit(solution)/shard_map/psum | solution.py:277
  1799.8 261.7 %reduce-scatter.14.cloned.1.call-start = ((), (), s32[]{:S(2)}) async-start(), calls=%async_computation.12 | async-start | bytes 1769472 | tf_op jit(solution)/shard_map/reduce_scatter | solution.py:290
  1801.8 261.8 %reduce-scatter.12.cloned.1.call-start = ((), (), s32[]{:S(2)}) async-start(), calls=%async_computation.11 | async-start | bytes 2211840 | tf_op jit(solution)/shard_map/reduce_scatter | solution.py:289
  1804.3 623.9 %reduce-scatter.16.cloned.1.call-start = ((), (), s32[]{:S(2)}) async-start(), calls=%async_computation.13 | async-start | bytes 28311552 | tf_op jit(solution)/shard_map/reduce_scatter | solution.py:291
  1817.2 1404.4 %reduce-scatter.20.cloned.1.call-start = ((), (), s32[]{:S(2)}) async-start(), calls=%async_computation.15 | async-start | bytes 56623104
  2017.1 1237.8 %reduce-scatter.10.cloned.1.call-start = ((), (), s32[]{:S(2)}) async-start(), calls=%async_computation.9 | async-start | bytes 1310720 | tf_op jit(solution)/shard_map/reduce_scatter | solution.py:214
  2025.5 32.8 copy-start.93
  2029.5 30.7 copy-start.157
  2029.5 30.7 copy-start.158
  2029.5 34.1 %copy-start.68 = (f32[3,128,160]{1,2,0:T(8,128)S(1)}, f32[3,128,160]{1,2,0:T(8,128)}, u32[]{:S(2)}) copy-start(f32[3,128,160]{1,2,0:T(8,128)} %param.37) | copy-start | bytes 737284
  2034.6 393.6 %copy-start.14 = (f32[3,1024,256]{2,1,0:T(8,128)S(1)}, f32[3,1024,256]{2,1,0:T(8,128)}, u32[]{:S(2)}) copy-start(f32[3,1024,256]{2,1,0:T(8,128)} %param.39) | copy-start | bytes 9437188
  2065.8 369.9 %copy-start.152 = (f32[3]{0:T(128)S(1)}, f32[3]{0:T(128)}, u32[]{:S(2)}) copy-start(f32[3]{0:T(128)} %get-tuple-element.372) | copy-start | bytes 40
  (136 other events, 999.6 us)
Sparse Core Ops, SparseCore 0:
  10.7 213.7 all-gather.5
  226.6 478.6 all-gather.3
  775.9 32.2 all-reduce.63
  1778.8 62.6 reduce-scatter.17
  1844.4 35.0 all-reduce.65
  1883.4 65.8 reduce-scatter.13
  1953.8 66.2 reduce-scatter.11
  2024.0 404.1 reduce-scatter.15
  2432.1 789.4 reduce-scatter.19
  3224.1 24.0 reduce-scatter.9
where the time goes:
time: 3360 us; the launch traced here: 3330 us
  waiting for transfers between devices  1700 us (51%)
  local copies, waits for them, and re-layouts  775 us (23%)
  other arithmetic  355 us (11%)
  blocking collectives  354 us (11%)
  matrix products  120 us (4%)
    unnamed x11, waiting for transfers between devices  786 us
    all_gather x1, waiting for transfers between devices, local(): lax.all_gather(lowered[0], 'seq', axis=1, tiled=True)  476 us
    reduce_scatter x1, waiting for transfers between devices, local(): lax.psum_scatter(grad_out, 'seq', scatter_dimension=2, tiled=True)  362 us
    pad x24, local copies, waits for them, and re-layouts, local(): lax.associative_scan(combine, (decay_rate, drive_term), axis=0)  257 us
    pad x24, local copies, waits for them, and re-layouts, local(): lax.associative_scan(combine, (decay_next, d_hidden), reverse=True, axis=0)  257 us
    all_gather x4, blocking collectives, prefix(): everything = jax.tree.map(lambda part: lax.all_gather(part, axis), x)  125 us
    unnamed x348, local copies, waits for them, and re-layouts  120 us
    another operation x3, local copies, waits for them, and re-layouts, masked_outer(): jnp.stack([lax.dot_general(operand * mask_low[:, modal_index:modal_index...  76.2 us
  transfers between devices with their start and end apart: 12, of which 6 were waited for; matrix products, arithmetic and copies ran while one was open for 10% of the time, Pallas kernels for 0%

commit v1 on v0

--- a/solution.py
+++ b/solution.py
@@ -1,6 +1,10 @@
+import functools
+
 import jax
 import jax.numpy as jnp
 from jax import lax
+from jax.experimental import pallas as pl
+from jax.experimental.pallas import tpu as pltpu
 from jax.sharding import PartitionSpec as P
 
 D = 2048
@@ -101,7 +105,7 @@
     return (moment_new, square_new, adam_ratio)
 
 
-def local(
+def generic_local(
     tokens,
     out_grad,
     modality,
@@ -366,6 +370,1066 @@
     )
 
 
+MESH = pl.DeviceIdType.MESH
+VMEM_LIMIT = 60 * 1024 * 1024
+LANES = 128
+F32 = jnp.float32
+BF16 = jnp.bfloat16
+NT = (((1,), (1,)), ((), ()))
+TN = (((0,), (0,)), ((), ()))
+
+
+def dot(a, b, dims=(((1,), (0,)), ((), ()))):
+    return lax.dot_general(a, b, dims, preferred_element_type=F32)
+
+
+def local_call(kernel, out_shape, n_in, scratch=(), cost=None):
+    return pl.pallas_call(
+        kernel,
+        out_shape=out_shape,
+        in_specs=[pl.BlockSpec(memory_space=pltpu.VMEM)] * n_in,
+        out_specs=jax.tree.map(lambda _: pl.BlockSpec(memory_space=pltpu.VMEM), out_shape),
+        scratch_shapes=list(scratch),
+        compiler_params=pltpu.CompilerParams(vmem_limit_bytes=VMEM_LIMIT),
+        cost_estimate=cost,
+    )
+
+
+def remote_call(kernel, out_shape, n_in, scratch, ident):
+    return pl.pallas_call(
+        kernel,
+        out_shape=out_shape,
+        in_specs=[pl.BlockSpec(memory_space=pltpu.VMEM)] * n_in,
+        out_specs=jax.tree.map(lambda _: pl.BlockSpec(memory_space=pltpu.VMEM), out_shape),
+        scratch_shapes=list(scratch),
+        compiler_params=pltpu.CompilerParams(
+            collective_id=ident, has_side_effects=True, vmem_limit_bytes=VMEM_LIMIT
+        ),
+    )
+
+
+def sds(shape, dtype=F32):
+    return jax.ShapeDtypeStruct(shape, dtype)
+
+
+def seq_copy(src, dst, send, recv, device):
+    return pltpu.make_async_remote_copy(
+        src_ref=src,
+        dst_ref=dst,
+        send_sem=send,
+        recv_sem=recv,
+        device_id=device,
+        device_id_type=MESH,
+    )
+
+
+def place(S, PN):
+    s, p = lax.axis_index("seq"), lax.axis_index("tp")
+    return s, p, lax.div(s, 2), lax.rem(s, 2)
+
+
+def greet_all(S, PN):
+    s, p = lax.axis_index("seq"), lax.axis_index("tp")
+    n = S * PN
+    me = s * PN + p
+    bar = pltpu.get_barrier_semaphore()
+
+    def greet(k, _):
+        j = lax.rem(me + k, n)
+        pl.semaphore_signal(
+            bar,
+            inc=1,
+            device_id={"seq": lax.div(j, PN), "tp": lax.rem(j, PN)},
+            device_id_type=MESH,
+        )
+        return 0
+
+    lax.fori_loop(1, n, greet, 0)
+    pl.semaphore_wait(bar, n - 1)
+
+
+class Spread:
+    def __init__(self, S, PN, own, buf, zs, zr, xs, xr, ys, yr, cs, cr, ls):
+        s, p, z, x = place(S, PN)
+        self.zn = S // 2
+        zn = self.zn
+        other_x = {"seq": 2 * z + 1 - x}
+        other_y = {"tp": lax.rem(p + 2, PN)}
+        other_c = {"tp": p + 1 - 2 * lax.rem(p, 2)}
+
+        def at(k, j):
+            return 2 * lax.rem(z - k + zn, zn) + (x if j == 0 else 1 - x)
+
+        self.local = pltpu.make_async_copy(own, buf.at[p, s], ls)
+        self.z = [
+            seq_copy(own, buf.at[p, s], zs.at[k], zr.at[k], {"seq": 2 * lax.rem(z + k, zn) + x})
+            for k in range(1, zn)
+        ]
+        self.x = []
+        self.y = {}
+        for k in range(zn):
+            src = own if k == 0 else buf.at[p, at(k, 0)]
+            self.x.append(seq_copy(src, buf.at[p, at(k, 0)], xs.at[k], xr.at[k], other_x))
+            for j in range(2):
+                src = own if (k == 0 and j == 0) else buf.at[p, at(k, j)]
+                self.y[k, j] = seq_copy(
+                    src, buf.at[p, at(k, j)], ys.at[2 * k + j], yr.at[2 * k + j], other_y
+                )
+        q = lax.rem(p + 2, PN)
+        self.c = [
+            seq_copy(buf.at[p], buf.at[p], cs.at[0], cr.at[0], other_c),
+            seq_copy(buf.at[q], buf.at[q], cs.at[1], cr.at[1], other_c),
+        ]
+
+    def start(self):
+        self.local.start()
+        for cp in self.z:
+            cp.start()
+        self.x[0].start()
+        self.y[0, 0].start()
+
+    def forward(self):
+        for k in range(1, self.zn):
+            self.z[k - 1].wait_recv()
+            self.x[k].start()
+            self.y[k, 0].start()
+        for k in range(self.zn):
+            self.x[k].wait_recv()
+            self.y[k, 1].start()
+        self.local.wait()
+        self.c[0].start()
+
+    def finish(self):
+        for cp in self.y.values():
+            cp.wait_recv()
+        self.c[1].start()
+        for cp in self.z + self.x + list(self.y.values()):
+            cp.wait_send()
+        for cp in self.c:
+            cp.wait()
+
+    @staticmethod
+    def semaphores(S):
+        dma = pltpu.SemaphoreType.DMA
+        return [dma((S // 2,))] * 4 + [dma((S,))] * 2 + [dma((2,))] * 2 + [dma]
+
+
+def row_copies(S, src, dst, send, recv):
+    s = lax.axis_index("seq")
+    out = []
+    for k in range(1, S):
+        d = lax.rem(s + k, S)
+        out.append(seq_copy(src(d), dst(s), send.at[k], recv.at[k], {"seq": d}))
+    return out
+
+
+def sum_over_all(S, PN, lr, bct, LR, BCT, got_l, got_b, ssl, rsl, ssb, rsb, sgl, rgl, sgb, rgb):
+    n = S * PN
+    s, p = lax.axis_index("seq"), lax.axis_index("tp")
+    me = s * PN + p
+    rows = lr.shape[0] // n
+    per = n // bct.shape[0]
+    high = bct.shape[1] // per
+
+    def device(j):
+        return {"seq": lax.div(j, PN), "tp": lax.rem(j, PN)}
+
+    def rows_of(j):
+        return pl.ds(pl.multiple_of(j * rows, 16), rows)
+
+    def slab(ref, j):
+        return ref.at[lax.div(j, per), pl.ds(pl.multiple_of(lax.rem(j, per) * high, 8), high)]
+
+    def first(k):
+        j = lax.rem(me + k, n)
+        return (
+            seq_copy(lr.at[rows_of(j)], got_l.at[k], ssl.at[k], rsl.at[k], device(j)),
+            seq_copy(slab(bct, j), got_b.at[k], ssb.at[k], rsb.at[k], device(j)),
+        )
+
+    def second(k):
+        j = lax.rem(me + k, n)
+        mine_l, mine_b = LR.at[rows_of(me)], slab(BCT, me)
+        return (
+            seq_copy(mine_l, mine_l, sgl.at[k], rgl.at[k], device(j)),
+            seq_copy(mine_b, mine_b, sgb.at[k], rgb.at[k], device(j)),
+        )
+
+    def start(copies, k):
+        for cp in copies(k):
+            cp.start()
+        return 0
+
+    def wait(copies, k):
+        for cp in copies(k):
+            cp.wait()
+        return 0
+
+    lax.fori_loop(1, n, lambda k, _: start(first, k), 0)
+    got_l[0] = lr[rows_of(me), :]
+    got_b[0] = slab(bct, me)[...]
+    lax.fori_loop(1, n, lambda k, _: wait(first, k), 0)
+    LR[rows_of(me), :] = jnp.sum(got_l[...], axis=0).astype(LR.dtype)
+    slab(BCT, me)[...] = jnp.sum(got_b[...], axis=0)
+    lax.fori_loop(1, n, lambda k, _: start(second, k), 0)
+    lax.fori_loop(1, n, lambda k, _: wait(second, k), 0)
+
+
+def sum_scratch(S, PN, T):
+    n = S * PN
+    dma = pltpu.SemaphoreType.DMA
+    slabs = (T // LANES) * 2 * N // n
+    return [pltpu.VMEM((n, T // n, R), F32), pltpu.VMEM((n, slabs, LANES), F32)] + [dma((n,))] * 8
+
+
+def softplus(v):
+    u = jnp.exp(-jnp.abs(v))
+    w = 1.0 + u
+    small = jnp.where(w == 1.0, u, jnp.log(w) * (u / jnp.where(w == 1.0, 1.0, w - 1.0)))
+    return jnp.maximum(v, 0.0) + small
+
+
+def masked_sum(acc, aux, r, C):
+    total = acc[:, 0:C] * aux[r, 0:1]
+    for m in range(1, M):
+        total = total + acc[:, m * C : (m + 1) * C] * aux[r, m : m + 1]
+    return total
+
+
+def forward_kernel(S, PN, *refs):
+    (tok, og, modrow, wdt_mine, gain_mine, wi, wg, wo, segs, ch, wlr, wbc) = refs[:12]
+    (act, conv, inner, low, bct, pre, H, gated, dgate, dmix, aux, X, NR, G, WD, INV) = refs[12:28]
+    rest = list(refs[28:])
+    take = lambda k: [rest.pop(0) for _ in range(k)]
+    tile, toks, ogs, nrm, Wi, Wg, Wo, AUX, GAIN = take(9)
+    step, drive, keep, Y, pad, act3, lr, bcp = take(8)
+    ag1, ag2 = take(9), take(9)
+    ws = take(12)
+    ls = take(1)[0]
+    sums = take(10)
+    s, p, z, x = place(S, PN)
+    TL, DD = tok.shape
+    T = S * TL
+    width = DD // S
+    quarter = DD // PN
+    C = act.shape[1]
+    rows = 128
+
+    wide = tok[...].astype(F32)
+    inv = lax.rsqrt(jnp.mean(wide * wide, axis=1, keepdims=True) + EPSILON)
+    row = jnp.transpose(jnp.broadcast_to(inv, (TL, LANES)))[0:8]
+    tile[...] = jnp.where(
+        lax.broadcasted_iota(jnp.int32, row.shape, 0) == 0, modrow[...], row
+    )
+    greet_all(S, PN)
+    chans = lambda d: pl.ds(pl.multiple_of(d * C, LANES), C)
+    block = lambda d: pl.ds(pl.multiple_of(d * width, width), width)
+    tokens = Spread(
+        S, PN, tok.at[:, pl.ds(pl.multiple_of(p * quarter, LANES), quarter)], toks, *ag1
+    )
+    small = (
+        row_copies(S, lambda d: tile, lambda t: AUX.at[t], ws[0], ws[1])
+        + row_copies(S, lambda d: gain_mine, lambda t: GAIN.at[t], ws[2], ws[3])
+    )
+    dts = row_copies(S, lambda d: wdt_mine.at[:, :, chans(d)], lambda t: WD.at[t], ws[4], ws[5])
+    inners = row_copies(S, lambda d: wi.at[d], lambda t: Wi.at[block(t)], ws[6], ws[7])
+    gates = row_copies(S, lambda d: wg.at[d], lambda t: Wg.at[block(t)], ws[8], ws[9])
+    outs = row_copies(S, lambda d: wo.at[d], lambda t: Wo.at[t], ws[10], ws[11])
+    cotangent = Spread(S, PN, og, ogs, *ag2)
+    for cp in small:
+        cp.start()
+    tokens.start()
+    for cp in inners:
+        cp.start()
+    own = [
+        pltpu.make_async_copy(tile, AUX.at[s], ls.at[0]),
+        pltpu.make_async_copy(gain_mine, GAIN.at[s], ls.at[1]),
+        pltpu.make_async_copy(wdt_mine.at[:, :, chans(s)], WD.at[s], ls.at[2]),
+        pltpu.make_async_copy(wi.at[s], Wi.at[block(s)], ls.at[3]),
+        pltpu.make_async_copy(wg.at[s], Wg.at[block(s)], ls.at[4]),
+        pltpu.make_async_copy(wo.at[s], Wo.at[s], ls.at[5]),
+    ]
+    for cp in own:
+        cp.start()
+    for cp in own:
+        cp.wait()
+    tokens.forward()
+    for cp in small:
+        cp.wait()
+    lane = lax.broadcasted_iota(jnp.int32, (TL, 8), 1)
+
+    def columns(t, _):
+        r = pl.ds(pl.multiple_of(t * TL, TL), TL)
+        turned = jnp.transpose(jnp.concatenate([AUX[t]] * (LANES // 8), axis=0))
+        mask = (turned[:, 0:1] == lane.astype(F32)).astype(F32)
+        aux[r, :] = jnp.where(
+            lane < M, mask, jnp.where(lane == 7, turned[:, 1:2], segs[r, :])
+        )
+        return 0
+
+    lax.fori_loop(0, S, columns, 0)
+    tokens.finish()
+    per = quarter // width
+
+    def norm(t, _):
+        r = pl.ds(pl.multiple_of(t * TL, TL), TL)
+        scale = aux[r, 7:8]
+        for q in range(PN):
+            scaled = toks[q, t].astype(F32) * scale
+            for j in range(per):
+                part = scaled[:, j * width : (j + 1) * width] * GAIN[q * per + j, 0:1, :]
+                nrm[r, q * quarter + j * width : q * quarter + (j + 1) * width] = part.astype(BF16)
+        return 0
+
+    lax.fori_loop(0, S, norm, 0)
+    for cp in inners:
+        cp.wait()
+    for cp in gates + dts:
+        cp.start()
+
+    big = 256
+    pad[0:8, :] = jnp.zeros((8, C), F32)
+
+    def first(i, _):
+        r = pl.ds(pl.multiple_of(i * big, big), big)
+        value = masked_sum(dot(nrm[r, :], Wi[...]), aux, r, C).astype(BF16)
+        inner[r, :] = value
+        pad[pl.ds(pl.multiple_of(i * big + 8, 8), big), :] = value.astype(F32)
+        return 0
+
+    lax.fori_loop(0, T // big, first, 0)
+
+    def convolve(i, _):
+        r = pl.ds(pl.multiple_of(i * rows, rows), rows)
+        window = pad[pl.ds(pl.multiple_of(i * rows, rows), rows + 8), :]
+        v = jnp.broadcast_to(ch[K : K + 1, :], (rows, C))
+        for k in range(K):
+            term = ch[k : k + 1, :] * window[8 - (K - 1) + k : 8 - (K - 1) + k + rows]
+            v = v + (term * aux[r, M + k : M + k + 1] if k < K - 1 else term)
+        conv[r, :] = v
+        a = (v / (1.0 + jnp.exp(-v))).astype(BF16)
+        act[r, :] = a
+        a_wide = a.astype(F32)
+        for m in range(M):
+            act3[r, m * C : (m + 1) * C] = (a_wide * aux[r, m : m + 1]).astype(BF16)
+        lr[r, :] = dot(act3[r, :], wlr[...])
+        bcp[i] = dot(wbc[...], act3[r, :], NT)
+        return 0
+
+    lax.fori_loop(0, T // rows, convolve, 0)
+    sum_over_all(S, PN, lr, bcp, low, bct, *sums)
+    for cp in dts:
+        cp.wait()
+    cotangent.start()
+    for cp in outs:
+        cp.start()
+
+    def prepare(i, _):
+        r = pl.ds(pl.multiple_of(i * rows, rows), rows)
+        low_wide = low[r, :].astype(F32)
+        bias = jnp.zeros((rows, C), F32)
+        for m in range(M):
+            mask = aux[r, m : m + 1]
+            masked = (low_wide * mask).astype(BF16)
+            bias = bias + mask * ch[K + 2 + m : K + 3 + m, :]
+            for t in range(S):
+                h = R // S
+                bias = bias + dot(masked[:, t * h : (t + 1) * h], WD[t, m])
+        pre[r, :] = bias
+        st = softplus(bias)
+        step[r, :] = st
+        drive[r, :] = st * act[r, :].astype(F32)
+        keep[r, :] = jnp.broadcast_to(aux[r, 6:7], (rows, C))
+        return 0
+
+    lax.fori_loop(0, T // rows, prepare, 0)
+    scan_forward(T, C, bct, ch, step, drive, keep, H, Y)
+    cotangent.forward()
+    for cp in gates:
+        cp.wait()
+
+    def gate(i, _):
+        r = pl.ds(pl.multiple_of(i * big, big), big)
+        drive[r, :] = masked_sum(dot(nrm[r, :], Wg[...]), aux, r, C)
+        return 0
+
+    lax.fori_loop(0, T // big, gate, 0)
+    cotangent.finish()
+    for cp in outs:
+        cp.wait()
+
+    def back(i, _):
+        r = pl.ds(pl.multiple_of(i * big, big), big)
+        acc = jnp.zeros((big, M * C), F32)
+        for q in range(PN):
+            g = ogs[q, pl.ds(i * (big // TL), big // TL)].reshape(big, quarter)
+            for j in range(per):
+                acc = acc + dot(g[:, j * width : (j + 1) * width], Wo[q * per + j], NT)
+        keep[r, :] = masked_sum(acc, aux, r, C)
+        return 0
+
+    lax.fori_loop(0, T // big, back, 0)
+
+    def finish(i, _):
+        r = pl.ds(pl.multiple_of(i * rows, rows), rows)
+        mixed = Y[r, :] + ch[K + 1 : K + 2, :] * act[r, :].astype(F32)
+        g, d = drive[r, :], keep[r, :]
+        sig = 1.0 / (1.0 + jnp.exp(-g))
+        gated[r, :] = (mixed * (g * sig)).astype(BF16)
+        dmix[r, :] = d * (g * sig)
+        dgate[r, :] = (d * mixed * (sig * (1.0 + g * (1.0 - sig)))).astype(BF16)
+        return 0
+
+    lax.fori_loop(0, T // rows, finish, 0)
+    mine = pl.ds(pl.multiple_of(lax.rem(s, per) * width, width), width)
+    NR[...] = nrm[:, pl.ds(pl.multiple_of(s * width, width), width)]
+
+    def own_features(t, _):
+        r = pl.ds(pl.multiple_of(t * TL, TL), TL)
+        X[r, :] = toks[lax.div(s, per), t, :, mine]
+        G[r, :] = ogs[lax.div(s, per), t, :, mine]
+        return 0
+
+    lax.fori_loop(0, S, own_features, 0)
+    INV[...] = jnp.broadcast_to(inv, INV.shape)
+
+
+def scan_forward(T, C, bct, ch, step, drive, keep, H, Y):
+    base = -jnp.exp(ch[K + 2 + M : K + 2 + M + N, :])
+    H[0] = jnp.zeros((N, C), F32)
+
+    def chunk(c, h):
+        bc = bct[c]
+
+        def eight(i, h):
+            cols = pltpu.roll(bc, lax.rem(LANES - 8 * i, LANES), 1)
+            t0 = pl.multiple_of(c * LANES + i * 8, 8)
+            r = pl.ds(t0, 8)
+            st, dr, kp = step[r, :], drive[r, :], keep[r, :]
+            ys = []
+            for j in range(8):
+                rate = jnp.exp(st[j : j + 1] * base) * kp[j : j + 1]
+                h = rate * h + dr[j : j + 1] * cols[0:N, j : j + 1]
+                H[t0 + j + 1] = h
+                ys.append(jnp.sum(cols[N : 2 * N, j : j + 1] * h, axis=0, keepdims=True))
+            Y[r, :] = jnp.concatenate(ys, axis=0)
+            return h
+
+        return lax.fori_loop(0, LANES // 8, eight, h)
+
+    lax.fori_loop(0, T // LANES, chunk, jnp.zeros((N, C), F32))
+
+
+def forward_call(S, PN, args, T, C, width):
+    dma = pltpu.SemaphoreType.DMA
+    TL, DD = args[0].shape
+    chunks = T // LANES
+    f = lambda *shape: sds(shape)
+    b = lambda *shape: sds(shape, BF16)
+    vf = lambda *shape: pltpu.VMEM(shape, F32)
+    vb = lambda *shape: pltpu.VMEM(shape, BF16)
+    out = (
+        b(T, C), f(T, C), b(T, C), b(T, R), f(chunks, 2 * N, LANES), f(T, C), f(T + 1, N, C),
+        b(T, C), b(T, C), f(T, C), f(T, 8), b(T, width), b(T, width), b(T, width),
+        b(S, M, R // S, C), f(TL, LANES),
+    )
+    scratch = (
+        [vf(8, TL), vb(PN, S, TL, DD // PN), vb(PN, S, TL, DD // PN), vb(T, DD)]
+        + [vb(DD, M * C), vb(DD, M * C), vb(S, M * C, width), vf(S, 8, TL), vf(S, 8, width)]
+        + [vf(T, C)] * 4
+        + [vf(T + 8, C), vb(T, M * C), vf(T, R), vf(chunks, 2 * N, LANES)]
+        + Spread.semaphores(S) * 2
+        + [dma((S,))] * 12
+        + [dma((6,))]
+        + sum_scratch(S, PN, T)
+    )
+    return remote_call(
+        functools.partial(forward_kernel, S, PN), out, len(args), scratch, 0
+    )(*args)
+
+
+def row_gather(S, block):
+    across = [(i, i ^ 1) for i in range(S)]
+    near = [block] + [
+        lax.ppermute(block, "seq", [(i, (i + 2 * k) % S) for i in range(S)])
+        for k in range(1, S // 2)
+    ]
+    out = []
+    for blk in near:
+        out += [blk, lax.ppermute(blk, "seq", across)]
+    return jnp.stack(out)
+
+
+def row_order(S):
+    s = lax.axis_index("seq")
+    z, x = lax.div(s, 2), lax.rem(s, 2)
+    zn = S // 2
+    return jnp.stack(
+        [lax.rem(z - k + zn, zn) * 2 + xx for k in range(zn) for xx in (x, 1 - x)]
+    ).astype(jnp.int32)
+
+
+def backward_sum_kernel(S, PN, lr, bct, more, LR, BCT, MORE, sx, rx, lx, *sums):
+    greet_all(S, PN)
+    s = lax.axis_index("seq")
+    step = more.shape[1] // S
+    part = lambda d: more.at[:, pl.ds(pl.multiple_of(d * step, 8), step), :]
+    copies = row_copies(S, part, lambda t: MORE.at[t], sx, rx)
+    for cp in copies:
+        cp.start()
+    own = pltpu.make_async_copy(part(s), MORE.at[s], lx)
+    own.start()
+    sum_over_all(S, PN, lr, bct, LR, BCT, *sums)
+    own.wait()
+    for cp in copies:
+        cp.wait()
+
+
+def backward_sum(S, PN, lr, bct, more):
+    dma = pltpu.SemaphoreType.DMA
+    return remote_call(
+        functools.partial(backward_sum_kernel, S, PN),
+        (
+            sds(lr.shape, BF16),
+            sds(bct.shape),
+            sds((S, more.shape[0], more.shape[1] // S, more.shape[2])),
+        ),
+        3,
+        [dma((S,)), dma((S,)), dma] + sum_scratch(S, PN, lr.shape[0]),
+        2,
+    )(lr, bct, more)
+
+
+def unscan_kernel(
+    pre, H, dmix, act, bct, aux, ch, wdtT, low,
+    dlow, dbct, gdt, gch, dact, step, drive, keep, DS, DB, dst3, low3, dst,
+):
+    T, C = act.shape
+    rows = 128
+
+    def prepare(i, _):
+        r = pl.ds(pl.multiple_of(i * rows, rows), rows)
+        sp = pre[r, :]
+        st = softplus(sp)
+        step[r, :] = st
+        drive[r, :] = st * act[r, :].astype(F32)
+        keep[r, :] = jnp.broadcast_to(aux[r, 6:7], (rows, C))
+        return 0
+
+    lax.fori_loop(0, T // rows, prepare, 0)
+    base = -jnp.exp(ch[K + 2 + M : K + 2 + M + N, :])
+    lane = lax.broadcasted_iota(jnp.int32, (N, LANES), 1)
+    nothing = jnp.zeros((N, C), F32)
+    chunks = T // LANES
+
+    def chunk(cc, carry):
+        c = chunks - 1 - cc
+        bc = bct[c]
+
+        def eight(ii, carry):
+            flow, hcur, gacc, accb, accc = carry
+            i = LANES // 8 - 1 - ii
+            cols = pltpu.roll(bc, lax.rem(LANES - 8 * i, LANES), 1)
+            t0 = pl.multiple_of(c * LANES + i * 8, 8)
+            r = pl.ds(t0, 8)
+            st, dr, kp, dm = step[r, :], drive[r, :], keep[r, :], dmix[r, :]
+            ds, db = [None] * 8, [None] * 8
+            for j in reversed(range(8)):
+                bcol, ccol = cols[0:N, j : j + 1], cols[N : 2 * N, j : j + 1]
+                back = ccol * dm[j : j + 1] + flow
+                rate = jnp.exp(st[j : j + 1] * base) * kp[j : j + 1]
+                hprev = H[t0 + j]
+                here = lane == 8 * i + j
+                accc = jnp.where(
+                    here, jnp.sum(dm[j : j + 1] * hcur, axis=1, keepdims=True), accc
+                )
+                accb = jnp.where(
+                    here, jnp.sum(back * dr[j : j + 1], axis=1, keepdims=True), accb
+                )
+                flow = rate * back
+                dlog = flow * hprev
+                gacc = gacc + dlog * st[j : j + 1]
+                ds[j] = jnp.sum(dlog * base, axis=0, keepdims=True)
+                db[j] = jnp.sum(back * bcol, axis=0, keepdims=True)
+                hcur = hprev
+            DS[r, :] = jnp.concatenate(ds, axis=0)
+            DB[r, :] = jnp.concatenate(db, axis=0)
+            return flow, hcur, gacc, accb, accc
+
+        blank = jnp.zeros((N, LANES), F32)
+        flow, hcur, gacc, accb, accc = lax.fori_loop(
+            0, LANES // 8, eight, carry + (blank, blank)
+        )
+        dbct[c, 0:N, :] = accb
+        dbct[c, N : 2 * N, :] = accc
+        return flow, hcur, gacc
+
+    _, _, gacc = lax.fori_loop(0, chunks, chunk, (nothing, H[T], nothing))
+
+    def finish(i, carry):
+        skip, bias = carry
+        r = pl.ds(pl.multiple_of(i * rows, rows), rows)
+        a = act[r, :].astype(F32)
+        back_b = DB[r, :]
+        grad = DS[r, :] + a * back_b
+        d = (grad / (1.0 + jnp.exp(-pre[r, :]))).astype(BF16)
+        dst[r, :] = d
+        wide = d.astype(F32)
+        low_wide = low[r, :].astype(F32)
+        sums = []
+        for m in range(M):
+            mask = aux[r, m : m + 1]
+            masked = wide * mask
+            sums.append(jnp.sum(masked, axis=0, keepdims=True))
+            dst3[r, m * C : (m + 1) * C] = masked.astype(BF16)
+            low3[r, m * R : (m + 1) * R] = (low_wide * mask).astype(BF16)
+        dlow[r, :] = dot(dst3[r, :], wdtT[...])
+        dact[r, :] = dmix[r, :] * ch[K + 1 : K + 2, :] + step[r, :] * back_b
+        skip = skip + jnp.sum(dmix[r, :] * a, axis=0, keepdims=True)
+        return skip, bias + jnp.concatenate(sums, axis=0)
+
+    skip, bias = lax.fori_loop(
+        0, T // rows, finish, (jnp.zeros((1, C), F32), jnp.zeros((M, C), F32))
+    )
+    gch[0:1, :] = skip
+    gch[1 : 1 + M, :] = bias
+    gch[1 + M : 1 + M + N, :] = base * gacc
+    for m in range(M):
+        gdt[m] = dot(low3[:, m * R : (m + 1) * R], dst[...], TN)
+
+
+def unconv_kernel(
+    dpar, act, conv, inner, aux, ch, wxT, dact, dinner, gx, gtap, pad, tail, dpar3, act3,
+):
+    T, C = act.shape
+    XWID = dpar.shape[1]
+    rows = 128
+    pad[0:8, :] = jnp.zeros((8, C), F32)
+    tail[T : T + 8, :] = jnp.zeros((8, C), F32)
+
+    def fill(i, _):
+        r = pl.ds(pl.multiple_of(i * rows, rows), rows)
+        pad[pl.ds(pl.multiple_of(i * rows + 8, 8), rows), :] = inner[r, :].astype(F32)
+        wide = dpar[r, :].astype(F32)
+        a = act[r, :].astype(F32)
+        total = dact[r, :]
+        for m in range(M):
+            mask = aux[r, m : m + 1]
+            total = total + dot((wide * mask).astype(BF16), wxT[m])
+            act3[r, m * C : (m + 1) * C] = (a * mask).astype(BF16)
+        v = conv[r, :]
+        sig = 1.0 / (1.0 + jnp.exp(-v))
+        tail[r, :] = (total * (sig * (1.0 + v * (1.0 - sig)))).astype(BF16).astype(F32)
+        return 0
+
+    lax.fori_loop(0, T // rows, fill, 0)
+
+    def body(i, sums):
+        r = pl.ds(pl.multiple_of(i * rows, rows), rows)
+        window = pad[pl.ds(pl.multiple_of(i * rows, rows), rows + 8), :]
+        d = tail[r, :]
+        ahead = tail[pl.ds(pl.multiple_of(i * rows, rows), rows + 8), :]
+        same = aux[pl.ds(pl.multiple_of(i * rows, rows), rows + 8), :]
+        total = ch[K - 1 : K, :] * d
+        new = []
+        for k in range(K):
+            off = K - 1 - k
+            shifted = window[8 - off : 8 - off + rows]
+            if k < K - 1:
+                shifted = shifted * aux[r, M + k : M + k + 1]
+                total = total + ch[k : k + 1, :] * (
+                    ahead[off : off + rows] * same[off : off + rows, M + k : M + k + 1]
+                )
+            new.append(jnp.sum(d * shifted, axis=0, keepdims=True))
+        new.append(jnp.sum(d, axis=0, keepdims=True))
+        dinner[r, :] = total.astype(BF16)
+        return sums + jnp.concatenate(new, axis=0)
+
+    gtap[0 : K + 1, :] = lax.fori_loop(0, T // rows, body, jnp.zeros((K + 1, C), F32))
+    for m in range(M):
+        gx[m] = dot(act3[:, m * C : (m + 1) * C], dpar[...], TN)
+
+
+def out_kernel(order, blk, G, aux, w, layer, grad, masked, acc):
+    i = pl.program_id(0)
+    T, C = blk.shape[1:]
+
+    @pl.when(i == 0)
+    def _():
+        acc[...] = jnp.zeros(acc.shape, F32)
+
+    wide = blk[0].astype(F32)
+    for m in range(M):
+        masked[:, m * C : (m + 1) * C] = (wide * aux[:, m : m + 1]).astype(BF16)
+        acc[...] += dot(masked[:, m * C : (m + 1) * C], w[m])
+        grad[m] = dot(masked[:, m * C : (m + 1) * C], G[...], TN)
+
+    @pl.when(i == pl.num_programs(0) - 1)
+    def _():
+        layer[...] = acc[...].astype(BF16)
+
+
+def out_project(S, order, blocks, G, aux, w):
+    T, C = blocks.shape[1:]
+    width = G.shape[1]
+    whole = lambda shape: pl.BlockSpec(shape, lambda i, o: (0,) * len(shape))
+    return pl.pallas_call(
+        out_kernel,
+        out_shape=(sds((T, width), BF16), sds((M, S * C, width))),
+        grid_spec=pltpu.PrefetchScalarGridSpec(
+            num_scalar_prefetch=1,
+            grid=(S,),
+            in_specs=[
+                pl.BlockSpec((1, T, C), lambda i, o: (i, 0, 0)),
+                whole((T, width)),
+                whole((T, 8)),
+                pl.BlockSpec((M, C, width), lambda i, o: (0, o[i], 0)),
+            ],
+            out_specs=[whole((T, width)), pl.BlockSpec((M, C, width), lambda i, o: (0, o[i], 0))],
+            scratch_shapes=[pltpu.VMEM((T, M * C), BF16), pltpu.VMEM((T, width), F32)],
+        ),
+        compiler_params=pltpu.CompilerParams(vmem_limit_bytes=VMEM_LIMIT),
+    )(order, blocks, G, aux, w)
+
+
+def in_kernel(order, b0, b1, A3T, W0, W1, aux, gain, X, dnorm, grad0, grad1, rowdot, gg, acc):
+    i = pl.program_id(0)
+    T, width = X.shape
+
+    @pl.when(i == 0)
+    def _():
+        acc[...] = jnp.zeros(acc.shape, F32)
+
+    d0, d1 = b0[0], b1[0]
+    grad0[...] = dot(A3T[...], d0)
+    grad1[...] = dot(A3T[...], d1)
+    for m in range(M):
+        rows = slice(m * width, (m + 1) * width)
+        acc[m] += dot(d0, W0[rows, :], NT) + dot(d1, W1[rows, :], NT)
+
+    @pl.when(i == pl.num_programs(0) - 1)
+    def _():
+        rows = 128
+
+        def body(k, total):
+            r = pl.ds(pl.multiple_of(k * rows, rows), rows)
+            d = acc[0, r, :] * aux[r, 0:1]
+            for m in range(1, M):
+                d = d + acc[m, r, :] * aux[r, m : m + 1]
+            scaled = X[r, :].astype(F32) * aux[r, 7:8]
+            gained = d * gain[...]
+            dnorm[r, :] = gained.astype(BF16)
+            along = jnp.sum(gained * scaled, axis=1, keepdims=True)
+            rowdot[k] = jnp.transpose(jnp.broadcast_to(along, (rows, LANES)))[0:8]
+            return total + jnp.sum(d * scaled, axis=0, keepdims=True)
+
+        total = lax.fori_loop(0, T // rows, body, jnp.zeros((1, width), F32))
+        gg[...] = jnp.broadcast_to(total, gg.shape)
+
+
+def in_project_back(S, order, b0, b1, A3T, W0, W1, aux, gain, X):
+    T, C = b0.shape[1:]
+    width = X.shape[1]
+    whole = lambda shape: pl.BlockSpec(shape, lambda i, o: (0,) * len(shape))
+    piece = pl.BlockSpec((M * width, C), lambda i, o: (0, o[i]))
+    return pl.pallas_call(
+        in_kernel,
+        out_shape=(
+            sds((T, width), BF16),
+            sds((M * width, S * C)),
+            sds((M * width, S * C)),
+            sds((T // 128, 8, 128)),
+            sds((8, width)),
+        ),
+        grid_spec=pltpu.PrefetchScalarGridSpec(
+            num_scalar_prefetch=1,
+            grid=(S,),
+            in_specs=[
+                pl.BlockSpec((1, T, C), lambda i, o: (i, 0, 0)),
+                pl.BlockSpec((1, T, C), lambda i, o: (i, 0, 0)),
+                whole((M * width, T)),
+                piece,
+                piece,
+                whole((T, 8)),
+                whole((1, width)),
+                whole((T, width)),
+            ],
+            out_specs=[
+                whole((T, width)),
+                piece,
+                piece,
+                whole((T // 128, 8, 128)),
+                whole((8, width)),
+            ],
+            scratch_shapes=[pltpu.VMEM((M, T, width), F32)],
+        ),
+        compiler_params=pltpu.CompilerParams(vmem_limit_bytes=VMEM_LIMIT),
+    )(order, b0, b1, A3T, W0, W1, aux, gain, X)
+
+
+def last_kernel(S, PN, lo, dn, gg, tile, rowdot, LO, DN, GG, TILE, mine, los, lor, dns, dnr, gs, gr, ts, tr, ls):
+    s, p = lax.axis_index("seq"), lax.axis_index("tp")
+    n = S * PN
+    ratio = S // PN
+    me = s * PN + p
+    home = lax.div(s, ratio)
+    slot = lax.rem(s, ratio) * PN + p
+    bar = pltpu.get_barrier_semaphore()
+
+    def device(j):
+        return {"seq": lax.div(j, PN), "tp": lax.rem(j, PN)}
+
+    def greet(k, _):
+        pl.semaphore_signal(
+            bar, inc=1, device_id=device(lax.rem(me + k, n)), device_id_type=MESH
+        )
+        return 0
+
+    lax.fori_loop(1, n, greet, 0)
+    first = lax.broadcasted_iota(jnp.int32, tile.shape, 0)
+    for b in range(S):
+        mine[b] = jnp.where(first == 1, rowdot[b], tile[...])
+    pl.semaphore_wait(bar, n - 1)
+    TL = lo.shape[0] // S
+
+    def block(k, start):
+        rows = pl.ds(k * TL, TL)
+        dev = {"seq": k, "tp": home}
+        away = jnp.logical_or(s != k, home != p)
+
+        @pl.when(away)
+        def _():
+            for cp in (
+                seq_copy(dn.at[rows], DN.at[slot], dns.at[k], dnr.at[slot], dev),
+                seq_copy(lo.at[rows], LO.at[slot], los.at[k], lor.at[slot], dev),
+            ):
+                if start:
+                    cp.start()
+                else:
+                    cp.wait_send()
+
+        if start:
+
+            @pl.when(jnp.logical_not(away))
+            def _():
+                a = pltpu.make_async_copy(dn.at[rows], DN.at[slot], ls.at[0])
+                b = pltpu.make_async_copy(lo.at[rows], LO.at[slot], ls.at[1])
+                a.start()
+                b.start()
+                a.wait()
+                b.wait()
+
+    def tiles(k):
+        j = lax.rem(me + k, n)
+        return seq_copy(mine.at[lax.div(j, PN)], TILE.at[k], ts.at[k], tr.at[k], device(j))
+
+    def send_tile(k, _):
+        tiles(k).start()
+        return 0
+
+    def wait_tile(k, _):
+        tiles(k).wait()
+        return 0
+
+    gains = [
+        seq_copy(gg, GG.at[k], gs.at[k], gr.at[k], {"tp": lax.rem(p + k, PN)})
+        for k in range(1, PN)
+    ]
+    for k in range(S):
+        block(k, True)
+    for cp in gains:
+        cp.start()
+    lax.fori_loop(1, n, send_tile, 0)
+    GG[0] = gg[...]
+    TILE[0] = mine[s]
+    for cp in gains:
+        cp.wait()
+    lax.fori_loop(1, n, wait_tile, 0)
+    for k in range(S):
+        block(k, False)
+    for h in range(ratio):
+        for q in range(PN):
+            t = ratio * p + h
+            i = h * PN + q
+
+            @pl.when(jnp.logical_or(t != s, p != q))
+            def _():
+                dev = {"seq": t, "tp": q}
+                seq_copy(dn.at[0:TL], DN.at[i], dns.at[0], dnr.at[i], dev).wait_recv()
+                seq_copy(lo.at[0:TL], LO.at[i], los.at[0], lor.at[i], dev).wait_recv()
+
+
+def last_exchange(S, PN, lo, dn, gg, tile, rowdot):
+    T, width = lo.shape
+    n = S * PN
+    dma = pltpu.SemaphoreType.DMA
+    return remote_call(
+        functools.partial(last_kernel, S, PN),
+        (
+            sds((S, T // S, width), BF16),
+            sds((S, T // S, width), BF16),
+            sds((PN,) + gg.shape),
+            sds((n,) + tile.shape),
+        ),
+        5,
+        [pltpu.VMEM((S,) + tile.shape, F32)]
+        + [dma((S,))] * 4
+        + [dma((PN,))] * 2
+        + [dma((n,))] * 2
+        + [dma((2,))],
+        3,
+    )(lo, dn, gg, tile, rowdot)
+
+
+def local(
+    tokens, out_grad, modality, segment,
+    w_in, w_x, w_dt, w_out, channel, norm_gain,
+    moment_in, moment_x, moment_dt, moment_out, moment_channel, moment_gain,
+    square_in, square_x, square_dt, square_out, square_channel, square_gain,
+    average_in, average_x, average_dt, average_out, average_channel, average_gain,
+):
+    S, PN = lax.axis_size("seq"), lax.axis_size("tp")
+    s, p = lax.axis_index("seq"), lax.axis_index("tp")
+    TL = tokens.shape[0]
+    T = S * TL
+    width = D // S
+    inner_width = w_out.shape[1]
+    C = inner_width // S
+    zn = S // 2
+    split = w_in.reshape(M, width, 2, S, C)
+    win = jnp.transpose(w_in, (2, 0, 1, 3)).astype(BF16).reshape(2, M * width, inner_width)
+    wi, wg = [
+        jnp.transpose(split[:, :, h], (2, 1, 0, 3)).astype(BF16).reshape(S, width, M * C)
+        for h in range(2)
+    ]
+    wout = w_out.astype(BF16)
+    wo = jnp.transpose(wout.reshape(M, S, C, width), (1, 0, 2, 3)).reshape(S, M * C, width)
+    wx = w_x.astype(BF16)
+    wlr = wx[:, :, :R].reshape(M * C, R)
+    wbc = jnp.transpose(wx[:, :, R:], (2, 0, 1)).reshape(2 * N, M * C)
+    modrow = jnp.broadcast_to(modality.astype(F32)[None], (8, TL))
+    ahead = jnp.concatenate([jnp.full((K - 1,), -1, jnp.int32), segment])
+    same = [(ahead[k : k + T] == segment).astype(F32) for k in range(K - 1)]
+    zero = jnp.zeros((T,), F32)
+    segs = jnp.stack([zero] * M + same + [same[K - 2], zero], axis=1)
+    gain = norm_gain[None, :]
+    order = row_order(S)
+    chunks = T // LANES
+
+    act, conv, inner, low, bct, pre, H, gated, dgate, dmix, aux, X, NR, G, WD, INV = forward_call(
+        S,
+        PN,
+        (
+            tokens, out_grad, modrow, w_dt.astype(BF16), jnp.broadcast_to(gain, (8, width)),
+            wi, wg, wo, segs, channel, wlr, wbc,
+        ),
+        T, C, width,
+    )
+    wdt = jnp.transpose(WD, (1, 0, 2, 3)).reshape(M, R, C)
+    col = lambda dtype=F32: pltpu.VMEM((T, C), dtype)
+    gated_all = row_gather(S, gated)
+    dgate_all = row_gather(S, dgate)
+
+    wdtT = jnp.transpose(wdt, (0, 2, 1)).reshape(M * C, R)
+    dlow, dbct, gdt, gch, dact = local_call(
+        unscan_kernel,
+        (
+            sds((T, R)),
+            sds((chunks, 2 * N, LANES)),
+            sds((M, R, C)),
+            sds((1 + M + N, C)),
+            sds((T, C)),
+        ),
+        9,
+        [col(), col(), col(), col(), col()]
+        + [pltpu.VMEM((T, M * C), BF16), pltpu.VMEM((T, M * R), BF16), col(BF16)],
+    )(pre, H, dmix, act, bct, aux, channel, wdtT, low)
+    dlow, dbct, gdt = backward_sum(S, PN, dlow, dbct, gdt)
+    dpar = jnp.concatenate(
+        [dlow, jnp.transpose(dbct, (0, 2, 1)).reshape(T, 2 * N).astype(BF16)], axis=1
+    )
+    grad_dt = jnp.transpose(gdt, (1, 2, 0, 3)).reshape(w_dt.shape)
+
+    dinner, grad_x, gtap = local_call(
+        unconv_kernel,
+        (sds((T, C), BF16), sds((M, C, R + 2 * N)), sds((8, C))),
+        8,
+        [
+            pltpu.VMEM((T + 8, C), F32),
+            pltpu.VMEM((T + 8, C), F32),
+            pltpu.VMEM((8, LANES), F32),
+            pltpu.VMEM((T, M * C), BF16),
+        ],
+    )(
+        dpar, act, conv, inner, jnp.concatenate([aux, jnp.zeros((8, 8), F32)]), channel,
+        jnp.transpose(wx, (0, 2, 1)), dact,
+    )
+    dinner_all = row_gather(S, dinner)
+    grad_channel = jnp.concatenate([gtap[: K + 1], gch], axis=0)
+
+    layer_part, grad_out = out_project(S, order, gated_all, G, aux, wout)
+    A3T = jnp.concatenate(
+        [jnp.transpose(NR * aux[:, m : m + 1].astype(BF16)) for m in range(M)], axis=0
+    )
+    dnorm_part, gin0, gin1, rowdot, gg = in_project_back(
+        S, order, dinner_all, dgate_all, A3T, win[0], win[1], aux, gain, X
+    )
+    grad_in = jnp.transpose(
+        jnp.stack([gin0, gin1]).reshape(2, M, width, inner_width), (1, 2, 0, 3)
+    )
+
+    grads = [grad_in, grad_x, grad_dt, grad_out, grad_channel]
+    weights = (w_in, w_x, w_dt, w_out, channel, norm_gain)
+    moments = (moment_in, moment_x, moment_dt, moment_out, moment_channel, moment_gain)
+    squares = (square_in, square_x, square_dt, square_out, square_channel, square_gain)
+    averages = (average_in, average_x, average_dt, average_out, average_channel, average_gain)
+    adam_all = [adam_parts(grads[i], moments[i], squares[i]) for i in range(5)]
+    directions = [adam_all[i][2] + WEIGHT_DECAY * weights[i] for i in range(4)]
+    squared = lambda v: jnp.sum(v * v, axis=tuple(range(1, v.ndim)))
+    sums = jnp.concatenate([squared(v) for v in weights[:4]] + [squared(v) for v in directions])
+    tile = jnp.broadcast_to(jnp.pad(sums, (0, LANES - sums.shape[0]))[None], (8, LANES))
+    LO, DN, GG, TILE = last_exchange(S, PN, layer_part, dnorm_part, gg, tile, rowdot)
+
+    totals = jnp.sum(TILE[:, 0, : 8 * M], axis=0).reshape(2, 4, M)
+    along = jnp.sum(TILE[:, 1, :], axis=0)[:, None]
+    adam_all.append(adam_parts(jnp.sum(GG[:, 0, :], axis=0), moment_gain, square_gain))
+
+    def columns(blocks):
+        b = jnp.sum(blocks.reshape(S // PN, PN, TL, width).astype(F32), axis=1)
+        return jnp.concatenate([b[h] for h in range(S // PN)], axis=1)
+
+    out_width = out_grad.shape[1]
+    mine = lax.dynamic_slice_in_dim(tokens, p * out_width, out_width, 1).astype(F32)
+    inv = INV[:, 0:1]
+    layer_out = mine + columns(LO)
+    tokens_grad = out_grad.astype(F32) + inv * (columns(DN) - mine * inv * (along / D))
+    trust = jnp.sqrt(totals[0]) / jnp.sqrt(totals[1])
+    new_weights, new_averages = [], []
+    for i in range(6):
+        w = weights[i]
+        if i < 4:
+            scale = MATRIX_RATE * trust[i].reshape((M,) + (1,) * (w.ndim - 1))
+            new = w - scale * directions[i]
+        else:
+            new = w - (CHANNEL_RATE if i == 4 else GAIN_RATE) * adam_all[i][2]
+        new_weights.append(new)
+        new_averages.append(AVERAGE_KEEP * averages[i] + (1.0 - AVERAGE_KEEP) * new)
+    return (
+        layer_out,
+        tokens_grad,
+        *new_weights,
+        *[a[0] for a in adam_all],
+        *[a[1] for a in adam_all],
+        *new_averages,
+    )
+
+
+def channels_fit(mesh):
+    S, PN = mesh.shape["seq"], mesh.shape["tp"]
+    n = S * PN
+    return PN == 4 and S % 4 == 0 and (2 * N) % n == 0 and (D * 2 // n) % LANES == 0
+
+
 def solution(mesh):
     placed = (
         P("seq", None),
@@ -398,7 +1462,7 @@
         P("seq"),
     )
     return jax.shard_map(
-        local,
+        local if channels_fit(mesh) else generic_local,
         mesh=mesh,
         in_specs=placed,
         out_specs=(

time: 3360 us -> 635 us (0.19)
  waiting for transfers between devices: 1700 us -> 22.9 us
  local copies, waits for them, and re-layouts: 775 us -> 82.8 us
  Pallas kernels: 0 us -> 380 us
  blocking collectives: 354 us -> 0 us
  other arithmetic: 355 us -> 93.3 us
  matrix products: 120 us -> 0 us
  starting transfers between devices: 4.63 us -> 47.8 us
    unnamed x11 -> x0, waiting for transfers between devices: 786 us -> none
    all_gather x2 -> x0, waiting for transfers between devices: 520 us -> none  [the longest x1 476 us: local(): lax.all_gather(lowered[0], 'seq', axis=1, tiled=True)]
    pad x48 -> x1, local copies, waits for them, and re-layouts: 514 us -> 0.01 us  [local(): jnp.pad(sums, (0, LANES - sums.shape[0]))[None]]
    pallas_call x0 -> x7, Pallas kernels: none -> 380 us  [the longest x1 198 us: forward_call(): remote_call(functools.partial(forward_kernel, S, PN), out, len(args), scr...]
    reduce_scatter x5 -> x0, waiting for transfers between devices: 362 us -> none  [the longest x1 362 us: local(): lax.psum_scatter(grad_out, 'seq', scatter_dimension=2, tiled=True)]
    all_gather x9 -> x0, blocking collectives: 280 us -> none  [the longest x4 125 us: prefix(): everything = jax.tree.map(lambda part: lax.all_gather(part, axis), x)]
    add x58 -> x7, other arithmetic: 187 us -> 25.4 us  [the longest x6 23.6 us: local(): new_averages.append(AVERAGE_KEEP * averages[i] + (1.0 - AVERAGE_KEEP) * new)]
    dot_general x42 -> x0, matrix products: 120 us -> none  [the longest x12 30.3 us: masked_outer(): lax.dot_general(operand * mask_low[:, modal_index:modal_index + 1], cotan...]
  transfers between devices with their start and end apart: 12 -> 21, of which waited for: 6 -> 6; matrix products, arithmetic and copies ran while one was open for 10% -> 10% of each run, Pallas kernels for 0% -> 20%
where the time goes in v1:
time: 635 us; the launch traced here: 628 us
  Pallas kernels  380 us (60%)
  other arithmetic  93.3 us (15%)
  local copies, waits for them, and re-layouts  82.8 us (13%)
  starting transfers between devices  47.8 us (8%)
  waiting for transfers between devices  22.9 us (4%)
    pallas_call x1, Pallas kernels, forward_call(): remote_call(functools.partial(forward_kernel, S, PN), out, len(args), scr...  198 us
    pallas_call x1, Pallas kernels, local(): local_call(unscan_kernel, (sds((T, R)), sds((chunks, 2 * N, LANES)), sds(...  65.9 us
    reduce_sum x5, other arithmetic, local(): squared = lambda v: jnp.sum(v * v, axis=tuple(range(1, v.ndim)))  53.3 us
    pallas_call x1, Pallas kernels, last_exchange(): remote_call(functools.partial(last_kernel, S, PN), (sds((S, T // S, width...  41.4 us
    unnamed x111, local copies, waits for them, and re-layouts  40.4 us
    ppermute x9, starting transfers between devices, row_gather(): lax.ppermute(block, 'seq', [(i, (i + 2 * k) % S) for i in range(S)])  34.6 us
    pallas_call x1, Pallas kernels, backward_sum(): remote_call(functools.partial(backward_sum_kernel, S, PN), (sds(lr.shape,...  34 us
    add x6, other arithmetic, local(): new_averages.append(AVERAGE_KEEP * averages[i] + (1.0 - AVERAGE_KEEP) * new)  23.6 us
  transfers between devices with their start and end apart: 21, of which 6 were waited for; matrix products, arithmetic and copies ran while one was open for 10% of the time, Pallas kernels for 20%

profile of v1, /device:TPU:0, one launch (start us, length us, event | category | flops | bytes accessed | tf_op | source)
XLA Modules:
  0.0 628.1 jit_solution(17288849012913372112)
XLA Ops:
  4.8 7.5 %copy.132 = bf16[3,256,2,1024]{1,3,2,0:T(8,128)(2,1)S(1)} copy(f32[3,256,2,1024]{3,2,1,0:T(2,128)} %param.32) | data formatting | bytes 9437184 | tf_op args[4]
  14.9 2.6 copy.138.refs_5_
  17.5 2.7 copy.134
  20.2 2.6 copy.139.refs_6_
  22.7 2.1 convert_element_type.74.w
  30.3 198.4 %shard_map.467 = (bf16[1024,128]{1,0:T(8,128)(2,1)}, f32[1024,128]{1,0:T(8,128)}, bf16[1024,128]{1,0:T(8,128)(2,1)}, bf16[1024,128]{1,0:T(8,128)(2,1)}, f32[8,32...) custom-call(bf16[128,2048]{1,0:T(8,128)(2,1)} %refs_0_.1, ...), custom_call_target="tpu_custom_call" | custom-call | tf_op jit(solution)/shard_map/pallas_call | solution.py:846
  230.4 2.6 collective-permute-start.1
  233.0 1.9 collective-permute-start.3
  234.8 3.1 collective-permute-start.5
  239.5 1.9 concatenate.27.aux
  241.4 65.9 %shard_map.469 = (f32[1024,128]{1,0:T(8,128)}, f32[8,32,128]{2,1,0:T(8,128)}, f32[3,128,128]{2,1,0:T(8,128)}, f32[20,128]{1,0:T(8,128)}, f32[1024,128]{1,0:T(8,128)}) custom-call(f32[1024,128]{1,0:T(8,128)} %get-tuple-element.68.pre, f32[1025,16,128]{2,1,0:T(8,128)} %get-tuple-element.69.H, f32[1024,128]{1,0:T(8,128)} %get-tuple-element.70.dmix, ...), custom_call_target="tpu_custom_call" | custom-call | tf_op jit(solution)/shard_map/pallas_call | solution.py:1334
  307.3 34.0 %shard_map.470 = (bf16[1024,128]{1,0:T(8,128)(2,1)}, f32[8,32,128]{2,1,0:T(8,128)}, f32[8,3,16,128]{3,2,1,0:T(8,128)}) custom-call(f32[1024,128]{1,0:T(8,128)} %get-tuple-element.75.lr, f32[8,32,128]{2,1,0:T(8,128)} %get-tuple-element.76.bct, f32[3,128,128]{2,1,0:T(8,128)} %get-tuple-element.77.more), custom_call_target="tpu_custom_call" | custom-call | tf_op jit(solution)/shard_map/pallas_call | solution.py:890
  342.4 1.9 pad_maximum_fusion.1.dpar
  344.3 6.5 %shard_map.471 = (bf16[1024,128]{1,0:T(8,128)(2,1)}, f32[3,128,160]{2,1,0:T(8,128)}, f32[8,128]{1,0:T(8,128)}) custom-call(bf16[1024,160]{1,0:T(8,128)(2,1)} %pad_maximum_fusion.1.dpar, bf16[1024,128]{1,0:T(8,128)(2,1)} %get-tuple-element.71.act, f32[1024,128]{1,0:T(8,128)} %get-tuple-element.80.conv, bf16[1024,128]{1,0:T(8,128)(2,1)} %get-tuple-element.81.inner, ...), custom_call_target="tpu_custom_call" | custom-call | tf_op jit(solution)/shard_map/pallas_call | solution.py:1353
  350.9 2.1 collective-permute-start.7
  352.9 1.7 bitcast_dynamic-update-slice_fusion.15
  354.7 1.9 copy.153
  356.5 1.9 bitcast_dynamic-update-slice_fusion.7
  358.4 2.0 copy.144
  360.9 1.9 fusion.24
  365.2 2.6 multiply_reduce_fusion.6
  369.0 1.7 multiply_reduce_fusion.4
  372.8 1.7 copy.147
  374.6 1.7 copy.148
  379.8 2.1 collective-permute-start.8
  381.9 1.7 bitcast_dynamic-update-slice_fusion.22
  383.5 3.3 collective-permute-start.10
  386.8 1.7 bitcast_dynamic-update-slice_fusion.21
  388.9 1.7 bitcast_dynamic-update-slice_fusion.14
  391.8 3.1 collective-permute-start.15
  397.4 4.9 collective-permute-done.15
  402.2 3.1 collective-permute-start.12
  407.8 7.4 %collective-permute-start.17 = (bf16[1024,128]{1,0:T(8,128)(2,1)S(1)}, bf16[1024,128]{1,0:T(8,128)(2,1)S(1)}, u32[]{:S(2)}, u32[]{:S(2)}) collective-permute-start(bf16[1024,128]{1,0:T(8,128)(2,1)S(1)} %copy-done.22), channel_id=1, source_target_pairs={{0,16},{4,20},{8,24},{12,28},{16,0},{20,4},{24,8},{28,12},{1,17},{... | collective-permute-start | bytes 786440 | tf_op jit(solution)/shard_map/ppermute | solution.py:854
  417.8 8.2 %collective-permute-start.19 = (bf16[1024,128]{1,0:T(8,128)(2,1)S(1)}, bf16[1024,128]{1,0:T(8,128)(2,1)S(1)}, u32[]{:S(2)}, u32[]{:S(2)}) collective-permute-start(bf16[1024,128]{1,0:T(8,128)(2,1)S(1)} %copy-done.22), channel_id=1, source_target_pairs={{0,24},{4,28},{8,0},{12,4},{16,8},{20,12},{24,16},{28,20},{1,25},{... | collective-permute-start | bytes 786440 | tf_op jit(solution)/shard_map/ppermute | solution.py:854
  426.0 1.7 bitcast_dynamic-update-slice_fusion.19
  434.4 2.5 collective-permute-done.16
  439.5 13.6 %collective-permute-done.18 = bf16[1024,128]{1,0:T(8,128)(2,1)S(1)} collective-permute-done((bf16[1024,128]{1,0:T(8,128)(2,1)S(1)}, bf16[1024,128]{1,0:T(8,128)(2,1)S(1)}, u32[]{:S(2)}, u32[]{:S(2)}) %collective-permute-start.18) | collective-permute-done | bytes 262176 | tf_op jit(solution)/shard_map/ppermute | solution.py:859
  456.8 21.4 %shard_map.472 = (bf16[1024,256]{1,0:T(8,128)(2,1)}, f32[768,1024]{1,0:T(8,128)}, f32[768,1024]{1,0:T(8,128)}, f32[8,8,128]{2,1,0:T(8,128)}, f32[8,256]{1,0:T(8,128)}) custom-call(s32[8]{0:T(128)} %stack.150.order, bf16[8,1024,128]{2,1,0:T(8,128)(2,1)} %bitcast_dynamic-update-slice_fusion.8.b0, bf16[8,1024,128]{2,1,0:T(8,128)(2,1)} %bitcast_dynamic-update-slice_fusion.b1, ...), custom_call_target="tpu_custom_call" | custom-call | tf_op jit(solution)/shard_map/pallas_call | solution.py:1135
  478.1 6.9 %copy.150 = f32[1,3,256,1024]{3,0,2,1:T(1,128)} copy(f32[1,3,256,1024]{3,2,1,0:T(8,128)} %bitcast.147) | data formatting | bytes 6291456 | tf_op jit(solution)/shard_map/stack | solution.py:1378
  485.1 4.9 copy.149
  490.0 1.7 bitcast_dynamic-update-slice_fusion.17
  492.4 12.0 %shard_map.468 = (bf16[1024,256]{1,0:T(8,128)(2,1)}, f32[3,1024,256]{2,1,0:T(8,128)}) custom-call(s32[8]{0:T(128)} %stack.150.order, bf16[8,1024,128]{2,1,0:T(8,128)(2,1)} %bitcast_dynamic-update-slice_fusion.16.blk, bf16[1024,256]{1,0:T(8,128)(2,1)} %get-tuple-element.65.G, f32[1024,8]{1,0:T(8,128)} %get-tuple-element.66.aux, bf16[3,1024,256]{2,1,0:T(8,128)(2,1)} %copy-done.1), custom_call_target="tpu_custom_call" | custom-call | tf_op jit(solution)/shard_map/pallas_call | solution.py:1076
  504.4 8.3 %multiply_reduce_fusion.2 = (f32[3]{0:T(128)S(1)}, f32[3]{0:T(128)S(1)}, f32[3,1024,256]{2,1,0:T(8,128)}, f32[3,1024,256]{2,1,0:T(8,128)}) fusion(f32[3,1024,256]{2,1,0:T(8,128)} %param.35, f32[3,1024,256]{2,1,0:T(8,128)} %get-tuple-element.93, f32[3,1024,256]{2,1,0:T(8,128)} %param.41, f32[3,1024,256]{2,1,0:T(8,128)} %param.47), kind=kLoop, calls=%fused_computation.13 | loop fusion | flops 13369338 | bytes 18874392 | tf_op jit(solution)/shard_map/reduce_sum | solution.py:1388
  514.4 39.4 %multiply_reduce_fusion = (f32[3]{0:T(128)S(1)}, f32[3,256,2,1024]{3,2,1,0:T(2,128)}, f32[3,256,2,1024]{3,2,1,0:T(2,128)}, f32[3,256,2,1024]{3,2,1,0:T(2,128)}, f32[3]{0:T(128)S(1)}) fusion(f32[3,256,2,1024]{3,2,1,0:T(2,128)S(1)} %bitcast.137, f32[1,3,256,1024]{3,0,2,1:T(1,128)S(1)} %copy-done.3, f32[1,3,256,1024]{3,0,2,1:T(1,128)S(1)} %copy-done.4, ...), kind=kLoop, calls=%fused_computation.5 | loop fusion | flops 28311544 | bytes 44040216 | tf_op jit(solution)/shard_map/reduce_sum | solution.py:1388
  554.5 41.4 %shard_map.473 = (bf16[8,128,256]{2,1,0:T(8,128)(2,1)}, bf16[8,128,256]{2,1,0:T(8,128)(2,1)}, f32[4,8,256]{2,1,0:T(8,128)}, f32[32,8,128]{2,1,0:T(8,128)}) custom-call(bf16[1024,256]{1,0:T(8,128)(2,1)} %get-tuple-element.67.lo, bf16[1024,256]{1,0:T(8,128)(2,1)} %get-tuple-element.87.dn, f32[8,256]{1,0:T(8,128)} %get-tuple-element.88.gg, ...), custom_call_target="tpu_custom_call" | custom-call | tf_op jit(solution)/shard_map/pallas_call | solution.py:1266
  603.1 16.5 %multiply_add_fusion = (f32[3,256,2,1024]{3,2,1,0:T(2,128)}, f32[3,256,2,1024]{3,2,1,0:T(2,128)}) fusion(f32[3,256,2,1024]{3,2,1,0:T(2,128)} %param.50, f32[3,256,2,1024]{3,2,1,0:T(2,128)} %param.32, f32[3,256,2,1024]{3,2,1,0:T(2,128)} %get-tuple-element.233, f32[3]{0:T(128)S(1)} %get-tuple-element.262), kind=kLoop, calls=%fused_computation.3 | loop fusion | flops 7864320 | bytes 31457292 | tf_op jit(solution)/shard_map/add | solution.py:1416
  620.6 4.7 multiply_add_fusion.3
  625.9 1.8 fusion.6
  (178 shorter events, 60.1 us)
Async XLA Ops:
  1.9 10.4 %copy-start.15 = (bf16[3,128,160]{1,2,0:T(8,128)(2,1)}, bf16[3,128,160]{1,2,0:T(8,128)(2,1)S(1)}, u32[]{:S(2)}) copy-start(bf16[3,128,160]{1,2,0:T(8,128)(2,1)S(1)} %get-tuple-element.255) | copy-start | bytes 368644
  228.7 151.1 %collective-permute-start = (bf16[1024,128]{1,0:T(8,128)(2,1)}, bf16[1024,128]{1,0:T(8,128)(2,1)}, u32[]{:S(2)}, u32[]{:S(2)}) collective-permute-start(bf16[1024,128]{1,0:T(8,128)(2,1)} %get-tuple-element.64), channel_id=1, source_target_pairs={{0,4},{4,0},{8,12},{12,8},{16,20},{20,16},{24,28},{28,24},{1,5},{5... | collective-permute-start | bytes 786440 | tf_op jit(solution)/shard_map/ppermute | solution.py:859
  230.4 153.2 %collective-permute-start.1 = (bf16[1024,128]{1,0:T(8,128)(2,1)}, bf16[1024,128]{1,0:T(8,128)(2,1)}, u32[]{:S(2)}, u32[]{:S(2)}) collective-permute-start(bf16[1024,128]{1,0:T(8,128)(2,1)} %get-tuple-element.64), channel_id=1, source_target_pairs={{0,8},{4,12},{8,16},{12,20},{16,24},{20,28},{24,0},{28,4},{1,9},{5... | collective-permute-start | bytes 786440 | tf_op jit(solution)/shard_map/ppermute | solution.py:854
  233.0 184.8 %collective-permute-start.3 = (bf16[1024,128]{1,0:T(8,128)(2,1)}, bf16[1024,128]{1,0:T(8,128)(2,1)}, u32[]{:S(2)}, u32[]{:S(2)}) collective-permute-start(bf16[1024,128]{1,0:T(8,128)(2,1)} %get-tuple-element.64), channel_id=1, source_target_pairs={{0,16},{4,20},{8,24},{12,28},{16,0},{20,4},{24,8},{28,12},{1,17},{... | collective-permute-start | bytes 786440 | tf_op jit(solution)/shard_map/ppermute | solution.py:854
  234.8 196.3 %collective-permute-start.5 = (bf16[1024,128]{1,0:T(8,128)(2,1)}, bf16[1024,128]{1,0:T(8,128)(2,1)}, u32[]{:S(2)}, u32[]{:S(2)}) collective-permute-start(bf16[1024,128]{1,0:T(8,128)(2,1)} %get-tuple-element.64), channel_id=1, source_target_pairs={{0,24},{4,28},{8,0},{12,4},{16,8},{20,12},{24,16},{28,20},{1,25},{... | collective-permute-start | bytes 786440 | tf_op jit(solution)/shard_map/ppermute | solution.py:854
  342.4 12.2 %copy-start.2 = (f32[1024,8]{1,0:T(8,128)S(1)}, f32[1024,8]{1,0:T(8,128)}, u32[]{:S(2)}) copy-start(f32[1024,8]{1,0:T(8,128)} %get-tuple-element.66.aux) | copy-start | bytes 98308
  350.9 37.6 %collective-permute-start.7 = (bf16[1024,128]{1,0:T(8,128)(2,1)}, bf16[1024,128]{1,0:T(8,128)(2,1)}, u32[]{:S(2)}, u32[]{:S(2)}) collective-permute-start(bf16[1024,128]{1,0:T(8,128)(2,1)} %get-tuple-element.83), channel_id=1, source_target_pairs={{0,4},{4,0},{8,12},{12,8},{16,20},{20,16},{24,28},{28,24},{1,5},{5... | collective-permute-start | bytes 786440 | tf_op jit(solution)/shard_map/ppermute | solution.py:859
  362.8 6.2 copy-start.9
  362.8 6.2 copy-start.19
  363.9 6.8 %copy-start.20 = (f32[25,128]{1,0:T(8,128)S(1)}, f32[25,128]{1,0:T(8,128)}, u32[]{:S(2)}) copy-start(f32[25,128]{1,0:T(8,128)} %ch.3) | copy-start | bytes 38404
  364.0 6.8 %copy-start.25 = (f32[25,128]{1,0:T(8,128)S(1)}, f32[25,128]{1,0:T(8,128)}, u32[]{:S(2)}) copy-start(f32[25,128]{1,0:T(8,128)} %param.54) | copy-start | bytes 38404
  364.0 6.7 %copy-start.26 = (f32[25,128]{1,0:T(8,128)S(1)}, f32[25,128]{1,0:T(8,128)}, u32[]{:S(2)}) copy-start(f32[25,128]{1,0:T(8,128)} %param.42) | copy-start | bytes 38404
  364.0 6.7 %copy-start.27 = (f32[25,128]{1,0:T(8,128)S(1)}, f32[25,128]{1,0:T(8,128)}, u32[]{:S(2)}) copy-start(f32[25,128]{1,0:T(8,128)} %param.48) | copy-start | bytes 38404
  364.0 6.7 %copy-start.28 = (f32[20,128]{1,0:T(8,128)S(1)}, f32[20,128]{1,0:T(8,128)}, u32[]{:S(2)}) copy-start(f32[20,128]{1,0:T(8,128)} %get-tuple-element.100) | copy-start | bytes 30724
  364.0 6.7 %copy-start.31 = (f32[8,128]{1,0:T(8,128)S(1)}, f32[8,128]{1,0:T(8,128)}, u32[]{:S(2)}) copy-start(f32[8,128]{1,0:T(8,128)} %get-tuple-element.99) | copy-start | bytes 12292
  376.3 15.5 %copy-start.22 = (bf16[1024,128]{1,0:T(8,128)(2,1)S(1)}, bf16[1024,128]{1,0:T(8,128)(2,1)}, u32[]{:S(2)}) copy-start(bf16[1024,128]{1,0:T(8,128)(2,1)} %get-tuple-element.84) | copy-start | bytes 786436
  379.8 12.0 %collective-permute-start.8 = (bf16[1024,128]{1,0:T(8,128)(2,1)S(1)}, bf16[1024,128]{1,0:T(8,128)(2,1)S(1)}, u32[]{:S(2)}, u32[]{:S(2)}) collective-permute-start(bf16[1024,128]{1,0:T(8,128)(2,1)S(1)} %copy-done.21), channel_id=1, source_target_pairs={{0,8},{4,12},{8,16},{12,20},{16,24},{20,28},{24,0},{28,4},{1,9},{5... | collective-permute-start | bytes 786440 | tf_op jit(solution)/shard_map/ppermute | solution.py:854
  383.5 24.2 %collective-permute-start.10 = (bf16[1024,128]{1,0:T(8,128)(2,1)S(1)}, bf16[1024,128]{1,0:T(8,128)(2,1)S(1)}, u32[]{:S(2)}, u32[]{:S(2)}) collective-permute-start(bf16[1024,128]{1,0:T(8,128)(2,1)S(1)} %copy-done.21), channel_id=1, source_target_pairs={{0,16},{4,20},{8,24},{12,28},{16,0},{20,4},{24,8},{28,12},{1,17},{... | collective-permute-start | bytes 786440 | tf_op jit(solution)/shard_map/ppermute | solution.py:854
  388.5 7.7 %collective-permute-start.14 = (bf16[1024,128]{1,0:T(8,128)(2,1)}, bf16[1024,128]{1,0:T(8,128)(2,1)S(1)}, u32[]{:S(2)}, u32[]{:S(2)}) collective-permute-start(bf16[1024,128]{1,0:T(8,128)(2,1)} %get-tuple-element.84), channel_id=1, source_target_pairs={{0,4},{4,0},{8,12},{12,8},{16,20},{20,16},{24,28},{28,24},{1,5},{5... | collective-permute-start | bytes 786440 | tf_op jit(solution)/shard_map/ppermute | solution.py:859
  391.8 10.4 %collective-permute-start.15 = (bf16[1024,128]{1,0:T(8,128)(2,1)S(1)}, bf16[1024,128]{1,0:T(8,128)(2,1)S(1)}, u32[]{:S(2)}, u32[]{:S(2)}) collective-permute-start(bf16[1024,128]{1,0:T(8,128)(2,1)S(1)} %copy-done.22), channel_id=1, source_target_pairs={{0,8},{4,12},{8,16},{12,20},{16,24},{20,28},{24,0},{28,4},{1,9},{5... | collective-permute-start | bytes 786440 | tf_op jit(solution)/shard_map/ppermute | solution.py:854
  396.2 9.9 %collective-permute-start.9 = (bf16[1024,128]{1,0:T(8,128)(2,1)S(1)}, bf16[1024,128]{1,0:T(8,128)(2,1)S(1)}, u32[]{:S(2)}, u32[]{:S(2)}) collective-permute-start(bf16[1024,128]{1,0:T(8,128)(2,1)S(1)} %collective-permute-done.8), channel_id=1, source_target_pairs={{0,4},{4,0},{8,12},{12,8},{16,20},{20,16},{24,28},{28,24},{1,5},{5... | collective-permute-start | bytes 786440 | tf_op jit(solution)/shard_map/ppermute | solution.py:859
  402.2 27.3 %collective-permute-start.12 = (bf16[1024,128]{1,0:T(8,128)(2,1)S(1)}, bf16[1024,128]{1,0:T(8,128)(2,1)S(1)}, u32[]{:S(2)}, u32[]{:S(2)}) collective-permute-start(bf16[1024,128]{1,0:T(8,128)(2,1)S(1)} %copy-done.21), channel_id=1, source_target_pairs={{0,24},{4,28},{8,0},{12,4},{16,8},{20,12},{24,16},{28,20},{1,25},{... | collective-permute-start | bytes 786440 | tf_op jit(solution)/shard_map/ppermute | solution.py:854
  406.1 9.8 %collective-permute-start.2 = (bf16[1024,128]{1,0:T(8,128)(2,1)}, bf16[1024,128]{1,0:T(8,128)(2,1)S(1)}, u32[]{:S(2)}, u32[]{:S(2)}) collective-permute-start(bf16[1024,128]{1,0:T(8,128)(2,1)} %collective-permute-done.1), channel_id=1, source_target_pairs={{0,4},{4,0},{8,12},{12,8},{16,20},{20,16},{24,28},{28,24},{1,5},{5... | collective-permute-start | bytes 786440 | tf_op jit(solution)/shard_map/ppermute | solution.py:859
  407.8 24.6 %collective-permute-start.17 = (bf16[1024,128]{1,0:T(8,128)(2,1)S(1)}, bf16[1024,128]{1,0:T(8,128)(2,1)S(1)}, u32[]{:S(2)}, u32[]{:S(2)}) collective-permute-start(bf16[1024,128]{1,0:T(8,128)(2,1)S(1)} %copy-done.22), channel_id=1, source_target_pairs={{0,16},{4,20},{8,24},{12,28},{16,0},{20,4},{24,8},{28,12},{1,17},{... | collective-permute-start | bytes 786440 | tf_op jit(solution)/shard_map/ppermute | solution.py:854
  415.9 11.8 %collective-permute-start.11 = (bf16[1024,128]{1,0:T(8,128)(2,1)S(1)}, bf16[1024,128]{1,0:T(8,128)(2,1)S(1)}, u32[]{:S(2)}, u32[]{:S(2)}) collective-permute-start(bf16[1024,128]{1,0:T(8,128)(2,1)S(1)} %collective-permute-done.10), channel_id=1, source_target_pairs={{0,4},{4,0},{8,12},{12,8},{16,20},{20,16},{24,28},{28,24},{1,5},{5... | collective-permute-start | bytes 786440 | tf_op jit(solution)/shard_map/ppermute | solution.py:859
  417.8 15.3 %collective-permute-start.19 = (bf16[1024,128]{1,0:T(8,128)(2,1)S(1)}, bf16[1024,128]{1,0:T(8,128)(2,1)S(1)}, u32[]{:S(2)}, u32[]{:S(2)}) collective-permute-start(bf16[1024,128]{1,0:T(8,128)(2,1)S(1)} %copy-done.22), channel_id=1, source_target_pairs={{0,24},{4,28},{8,0},{12,4},{16,8},{20,12},{24,16},{28,20},{1,25},{... | collective-permute-start | bytes 786440 | tf_op jit(solution)/shard_map/ppermute | solution.py:854
  427.6 9.2 %collective-permute-start.16 = (bf16[1024,128]{1,0:T(8,128)(2,1)S(1)}, bf16[1024,128]{1,0:T(8,128)(2,1)S(1)}, u32[]{:S(2)}, u32[]{:S(2)}) collective-permute-start(bf16[1024,128]{1,0:T(8,128)(2,1)S(1)} %collective-permute-done.15), channel_id=1, source_target_pairs={{0,4},{4,0},{8,12},{12,8},{16,20},{20,16},{24,28},{28,24},{1,5},{5... | collective-permute-start | bytes 786440 | tf_op jit(solution)/shard_map/ppermute | solution.py:859
  429.6 25.0 %collective-permute-start.4 = (bf16[1024,128]{1,0:T(8,128)(2,1)}, bf16[1024,128]{1,0:T(8,128)(2,1)S(1)}, u32[]{:S(2)}, u32[]{:S(2)}) collective-permute-start(bf16[1024,128]{1,0:T(8,128)(2,1)} %collective-permute-done.3), channel_id=1, source_target_pairs={{0,4},{4,0},{8,12},{12,8},{16,20},{20,16},{24,28},{28,24},{1,5},{5... | collective-permute-start | bytes 786440 | tf_op jit(solution)/shard_map/ppermute | solution.py:859
  431.1 24.2 %collective-permute-start.13 = (bf16[1024,128]{1,0:T(8,128)(2,1)S(1)}, bf16[1024,128]{1,0:T(8,128)(2,1)S(1)}, u32[]{:S(2)}, u32[]{:S(2)}) collective-permute-start(bf16[1024,128]{1,0:T(8,128)(2,1)S(1)} %collective-permute-done.12), channel_id=1, source_target_pairs={{0,4},{4,0},{8,12},{12,8},{16,20},{20,16},{24,28},{28,24},{1,5},{5... | collective-permute-start | bytes 786440 | tf_op jit(solution)/shard_map/ppermute | solution.py:859
  432.3 59.3 %collective-permute-start.6 = (bf16[1024,128]{1,0:T(8,128)(2,1)}, bf16[1024,128]{1,0:T(8,128)(2,1)S(1)}, u32[]{:S(2)}, u32[]{:S(2)}) collective-permute-start(bf16[1024,128]{1,0:T(8,128)(2,1)} %collective-permute-done.5), channel_id=1, source_target_pairs={{0,4},{4,0},{8,12},{12,8},{16,20},{20,16},{24,28},{28,24},{1,5},{5... | collective-permute-start | bytes 786440 | tf_op jit(solution)/shard_map/ppermute | solution.py:859
  433.1 20.0 %collective-permute-start.18 = (bf16[1024,128]{1,0:T(8,128)(2,1)S(1)}, bf16[1024,128]{1,0:T(8,128)(2,1)S(1)}, u32[]{:S(2)}, u32[]{:S(2)}) collective-permute-start(bf16[1024,128]{1,0:T(8,128)(2,1)S(1)} %collective-permute-done.17), channel_id=1, source_target_pairs={{0,4},{4,0},{8,12},{12,8},{16,20},{20,16},{24,28},{28,24},{1,5},{5... | collective-permute-start | bytes 786440 | tf_op jit(solution)/shard_map/ppermute | solution.py:859
  436.9 19.2 %collective-permute-start.20 = (bf16[1024,128]{1,0:T(8,128)(2,1)S(1)}, bf16[1024,128]{1,0:T(8,128)(2,1)S(1)}, u32[]{:S(2)}, u32[]{:S(2)}) collective-permute-start(bf16[1024,128]{1,0:T(8,128)(2,1)S(1)} %collective-permute-done.19), channel_id=1, source_target_pairs={{0,4},{4,0},{8,12},{12,8},{16,20},{20,16},{24,28},{28,24},{1,5},{5... | collective-permute-start | bytes 786440 | tf_op jit(solution)/shard_map/ppermute | solution.py:859
  478.1 6.9 %copy-start.12 = (f32[768,1024]{1,0:T(8,128)S(1)}, f32[768,1024]{1,0:T(8,128)}, u32[]{:S(2)}) copy-start(f32[768,1024]{1,0:T(8,128)} %get-tuple-element.89) | copy-start | bytes 9437188
  492.4 20.4 %slice-start = ((s8[6291456]{0:T(1024)(128)(4,1)}), s8[2097152]{0:T(1024)(128)(4,1)S(1)}, s32[]{:S(2)}) async-start(s8[6291456]{0:T(1024)(128)(4,1)} %bitcast.136), calls=%async_computation | async-start | bytes 4194304
  504.4 8.3 %slice-start.1 = ((s8[6291456]{0:T(1024)(128)(4,1)}), s8[4194304]{0:T(1024)(128)(4,1)S(1)}, s32[]{:S(2)}) async-start(s8[6291456]{0:T(1024)(128)(4,1)} %bitcast.136), calls=%async_computation.1 | async-start | bytes 8388608
  504.4 8.6 %copy-start.3 = (f32[1,3,256,1024]{3,0,2,1:T(1,128)S(1)}, f32[1,3,256,1024]{3,0,2,1:T(1,128)}, u32[]{:S(2)}) copy-start(f32[1,3,256,1024]{3,0,2,1:T(1,128)} %copy.150) | copy-start | bytes 9437188
  504.4 10.0 %copy-start.4 = (f32[1,3,256,1024]{3,0,2,1:T(1,128)S(1)}, f32[1,3,256,1024]{3,0,2,1:T(1,128)}, u32[]{:S(2)}) copy-start(f32[1,3,256,1024]{3,0,2,1:T(1,128)} %copy.149) | copy-start | bytes 9437188
  514.4 39.4 %copy-start.33 = (f32[3]{0:T(128)S(1)}, f32[3]{0:T(128)}, u32[]{:S(2)}) copy-start(f32[3]{0:T(128)} %get-tuple-element.211) | copy-start | bytes 40
  514.4 39.4 %copy-start.34 = (f32[3]{0:T(128)S(1)}, f32[3]{0:T(128)}, u32[]{:S(2)}) copy-start(f32[3]{0:T(128)} %get-tuple-element.212) | copy-start | bytes 40
  514.4 39.4 %copy-start.35 = (f32[3]{0:T(128)S(1)}, f32[3]{0:T(128)}, u32[]{:S(2)}) copy-start(f32[3]{0:T(128)} %get-tuple-element.229) | copy-start | bytes 40
  603.1 16.6 %copy-start.14 = (f32[3,16,1024]{2,1,0:T(8,128)S(1)}, f32[3,16,1024]{2,1,0:T(8,128)}, u32[]{:S(2)}) copy-start(f32[3,16,1024]{2,1,0:T(8,128)} %param.34) | copy-start | bytes 589828
  603.1 16.6 %copy-start.16 = (f32[3,16,1024]{2,1,0:T(8,128)S(1)}, f32[3,16,1024]{2,1,0:T(8,128)}, u32[]{:S(2)}) copy-start(f32[3,16,1024]{2,1,0:T(8,128)} %get-tuple-element.238) | copy-start | bytes 589828
  603.1 16.6 %copy-start.17 = (f32[3,16,1024]{2,1,0:T(8,128)S(1)}, f32[3,16,1024]{2,1,0:T(8,128)}, u32[]{:S(2)}) copy-start(f32[3,16,1024]{2,1,0:T(8,128)} %get-tuple-element.239) | copy-start | bytes 589828
  603.1 16.6 %copy-start.23 = (f32[3,16,1024]{2,1,0:T(8,128)S(1)}, f32[3,16,1024]{2,1,0:T(8,128)}, u32[]{:S(2)}) copy-start(f32[3,16,1024]{2,1,0:T(8,128)} %param.52) | copy-start | bytes 589828
  603.1 17.5 %copy-start = (f32[3,1024,256]{2,1,0:T(8,128)S(1)}, f32[3,1024,256]{2,1,0:T(8,128)}, u32[]{:S(2)}) copy-start(f32[3,1024,256]{2,1,0:T(8,128)} %param.35) | copy-start | bytes 9437188
  603.1 17.5 %copy-start.5 = (f32[3,1024,256]{2,1,0:T(8,128)S(1)}, f32[3,1024,256]{2,1,0:T(8,128)}, u32[]{:S(2)}) copy-start(f32[3,1024,256]{2,1,0:T(8,128)} %get-tuple-element.236) | copy-start | bytes 9437188
  603.1 17.4 %copy-start.6 = (f32[3,1024,256]{2,1,0:T(8,128)S(1)}, f32[3,1024,256]{2,1,0:T(8,128)}, u32[]{:S(2)}) copy-start(f32[3,1024,256]{2,1,0:T(8,128)} %get-tuple-element.237) | copy-start | bytes 9437188
  603.1 17.4 %copy-start.13 = (f32[3,1024,256]{2,1,0:T(8,128)S(1)}, f32[3,1024,256]{2,1,0:T(8,128)}, u32[]{:S(2)}) copy-start(f32[3,1024,256]{2,1,0:T(8,128)} %param.53) | copy-start | bytes 9437188
  (14 other events, 57.4 us)

commit v2 on v1

--- a/solution.py
+++ b/solution.py
@@ -582,6 +582,48 @@
     return [pltpu.VMEM((n, T // n, R), F32), pltpu.VMEM((n, slabs, LANES), F32)] + [dma((n,))] * 8
 
 
+class RowGather:
+    def __init__(self, S, own, place_of, zs, zr, xs, xr, ls):
+        s, p, z, x = place(S, 1)
+        self.zn = zn = S // 2
+        other = {"seq": 2 * z + 1 - x}
+        at = lambda k: 2 * lax.rem(z - k + zn, zn) + x
+        self.local = pltpu.make_async_copy(own, place_of(s), ls)
+        self.z = [
+            seq_copy(own, place_of(s), zs.at[k], zr.at[k], {"seq": 2 * lax.rem(z + k, zn) + x})
+            for k in range(1, zn)
+        ]
+        self.x = [
+            seq_copy(
+                own if k == 0 else place_of(at(k)), place_of(at(k)), xs.at[k], xr.at[k], other
+            )
+            for k in range(zn)
+        ]
+
+    def start(self):
+        self.local.start()
+        for cp in self.z:
+            cp.start()
+        self.x[0].start()
+
+    def forward(self):
+        for k in range(1, self.zn):
+            self.z[k - 1].wait_recv()
+            self.x[k].start()
+
+    def finish(self):
+        self.local.wait()
+        for cp in self.z:
+            cp.wait_send()
+        for cp in self.x:
+            cp.wait()
+
+    @staticmethod
+    def semaphores(S):
+        dma = pltpu.SemaphoreType.DMA
+        return [dma((S // 2,))] * 4 + [dma]
+
+
 def softplus(v):
     u = jnp.exp(-jnp.abs(v))
     w = 1.0 + u
@@ -596,17 +638,23 @@
     return total
 
 
-def forward_kernel(S, PN, *refs):
-    (tok, og, modrow, wdt_mine, gain_mine, wi, wg, wo, segs, ch, wlr, wbc) = refs[:12]
-    (act, conv, inner, low, bct, pre, H, gated, dgate, dmix, aux, X, NR, G, WD, INV) = refs[12:28]
-    rest = list(refs[28:])
+def block_kernel(S, PN, *refs):
+    rest = list(refs)
     take = lambda k: [rest.pop(0) for _ in range(k)]
-    tile, toks, ogs, nrm, Wi, Wg, Wo, AUX, GAIN = take(9)
+    tok, og, modrow, wdt_mine, gain_mine, wi, wg, wo, segs, ch, wlr, wbc, wxT = take(13)
+    LO, DN, GG, ROW, MORE, gx, gtap, gch, NR, G, AUXC, dall_out, gall_out, INV = take(14)
+    tile, toks, ogs, nrm, Wi, Wg, Wo, AUX, GAIN, WD = take(10)
     step, drive, keep, Y, pad, act3, lr, bcp = take(8)
+    act, conv, inner, low, bct, pre, H, gated, dgate, dmix, aux, X = take(12)
+    gall, dall, DS, DB, dst3, low3, dst, dlow, dbct, dact, gdt = take(11)
+    LR2, BCT2, tail, dpar, dinner, part, rowdot, ggs = take(8)
     ag1, ag2 = take(9), take(9)
     ws = take(12)
     ls = take(1)[0]
     sums = take(10)
+    rows_g, rows_d, rows_i = take(5), take(5), take(5)
+    mx, mr, ml = take(3)
+    last = take(8)
     s, p, z, x = place(S, PN)
     TL, DD = tok.shape
     T = S * TL
@@ -668,6 +716,7 @@
         return 0
 
     lax.fori_loop(0, S, columns, 0)
+    aux[T : T + 8, :] = jnp.zeros((8, 8), F32)
     tokens.finish()
     per = quarter // width
 
@@ -781,6 +830,13 @@
         return 0
 
     lax.fori_loop(0, T // rows, finish, 0)
+    gathers = [
+        RowGather(S, gated, lambda t: gall.at[t], *rows_g),
+        RowGather(S, dgate, lambda t: dall.at[t, :, C : 2 * C], *rows_d),
+        RowGather(S, dinner, lambda t: dall.at[t, :, 0:C], *rows_i),
+    ]
+    gathers[0].start()
+    gathers[1].start()
     mine = pl.ds(pl.multiple_of(lax.rem(s, per) * width, width), width)
     NR[...] = nrm[:, pl.ds(pl.multiple_of(s * width, width), width)]
 
@@ -788,10 +844,188 @@
         r = pl.ds(pl.multiple_of(t * TL, TL), TL)
         X[r, :] = toks[lax.div(s, per), t, :, mine]
         G[r, :] = ogs[lax.div(s, per), t, :, mine]
+        drive[r, :] = step[r, :] * act[r, :].astype(F32)
+        keep[r, :] = jnp.broadcast_to(aux[r, 6:7], (TL, C))
         return 0
 
     lax.fori_loop(0, S, own_features, 0)
     INV[...] = jnp.broadcast_to(inv, INV.shape)
+    scan_backward(
+        pre, H, dmix, act, bct, aux, ch, WD, low,
+        dlow, dbct, gdt, gch, dact, step, drive, keep, DS, DB, dst3, low3, dst,
+        [(T // LANES // 2, gathers[0].forward)],
+    )
+    gathers[1].forward()
+    h = R // S
+    part_dt = lambda d: gdt.at[:, pl.ds(pl.multiple_of(d * h, 8), h), :]
+    more = row_copies(S, part_dt, lambda t: MORE.at[t], mx, mr)
+    more_own = pltpu.make_async_copy(part_dt(s), MORE.at[s], ml)
+    for cp in more + [more_own]:
+        cp.start()
+    sum_over_all(S, PN, dlow, dbct, LR2, BCT2, *sums)
+    convolve_backward(
+        LR2, BCT2, act, conv, aux, ch, wxT, dact, dinner, gx, gtap, pad, tail, act3, dpar
+    )
+    gathers[2].start()
+    for cp in more + [more_own]:
+        cp.wait()
+    gathers[0].finish()
+    out_gall = pltpu.make_async_copy(gall, gall_out, ls.at[0])
+    out_gall.start()
+
+    def layer(i, _):
+        r = pl.ds(pl.multiple_of(i * big, big), big)
+
+        def add(b, total):
+            wide = gall[b, r, :].astype(F32)
+            for m in range(M):
+                total = total + dot(
+                    (wide * aux[r, m : m + 1]).astype(BF16), wo[b, m * C : (m + 1) * C, :]
+                )
+            return total
+
+        total = lax.fori_loop(0, S, add, jnp.zeros((big, width), F32))
+        part[0, r, :] = total.astype(BF16)
+        return 0
+
+    lax.fori_loop(0, T // big, layer, 0)
+    to_out = LastBlocks(S, PN, part.at[0], LO, last[0], last[1], ls.at[1])
+    to_out.start()
+    gathers[2].forward()
+    gathers[1].finish()
+    gathers[2].finish()
+    out_dall = pltpu.make_async_copy(dall, dall_out, ls.at[2])
+    out_dall.start()
+
+    def normed_back(i, total):
+        r = pl.ds(pl.multiple_of(i * big, big), big)
+
+        def add(b, accs):
+            d0, d1 = dall[b, r, 0:C], dall[b, r, C : 2 * C]
+            return tuple(
+                accs[m]
+                + dot(d0, wi[b, :, m * C : (m + 1) * C], NT)
+                + dot(d1, wg[b, :, m * C : (m + 1) * C], NT)
+                for m in range(M)
+            )
+
+        accs = lax.fori_loop(0, S, add, (jnp.zeros((big, width), F32),) * M)
+        d = accs[0] * aux[r, 0:1]
+        for m in range(1, M):
+            d = d + accs[m] * aux[r, m : m + 1]
+        scaled = X[r, :].astype(F32) * aux[r, 7:8]
+        gained = d * gain_mine[0:1, :]
+        part[1, r, :] = gained.astype(BF16)
+        along = jnp.sum(gained * scaled, axis=1, keepdims=True)
+        for j in range(big // TL):
+            turned = jnp.transpose(jnp.broadcast_to(along[j * TL : (j + 1) * TL], (TL, LANES)))
+            rowdot[i * (big // TL) + j] = turned[0:8]
+        return total + jnp.sum(d * scaled, axis=0, keepdims=True)
+
+    total = lax.fori_loop(0, T // big, normed_back, jnp.zeros((1, width), F32))
+    ggs[...] = jnp.broadcast_to(total, ggs.shape)
+    to_in = LastBlocks(S, PN, part.at[1], DN, last[2], last[3], ls.at[3])
+    to_in.start()
+    gains = [
+        seq_copy(ggs, GG.at[k], last[4].at[k], last[5].at[k], {"tp": lax.rem(p + k, PN)})
+        for k in range(1, PN)
+    ]
+    for cp in gains:
+        cp.start()
+    n = S * PN
+    me = s * PN + p
+
+    def tile_copy(k):
+        j = lax.rem(me + k, n)
+        device = {"seq": lax.div(j, PN), "tp": lax.rem(j, PN)}
+        return seq_copy(
+            rowdot.at[lax.div(j, PN)], ROW.at[k], last[6].at[k], last[7].at[k], device
+        )
+
+    def send_tile(k, _):
+        tile_copy(k).start()
+        return 0
+
+    def wait_tile(k, _):
+        tile_copy(k).wait()
+        return 0
+
+    lax.fori_loop(1, n, send_tile, 0)
+    GG[0] = ggs[...]
+    ROW[0] = rowdot[s]
+    AUXC[...] = aux[0:T, :]
+    for cp in gains:
+        cp.wait()
+    lax.fori_loop(1, n, wait_tile, 0)
+    to_out.finish()
+    to_in.finish()
+    out_gall.wait()
+    out_dall.wait()
+
+
+class LastBlocks:
+    def __init__(self, S, PN, part, out, send, recv, ls):
+        s, p = lax.axis_index("seq"), lax.axis_index("tp")
+        ratio = S // PN
+        self.S, self.PN, self.ratio = S, PN, ratio
+        self.s, self.p, self.home = s, p, lax.div(s, ratio)
+        self.slot = lax.rem(s, ratio) * PN + p
+        self.part, self.out, self.send, self.recv, self.ls = part, out, send, recv, ls
+        self.TL = part.shape[0] // S
+
+    def away(self, k):
+        return jnp.logical_or(self.s != k, self.home != self.p)
+
+    def copy(self, k):
+        return seq_copy(
+            self.part.at[pl.ds(k * self.TL, self.TL)],
+            self.out.at[self.slot],
+            self.send.at[k],
+            self.recv.at[self.slot],
+            {"seq": k, "tp": self.home},
+        )
+
+    def own(self, k):
+        return pltpu.make_async_copy(
+            self.part.at[pl.ds(k * self.TL, self.TL)], self.out.at[self.slot], self.ls
+        )
+
+    def start(self):
+        for k in range(self.S):
+
+            @pl.when(self.away(k))
+            def _():
+                self.copy(k).start()
+
+            @pl.when(jnp.logical_not(self.away(k)))
+            def _():
+                self.own(k).start()
+
+    def finish(self):
+        for k in range(self.S):
+
+            @pl.when(self.away(k))
+            def _():
+                self.copy(k).wait_send()
+
+            @pl.when(jnp.logical_not(self.away(k)))
+            def _():
+                self.own(k).wait()
+
+        for h in range(self.ratio):
+            for q in range(self.PN):
+                t = self.ratio * self.p + h
+                i = h * self.PN + q
+
+                @pl.when(jnp.logical_or(t != self.s, self.p != q))
+                def _():
+                    seq_copy(
+                        self.part.at[0 : self.TL],
+                        self.out.at[i],
+                        self.send.at[0],
+                        self.recv.at[i],
+                        {"seq": t, "tp": q},
+                    ).wait_recv()
 
 
 def scan_forward(T, C, bct, ch, step, drive, keep, H, Y):
@@ -820,103 +1054,13 @@
     lax.fori_loop(0, T // LANES, chunk, jnp.zeros((N, C), F32))
 
 
-def forward_call(S, PN, args, T, C, width):
-    dma = pltpu.SemaphoreType.DMA
-    TL, DD = args[0].shape
-    chunks = T // LANES
-    f = lambda *shape: sds(shape)
-    b = lambda *shape: sds(shape, BF16)
-    vf = lambda *shape: pltpu.VMEM(shape, F32)
-    vb = lambda *shape: pltpu.VMEM(shape, BF16)
-    out = (
-        b(T, C), f(T, C), b(T, C), b(T, R), f(chunks, 2 * N, LANES), f(T, C), f(T + 1, N, C),
-        b(T, C), b(T, C), f(T, C), f(T, 8), b(T, width), b(T, width), b(T, width),
-        b(S, M, R // S, C), f(TL, LANES),
-    )
-    scratch = (
-        [vf(8, TL), vb(PN, S, TL, DD // PN), vb(PN, S, TL, DD // PN), vb(T, DD)]
-        + [vb(DD, M * C), vb(DD, M * C), vb(S, M * C, width), vf(S, 8, TL), vf(S, 8, width)]
-        + [vf(T, C)] * 4
-        + [vf(T + 8, C), vb(T, M * C), vf(T, R), vf(chunks, 2 * N, LANES)]
-        + Spread.semaphores(S) * 2
-        + [dma((S,))] * 12
-        + [dma((6,))]
-        + sum_scratch(S, PN, T)
-    )
-    return remote_call(
-        functools.partial(forward_kernel, S, PN), out, len(args), scratch, 0
-    )(*args)
-
-
-def row_gather(S, block):
-    across = [(i, i ^ 1) for i in range(S)]
-    near = [block] + [
-        lax.ppermute(block, "seq", [(i, (i + 2 * k) % S) for i in range(S)])
-        for k in range(1, S // 2)
-    ]
-    out = []
-    for blk in near:
-        out += [blk, lax.ppermute(blk, "seq", across)]
-    return jnp.stack(out)
-
-
-def row_order(S):
-    s = lax.axis_index("seq")
-    z, x = lax.div(s, 2), lax.rem(s, 2)
-    zn = S // 2
-    return jnp.stack(
-        [lax.rem(z - k + zn, zn) * 2 + xx for k in range(zn) for xx in (x, 1 - x)]
-    ).astype(jnp.int32)
-
-
-def backward_sum_kernel(S, PN, lr, bct, more, LR, BCT, MORE, sx, rx, lx, *sums):
-    greet_all(S, PN)
-    s = lax.axis_index("seq")
-    step = more.shape[1] // S
-    part = lambda d: more.at[:, pl.ds(pl.multiple_of(d * step, 8), step), :]
-    copies = row_copies(S, part, lambda t: MORE.at[t], sx, rx)
-    for cp in copies:
-        cp.start()
-    own = pltpu.make_async_copy(part(s), MORE.at[s], lx)
-    own.start()
-    sum_over_all(S, PN, lr, bct, LR, BCT, *sums)
-    own.wait()
-    for cp in copies:
-        cp.wait()
-
-
-def backward_sum(S, PN, lr, bct, more):
-    dma = pltpu.SemaphoreType.DMA
-    return remote_call(
-        functools.partial(backward_sum_kernel, S, PN),
-        (
-            sds(lr.shape, BF16),
-            sds(bct.shape),
-            sds((S, more.shape[0], more.shape[1] // S, more.shape[2])),
-        ),
-        3,
-        [dma((S,)), dma((S,)), dma] + sum_scratch(S, PN, lr.shape[0]),
-        2,
-    )(lr, bct, more)
-
-
-def unscan_kernel(
-    pre, H, dmix, act, bct, aux, ch, wdtT, low,
-    dlow, dbct, gdt, gch, dact, step, drive, keep, DS, DB, dst3, low3, dst,
+def scan_backward(
+    pre, H, dmix, act, bct, aux, ch, WD, low,
+    dlow, dbct, gdt, gch, dact, step, drive, keep, DS, DB, dst3, low3, dst, hooks,
 ):
     T, C = act.shape
     rows = 128
 
-    def prepare(i, _):
-        r = pl.ds(pl.multiple_of(i * rows, rows), rows)
-        sp = pre[r, :]
-        st = softplus(sp)
-        step[r, :] = st
-        drive[r, :] = st * act[r, :].astype(F32)
-        keep[r, :] = jnp.broadcast_to(aux[r, 6:7], (rows, C))
-        return 0
-
-    lax.fori_loop(0, T // rows, prepare, 0)
     base = -jnp.exp(ch[K + 2 + M : K + 2 + M + N, :])
     lane = lax.broadcasted_iota(jnp.int32, (N, LANES), 1)
     nothing = jnp.zeros((N, C), F32)
@@ -964,7 +1108,13 @@
         dbct[c, N : 2 * N, :] = accc
         return flow, hcur, gacc
 
-    _, _, gacc = lax.fori_loop(0, chunks, chunk, (nothing, H[T], nothing))
+    carry, done = (nothing, H[T], nothing), 0
+    for upto, call in hooks + [(chunks, None)]:
+        carry = lax.fori_loop(done, upto, chunk, carry)
+        done = upto
+        if call is not None:
+            call()
+    gacc = carry[2]
 
     def finish(i, carry):
         skip, bias = carry
@@ -983,7 +1133,12 @@
             sums.append(jnp.sum(masked, axis=0, keepdims=True))
             dst3[r, m * C : (m + 1) * C] = masked.astype(BF16)
             low3[r, m * R : (m + 1) * R] = (low_wide * mask).astype(BF16)
-        dlow[r, :] = dot(dst3[r, :], wdtT[...])
+        h = R // WD.shape[0]
+        for t in range(WD.shape[0]):
+            total = dot(dst3[r, 0:C], WD[t, 0], NT)
+            for m in range(1, M):
+                total = total + dot(dst3[r, m * C : (m + 1) * C], WD[t, m], NT)
+            dlow[r, t * h : (t + 1) * h] = total
         dact[r, :] = dmix[r, :] * ch[K + 1 : K + 2, :] + step[r, :] * back_b
         skip = skip + jnp.sum(dmix[r, :] * a, axis=0, keepdims=True)
         return skip, bias + jnp.concatenate(sums, axis=0)
@@ -998,25 +1153,24 @@
         gdt[m] = dot(low3[:, m * R : (m + 1) * R], dst[...], TN)
 
 
-def unconv_kernel(
-    dpar, act, conv, inner, aux, ch, wxT, dact, dinner, gx, gtap, pad, tail, dpar3, act3,
+def convolve_backward(
+    dlow, dbct, act, conv, aux, ch, wxT, dact, dinner, gx, gtap, pad, tail, act3, dpar,
 ):
     T, C = act.shape
-    XWID = dpar.shape[1]
     rows = 128
-    pad[0:8, :] = jnp.zeros((8, C), F32)
     tail[T : T + 8, :] = jnp.zeros((8, C), F32)
+    blank = jnp.zeros((LANES - 2 * N, LANES), F32)
 
     def fill(i, _):
         r = pl.ds(pl.multiple_of(i * rows, rows), rows)
-        pad[pl.ds(pl.multiple_of(i * rows + 8, 8), rows), :] = inner[r, :].astype(F32)
+        turned = jnp.transpose(jnp.concatenate([dbct[i], blank], axis=0))
+        dpar[r, 0:R] = dlow[r, :]
+        dpar[r, R : R + 2 * N] = turned[:, 0 : 2 * N].astype(BF16)
         wide = dpar[r, :].astype(F32)
-        a = act[r, :].astype(F32)
         total = dact[r, :]
         for m in range(M):
             mask = aux[r, m : m + 1]
             total = total + dot((wide * mask).astype(BF16), wxT[m])
-            act3[r, m * C : (m + 1) * C] = (a * mask).astype(BF16)
         v = conv[r, :]
         sig = 1.0 / (1.0 + jnp.exp(-v))
         tail[r, :] = (total * (sig * (1.0 + v * (1.0 - sig)))).astype(BF16).astype(F32)
@@ -1050,235 +1204,310 @@
         gx[m] = dot(act3[:, m * C : (m + 1) * C], dpar[...], TN)
 
 
-def out_kernel(order, blk, G, aux, w, layer, grad, masked, acc):
+def block_call(S, PN, args, T, C, width):
+    dma = pltpu.SemaphoreType.DMA
+    TL, DD = args[0].shape
+    chunks = T // LANES
+    f = lambda *shape: sds(shape)
+    b = lambda *shape: sds(shape, BF16)
+    vf = lambda *shape: pltpu.VMEM(shape, F32)
+    vb = lambda *shape: pltpu.VMEM(shape, BF16)
+    n = S * PN
+    out = (
+        b(S, TL, width), b(S, TL, width), f(PN, 8, width), f(n, 8, LANES),
+        f(S, M, R // S, C), f(M, C, R + 2 * N), f(8, C), f(1 + M + N, C),
+        b(T, width), b(T, width), f(T, 8), b(S, T, 2 * C), b(S, T, C), f(TL, LANES),
+    )
+    scratch = (
+        [vf(8, TL), vb(PN, S, TL, DD // PN), vb(PN, S, TL, DD // PN), vb(T, DD)]
+        + [vb(DD, M * C), vb(DD, M * C), vb(S, M * C, width), vf(S, 8, TL), vf(S, 8, width)]
+        + [vb(S, M, R // S, C)]
+        + [vf(T, C)] * 4
+        + [vf(T + 8, C), vb(T, M * C), vf(T, R), vf(chunks, 2 * N, LANES)]
+        + [vb(T, C), vf(T, C), vb(T, C), vb(T, R), vf(chunks, 2 * N, LANES), vf(T, C)]
+        + [vf(T + 1, N, C), vb(T, C), vb(T, C), vf(T, C), vf(T + 8, 8), vb(T, width)]
+        + [vb(S, T, C), vb(S, T, 2 * C), vf(T, C), vf(T, C), vb(T, M * C), vb(T, M * R)]
+        + [vb(T, C), vf(T, R), vf(chunks, 2 * N, LANES), vf(T, C), vf(M, R, C)]
+        + [vb(T, R), vf(chunks, 2 * N, LANES), vf(T + 8, C), vb(T, R + 2 * N), vb(T, C)]
+        + [vb(2, T, width), vf(S, 8, LANES), vf(8, width)]
+        + Spread.semaphores(S) * 2
+        + [dma((S,))] * 12
+        + [dma((6,))]
+        + sum_scratch(S, PN, T)
+        + RowGather.semaphores(S) * 3
+        + [dma((S,)), dma((S,)), dma]
+        + [dma((S,))] * 4 + [dma((PN,))] * 2 + [dma((n,))] * 2
+    )
+    vm, hb = pl.BlockSpec(memory_space=pltpu.VMEM), pl.BlockSpec(memory_space=pl.ANY)
+    return pl.pallas_call(
+        functools.partial(block_kernel, S, PN),
+        out_shape=out,
+        in_specs=[vm] * len(args),
+        out_specs=[hb if i in (11, 12) else vm for i in range(len(out))],
+        scratch_shapes=scratch,
+        compiler_params=pltpu.CompilerParams(
+            collective_id=0, has_side_effects=True, vmem_limit_bytes=VMEM_LIMIT
+        ),
+    )(*args)
+
+
+def cast_kernel(w_in, w_out, wi, wg, wo):
+    S, width, C = wi.shape
+    stride = 2 * S
+    for b in range(S):
+        wi[b] = w_in[pl.ds(2 * b, width, stride=stride), :].astype(BF16)
+        wg[b] = w_in[pl.ds(2 * b + 1, width, stride=stride), :].astype(BF16)
+        wo[b] = w_out[0, b * C : (b + 1) * C, :].astype(BF16)
+
+
+def cast_weights(S, flat, w_out):
+    _, inner_width, width = w_out.shape
+    C = inner_width // S
+    return pl.pallas_call(
+        cast_kernel,
+        out_shape=(
+            sds((S, width, M * C), BF16),
+            sds((S, width, M * C), BF16),
+            sds((S, M * C, width), BF16),
+        ),
+        grid=(M,),
+        in_specs=[
+            pl.BlockSpec((width * 2 * S, C), lambda m: (m, 0)),
+            pl.BlockSpec((1, inner_width, width), lambda m: (m, 0, 0)),
+        ],
+        out_specs=[
+            pl.BlockSpec((S, width, C), lambda m: (0, 0, m)),
+            pl.BlockSpec((S, width, C), lambda m: (0, 0, m)),
+            pl.BlockSpec((S, C, width), lambda m: (0, m, 0)),
+        ],
+        compiler_params=pltpu.CompilerParams(vmem_limit_bytes=VMEM_LIMIT),
+    )(flat, w_out)
+
+
+def to_rows(w, S):
+    m, width, two, channels = w.shape
+    c = channels // S
+    return w.reshape(m, width, two, S, c).transpose(0, 1, 3, 2, 4).reshape(-1, c)
+
+
+def from_rows(rows, S, shape):
+    m, width, two, channels = shape
+    c = channels // S
+    return rows.reshape(m, width, S, two, c).transpose(0, 1, 3, 2, 4).reshape(shape)
+
+
+def adam_terms(g, m, s):
+    new_m = BETA_ONE * m + (1.0 - BETA_ONE) * g
+    new_s = BETA_TWO * s + (1.0 - BETA_TWO) * (g * g)
+    root = jnp.sqrt(new_s * (1.0 / (1.0 - BETA_TWO**STEP))) + ADAM_EPSILON
+    return new_m, new_s, (new_m * (1.0 / (1.0 - BETA_ONE**STEP))) / root
+
+
+def corner(shape, row, value):
+    at = lambda k: lax.broadcasted_iota(jnp.int32, shape, k)
+    return jnp.where(jnp.logical_and(at(0) == row, at(1) == 0), value, 0.0)
+
+
+def adam_in_kernel(NR, aux, dall, w, m, s, nm, ns, dr, norms, turned, gs):
     i = pl.program_id(0)
-    T, C = blk.shape[1:]
+    T, width = NR.shape
+    S = dall.shape[0]
+    C = dall.shape[2] // 2
+    mask = aux[:, 0:1]
+    for k in range(1, M):
+        mask = jnp.where(i == k, aux[:, k : k + 1], mask)
+    turned[...] = jnp.transpose((NR[...].astype(F32) * mask).astype(BF16))
+    for b in range(S):
+        g = dot(turned[...], dall[b])
+        gs[pl.ds(2 * b, width, stride=2 * S), :] = g[:, 0:C]
+        gs[pl.ds(2 * b + 1, width, stride=2 * S), :] = g[:, C : 2 * C]
+    rows = 256
+
+    def body(k, sums):
+        r = pl.ds(pl.multiple_of(k * rows, rows), rows)
+        weight = w[r, :]
+        new_m, new_s, ratio = adam_terms(gs[r, :], m[r, :], s[r, :])
+        direction = ratio + WEIGHT_DECAY * weight
+        nm[r, :] = new_m
+        ns[r, :] = new_s
+        dr[r, :] = direction
+        fold = lambda v: jnp.sum((v * v).reshape(rows // 8, 8, C), axis=0)
+        return sums[0] + fold(weight), sums[1] + fold(direction)
+
+    zero = jnp.zeros((8, C), F32)
+    a, b = lax.fori_loop(0, w.shape[0] // rows, body, (zero, zero))
+    norms[0, 0] = a
+    norms[0, 1] = b
+
+
+def adam_in(NR, aux, dall, w, m, s):
+    T, width = NR.shape
+    S, _, two = dall.shape
+    C = two // 2
+    piece = pl.BlockSpec((width * 2 * S, C), lambda i: (i, 0))
+    whole = lambda shape: pl.BlockSpec(shape, lambda i: (0,) * len(shape))
+    return pl.pallas_call(
+        adam_in_kernel,
+        out_shape=(sds(w.shape), sds(w.shape), sds(w.shape), sds((M, 2, 8, C))),
+        grid=(M,),
+        in_specs=[whole((T, width)), whole((T, 8)), whole(dall.shape), piece, piece, piece],
+        out_specs=[piece, piece, piece, pl.BlockSpec((1, 2, 8, C), lambda i: (i, 0, 0, 0))],
+        scratch_shapes=[pltpu.VMEM((width, T), BF16), pltpu.VMEM((width * 2 * S, C), F32)],
+        compiler_params=pltpu.CompilerParams(vmem_limit_bytes=VMEM_LIMIT),
+    )(NR, aux, dall, w, m, s)
+
+
+def adam_out_kernel(gall, G, aux, w, m, s, nm, ns, dr, norms, turned):
+    i = pl.program_id(0)
+    T, C = gall.shape[1:]
+    wide = gall[0].astype(F32)
 
     @pl.when(i == 0)
     def _():
-        acc[...] = jnp.zeros(acc.shape, F32)
-
-    wide = blk[0].astype(F32)
+        norms[...] = jnp.zeros(norms.shape, F32)
+
+    for k in range(M):
+        turned[...] = jnp.transpose((wide * aux[:, k : k + 1]).astype(BF16))
+        weight = w[k]
+        new_m, new_s, ratio = adam_terms(dot(turned[...], G[...]), m[k], s[k])
+        direction = ratio + WEIGHT_DECAY * weight
+        nm[k] = new_m
+        ns[k] = new_s
+        dr[k] = direction
+        fold = lambda v: jnp.sum((v * v).reshape(C // 8, 8, v.shape[1]), axis=0)
+        norms[k, 0] += fold(weight)
+        norms[k, 1] += fold(direction)
+
+
+def adam_out(gall, G, aux, w, m, s):
+    S, T, C = gall.shape
+    width = G.shape[1]
+    piece = pl.BlockSpec((M, C, width), lambda i: (0, i, 0))
+    whole = lambda shape: pl.BlockSpec(shape, lambda i: (0,) * len(shape))
+    return pl.pallas_call(
+        adam_out_kernel,
+        out_shape=(sds(w.shape), sds(w.shape), sds(w.shape), sds((M, 2, 8, width))),
+        grid=(S,),
+        in_specs=[
+            pl.BlockSpec((1, T, C), lambda i: (i, 0, 0)),
+            whole((T, width)),
+            whole((T, 8)),
+            piece,
+            piece,
+            piece,
+        ],
+        out_specs=[piece, piece, piece, whole((M, 2, 8, width))],
+        scratch_shapes=[pltpu.VMEM((C, T), BF16)],
+        compiler_params=pltpu.CompilerParams(vmem_limit_bytes=VMEM_LIMIT),
+    )(gall, G, aux, w, m, s)
+
+
+def adam_small_kernel(
+    gx, more, gtap, gch, GG, wx, mx, sx, ax, wd, md, sd, ch, mc, sc, ac, gn, mg, sg, ag, nin, nout,
+    nmx, nsx, dx, nmd, nsd, dd, nwc, nmc, nsc, nac, nwg, nmg, nsg, nag, tile, gc, gd,
+):
+    S = more.shape[0]
+    C = more.shape[3]
+    total = jnp.zeros((8, LANES), F32)
+    lane = lax.broadcasted_iota(jnp.int32, total.shape, 1)
+
+    def put(total, k, value):
+        return jnp.where(lane == k, value, total)
+
+    square = lambda v: jnp.sum(v * v)
+    for t in range(S):
+        gd[:, :, t * C : (t + 1) * C] = more[t]
     for m in range(M):
-        masked[:, m * C : (m + 1) * C] = (wide * aux[:, m : m + 1]).astype(BF16)
-        acc[...] += dot(masked[:, m * C : (m + 1) * C], w[m])
-        grad[m] = dot(masked[:, m * C : (m + 1) * C], G[...], TN)
-
-    @pl.when(i == pl.num_programs(0) - 1)
-    def _():
-        layer[...] = acc[...].astype(BF16)
-
-
-def out_project(S, order, blocks, G, aux, w):
-    T, C = blocks.shape[1:]
-    width = G.shape[1]
-    whole = lambda shape: pl.BlockSpec(shape, lambda i, o: (0,) * len(shape))
-    return pl.pallas_call(
-        out_kernel,
-        out_shape=(sds((T, width), BF16), sds((M, S * C, width))),
-        grid_spec=pltpu.PrefetchScalarGridSpec(
-            num_scalar_prefetch=1,
-            grid=(S,),
-            in_specs=[
-                pl.BlockSpec((1, T, C), lambda i, o: (i, 0, 0)),
-                whole((T, width)),
-                whole((T, 8)),
-                pl.BlockSpec((M, C, width), lambda i, o: (0, o[i], 0)),
-            ],
-            out_specs=[whole((T, width)), pl.BlockSpec((M, C, width), lambda i, o: (0, o[i], 0))],
-            scratch_shapes=[pltpu.VMEM((T, M * C), BF16), pltpu.VMEM((T, width), F32)],
-        ),
-        compiler_params=pltpu.CompilerParams(vmem_limit_bytes=VMEM_LIMIT),
-    )(order, blocks, G, aux, w)
-
-
-def in_kernel(order, b0, b1, A3T, W0, W1, aux, gain, X, dnorm, grad0, grad1, rowdot, gg, acc):
-    i = pl.program_id(0)
-    T, width = X.shape
-
-    @pl.when(i == 0)
-    def _():
-        acc[...] = jnp.zeros(acc.shape, F32)
-
-    d0, d1 = b0[0], b1[0]
-    grad0[...] = dot(A3T[...], d0)
-    grad1[...] = dot(A3T[...], d1)
-    for m in range(M):
-        rows = slice(m * width, (m + 1) * width)
-        acc[m] += dot(d0, W0[rows, :], NT) + dot(d1, W1[rows, :], NT)
-
-    @pl.when(i == pl.num_programs(0) - 1)
-    def _():
-        rows = 128
-
-        def body(k, total):
-            r = pl.ds(pl.multiple_of(k * rows, rows), rows)
-            d = acc[0, r, :] * aux[r, 0:1]
-            for m in range(1, M):
-                d = d + acc[m, r, :] * aux[r, m : m + 1]
-            scaled = X[r, :].astype(F32) * aux[r, 7:8]
-            gained = d * gain[...]
-            dnorm[r, :] = gained.astype(BF16)
-            along = jnp.sum(gained * scaled, axis=1, keepdims=True)
-            rowdot[k] = jnp.transpose(jnp.broadcast_to(along, (rows, LANES)))[0:8]
-            return total + jnp.sum(d * scaled, axis=0, keepdims=True)
-
-        total = lax.fori_loop(0, T // rows, body, jnp.zeros((1, width), F32))
-        gg[...] = jnp.broadcast_to(total, gg.shape)
-
-
-def in_project_back(S, order, b0, b1, A3T, W0, W1, aux, gain, X):
-    T, C = b0.shape[1:]
-    width = X.shape[1]
-    whole = lambda shape: pl.BlockSpec(shape, lambda i, o: (0,) * len(shape))
-    piece = pl.BlockSpec((M * width, C), lambda i, o: (0, o[i]))
-    return pl.pallas_call(
-        in_kernel,
-        out_shape=(
-            sds((T, width), BF16),
-            sds((M * width, S * C)),
-            sds((M * width, S * C)),
-            sds((T // 128, 8, 128)),
-            sds((8, width)),
-        ),
-        grid_spec=pltpu.PrefetchScalarGridSpec(
-            num_scalar_prefetch=1,
-            grid=(S,),
-            in_specs=[
-                pl.BlockSpec((1, T, C), lambda i, o: (i, 0, 0)),
-                pl.BlockSpec((1, T, C), lambda i, o: (i, 0, 0)),
-                whole((M * width, T)),
-                piece,
-                piece,
-                whole((T, 8)),
-                whole((1, width)),
-                whole((T, width)),
-            ],
-            out_specs=[
-                whole((T, width)),
-                piece,
-                piece,
-                whole((T // 128, 8, 128)),
-                whole((8, width)),
-            ],
-            scratch_shapes=[pltpu.VMEM((M, T, width), F32)],
-        ),
-        compiler_params=pltpu.CompilerParams(vmem_limit_bytes=VMEM_LIMIT),
-    )(order, b0, b1, A3T, W0, W1, aux, gain, X)
-
-
-def last_kernel(S, PN, lo, dn, gg, tile, rowdot, LO, DN, GG, TILE, mine, los, lor, dns, dnr, gs, gr, ts, tr, ls):
+        total = put(total, m, jnp.sum(nin[m, 0]))
+        total = put(total, 4 * M + m, jnp.sum(nin[m, 1]))
+        total = put(total, 3 * M + m, jnp.sum(nout[m, 0]))
+        total = put(total, 7 * M + m, jnp.sum(nout[m, 1]))
+        new_m, new_s, ratio = adam_terms(gx[m], mx[m], sx[m])
+        direction = ratio + WEIGHT_DECAY * wx[m]
+        nmx[m] = new_m
+        nsx[m] = new_s
+        dx[m] = direction
+        total = put(total, M + m, square(wx[m]))
+        total = put(total, 5 * M + m, square(direction))
+        new_m, new_s, ratio = adam_terms(gd[m], md[m], sd[m])
+        direction = ratio + WEIGHT_DECAY * wd[m]
+        nmd[m] = new_m
+        nsd[m] = new_s
+        dd[m] = direction
+        total = put(total, 2 * M + m, square(wd[m]))
+        total = put(total, 6 * M + m, square(direction))
+    tile[...] = total
+    gc[0 : K + 1, :] = gtap[0 : K + 1, :]
+    gc[K + 1 :, :] = gch[...]
+    new_m, new_s, ratio = adam_terms(gc[...], mc[...], sc[...])
+    new = ch[...] - CHANNEL_RATE * ratio
+    nwc[...] = new
+    nmc[...] = new_m
+    nsc[...] = new_s
+    nac[...] = AVERAGE_KEEP * ac[...] + (1.0 - AVERAGE_KEEP) * new
+    g = GG[0, 0:1, :]
+    for q in range(1, GG.shape[0]):
+        g = g + GG[q, 0:1, :]
+    new_m, new_s, ratio = adam_terms(g, mg[...], sg[...])
+    new = gn[...] - GAIN_RATE * ratio
+    nwg[...] = new
+    nmg[...] = new_m
+    nsg[...] = new_s
+    nag[...] = AVERAGE_KEEP * ag[...] + (1.0 - AVERAGE_KEEP) * new
+
+
+def norms_kernel(S, PN, tile, TILE, ts, tr):
+    greet_all(S, PN)
     s, p = lax.axis_index("seq"), lax.axis_index("tp")
     n = S * PN
-    ratio = S // PN
     me = s * PN + p
-    home = lax.div(s, ratio)
-    slot = lax.rem(s, ratio) * PN + p
-    bar = pltpu.get_barrier_semaphore()
-
-    def device(j):
-        return {"seq": lax.div(j, PN), "tp": lax.rem(j, PN)}
-
-    def greet(k, _):
-        pl.semaphore_signal(
-            bar, inc=1, device_id=device(lax.rem(me + k, n)), device_id_type=MESH
-        )
-        return 0
-
-    lax.fori_loop(1, n, greet, 0)
-    first = lax.broadcasted_iota(jnp.int32, tile.shape, 0)
-    for b in range(S):
-        mine[b] = jnp.where(first == 1, rowdot[b], tile[...])
-    pl.semaphore_wait(bar, n - 1)
-    TL = lo.shape[0] // S
-
-    def block(k, start):
-        rows = pl.ds(k * TL, TL)
-        dev = {"seq": k, "tp": home}
-        away = jnp.logical_or(s != k, home != p)
-
-        @pl.when(away)
-        def _():
-            for cp in (
-                seq_copy(dn.at[rows], DN.at[slot], dns.at[k], dnr.at[slot], dev),
-                seq_copy(lo.at[rows], LO.at[slot], los.at[k], lor.at[slot], dev),
-            ):
-                if start:
-                    cp.start()
-                else:
-                    cp.wait_send()
-
-        if start:
-
-            @pl.when(jnp.logical_not(away))
-            def _():
-                a = pltpu.make_async_copy(dn.at[rows], DN.at[slot], ls.at[0])
-                b = pltpu.make_async_copy(lo.at[rows], LO.at[slot], ls.at[1])
-                a.start()
-                b.start()
-                a.wait()
-                b.wait()
-
-    def tiles(k):
+
+    def copy(k):
         j = lax.rem(me + k, n)
-        return seq_copy(mine.at[lax.div(j, PN)], TILE.at[k], ts.at[k], tr.at[k], device(j))
-
-    def send_tile(k, _):
-        tiles(k).start()
-        return 0
-
-    def wait_tile(k, _):
-        tiles(k).wait()
-        return 0
-
-    gains = [
-        seq_copy(gg, GG.at[k], gs.at[k], gr.at[k], {"tp": lax.rem(p + k, PN)})
-        for k in range(1, PN)
-    ]
-    for k in range(S):
-        block(k, True)
-    for cp in gains:
-        cp.start()
-    lax.fori_loop(1, n, send_tile, 0)
-    GG[0] = gg[...]
-    TILE[0] = mine[s]
-    for cp in gains:
-        cp.wait()
-    lax.fori_loop(1, n, wait_tile, 0)
-    for k in range(S):
-        block(k, False)
-    for h in range(ratio):
-        for q in range(PN):
-            t = ratio * p + h
-            i = h * PN + q
-
-            @pl.when(jnp.logical_or(t != s, p != q))
-            def _():
-                dev = {"seq": t, "tp": q}
-                seq_copy(dn.at[0:TL], DN.at[i], dns.at[0], dnr.at[i], dev).wait_recv()
-                seq_copy(lo.at[0:TL], LO.at[i], los.at[0], lor.at[i], dev).wait_recv()
-
-
-def last_exchange(S, PN, lo, dn, gg, tile, rowdot):
-    T, width = lo.shape
+        device = {"seq": lax.div(j, PN), "tp": lax.rem(j, PN)}
+        return seq_copy(tile, TILE.at[k], ts.at[k], tr.at[k], device)
+
+    def send(k, _):
+        copy(k).start()
+        return 0
+
+    def wait(k, _):
+        copy(k).wait()
+        return 0
+
+    lax.fori_loop(1, n, send, 0)
+    TILE[0] = tile[...]
+    lax.fori_loop(1, n, wait, 0)
+
+
+def norms_over_all(S, PN, tile):
     n = S * PN
     dma = pltpu.SemaphoreType.DMA
     return remote_call(
-        functools.partial(last_kernel, S, PN),
-        (
-            sds((S, T // S, width), BF16),
-            sds((S, T // S, width), BF16),
-            sds((PN,) + gg.shape),
-            sds((n,) + tile.shape),
-        ),
-        5,
-        [pltpu.VMEM((S,) + tile.shape, F32)]
-        + [dma((S,))] * 4
-        + [dma((PN,))] * 2
-        + [dma((n,))] * 2
-        + [dma((2,))],
-        3,
-    )(lo, dn, gg, tile, rowdot)
+        functools.partial(norms_kernel, S, PN), sds((n,) + tile.shape), 1, [dma((n,))] * 2, 1
+    )(tile)
+
+
+def final_rows_kernel(scale, w, dr, avg, nw, na):
+    k = scale[pl.program_id(0)]
+    new = w[...] - k * dr[...]
+    nw[...] = new
+    na[...] = AVERAGE_KEEP * avg[...] + (1.0 - AVERAGE_KEEP) * new
+
+
+def final_rows(scale, w, dr, avg, pieces):
+    shape = w.shape
+    rows = lambda v: v.reshape(M * pieces, -1, shape[-1])
+    block = pl.BlockSpec((1, w.size // shape[-1] // M // pieces, shape[-1]), lambda i: (i, 0, 0))
+    nw, na = pl.pallas_call(
+        final_rows_kernel,
+        out_shape=(sds(rows(w).shape), sds(rows(w).shape)),
+        grid=(M * pieces,),
+        in_specs=[pl.BlockSpec(memory_space=pltpu.SMEM), block, block, block],
+        out_specs=[block, block],
+        compiler_params=pltpu.CompilerParams(vmem_limit_bytes=VMEM_LIMIT),
+    )(jnp.repeat(scale, pieces), rows(w), rows(dr), rows(avg))
+    return nw.reshape(shape), na.reshape(shape)
 
 
 def local(
@@ -1289,21 +1518,14 @@
     average_in, average_x, average_dt, average_out, average_channel, average_gain,
 ):
     S, PN = lax.axis_size("seq"), lax.axis_size("tp")
-    s, p = lax.axis_index("seq"), lax.axis_index("tp")
+    p = lax.axis_index("tp")
     TL = tokens.shape[0]
     T = S * TL
     width = D // S
     inner_width = w_out.shape[1]
     C = inner_width // S
-    zn = S // 2
-    split = w_in.reshape(M, width, 2, S, C)
-    win = jnp.transpose(w_in, (2, 0, 1, 3)).astype(BF16).reshape(2, M * width, inner_width)
-    wi, wg = [
-        jnp.transpose(split[:, :, h], (2, 1, 0, 3)).astype(BF16).reshape(S, width, M * C)
-        for h in range(2)
-    ]
-    wout = w_out.astype(BF16)
-    wo = jnp.transpose(wout.reshape(M, S, C, width), (1, 0, 2, 3)).reshape(S, M * C, width)
+    flat_in = to_rows(w_in, S)
+    wi, wg, wo = cast_weights(S, flat_in, w_out)
     wx = w_x.astype(BF16)
     wlr = wx[:, :, :R].reshape(M * C, R)
     wbc = jnp.transpose(wx[:, :, R:], (2, 0, 1)).reshape(2 * N, M * C)
@@ -1313,121 +1535,70 @@
     zero = jnp.zeros((T,), F32)
     segs = jnp.stack([zero] * M + same + [same[K - 2], zero], axis=1)
     gain = norm_gain[None, :]
-    order = row_order(S)
-    chunks = T // LANES
-
-    act, conv, inner, low, bct, pre, H, gated, dgate, dmix, aux, X, NR, G, WD, INV = forward_call(
+    LO, DN, GG, ROW, MORE, gx, gtap, gch, NR, G, aux, dall, gall, INV = block_call(
         S,
         PN,
         (
             tokens, out_grad, modrow, w_dt.astype(BF16), jnp.broadcast_to(gain, (8, width)),
-            wi, wg, wo, segs, channel, wlr, wbc,
+            wi, wg, wo, segs, channel, wlr, wbc, jnp.transpose(wx, (0, 2, 1)),
         ),
         T, C, width,
     )
-    wdt = jnp.transpose(WD, (1, 0, 2, 3)).reshape(M, R, C)
-    col = lambda dtype=F32: pltpu.VMEM((T, C), dtype)
-    gated_all = row_gather(S, gated)
-    dgate_all = row_gather(S, dgate)
-
-    wdtT = jnp.transpose(wdt, (0, 2, 1)).reshape(M * C, R)
-    dlow, dbct, gdt, gch, dact = local_call(
-        unscan_kernel,
-        (
-            sds((T, R)),
-            sds((chunks, 2 * N, LANES)),
-            sds((M, R, C)),
-            sds((1 + M + N, C)),
-            sds((T, C)),
-        ),
-        9,
-        [col(), col(), col(), col(), col()]
-        + [pltpu.VMEM((T, M * C), BF16), pltpu.VMEM((T, M * R), BF16), col(BF16)],
-    )(pre, H, dmix, act, bct, aux, channel, wdtT, low)
-    dlow, dbct, gdt = backward_sum(S, PN, dlow, dbct, gdt)
-    dpar = jnp.concatenate(
-        [dlow, jnp.transpose(dbct, (0, 2, 1)).reshape(T, 2 * N).astype(BF16)], axis=1
-    )
-    grad_dt = jnp.transpose(gdt, (1, 2, 0, 3)).reshape(w_dt.shape)
-
-    dinner, grad_x, gtap = local_call(
-        unconv_kernel,
-        (sds((T, C), BF16), sds((M, C, R + 2 * N)), sds((8, C))),
-        8,
-        [
-            pltpu.VMEM((T + 8, C), F32),
-            pltpu.VMEM((T + 8, C), F32),
-            pltpu.VMEM((8, LANES), F32),
-            pltpu.VMEM((T, M * C), BF16),
-        ],
+    nm_in, ns_in, dir_in, norm_in = adam_in(
+        NR, aux, dall, flat_in, to_rows(moment_in, S), to_rows(square_in, S)
+    )
+    nm_out, ns_out, dir_out, norm_out = adam_out(gall, G, aux, w_out, moment_out, square_out)
+    like = lambda v: sds(v.shape)
+    row = lambda v: v[None, :]
+    vec = sds((1, width))
+    (
+        nm_x, ns_x, dir_x, nm_dt, ns_dt, dir_dt, nw_ch, nm_ch, ns_ch, na_ch,
+        nw_g, nm_g, ns_g, na_g, tile,
+    ) = local_call(
+        adam_small_kernel,
+        (like(w_x),) * 3 + (like(w_dt),) * 3 + (like(channel),) * 4 + (vec,) * 4
+        + (sds((8, LANES)),),
+        22,
+        [pltpu.VMEM(channel.shape, F32), pltpu.VMEM(w_dt.shape, F32)],
     )(
-        dpar, act, conv, inner, jnp.concatenate([aux, jnp.zeros((8, 8), F32)]), channel,
-        jnp.transpose(wx, (0, 2, 1)), dact,
-    )
-    dinner_all = row_gather(S, dinner)
-    grad_channel = jnp.concatenate([gtap[: K + 1], gch], axis=0)
-
-    layer_part, grad_out = out_project(S, order, gated_all, G, aux, wout)
-    A3T = jnp.concatenate(
-        [jnp.transpose(NR * aux[:, m : m + 1].astype(BF16)) for m in range(M)], axis=0
-    )
-    dnorm_part, gin0, gin1, rowdot, gg = in_project_back(
-        S, order, dinner_all, dgate_all, A3T, win[0], win[1], aux, gain, X
-    )
-    grad_in = jnp.transpose(
-        jnp.stack([gin0, gin1]).reshape(2, M, width, inner_width), (1, 2, 0, 3)
-    )
-
-    grads = [grad_in, grad_x, grad_dt, grad_out, grad_channel]
-    weights = (w_in, w_x, w_dt, w_out, channel, norm_gain)
-    moments = (moment_in, moment_x, moment_dt, moment_out, moment_channel, moment_gain)
-    squares = (square_in, square_x, square_dt, square_out, square_channel, square_gain)
-    averages = (average_in, average_x, average_dt, average_out, average_channel, average_gain)
-    adam_all = [adam_parts(grads[i], moments[i], squares[i]) for i in range(5)]
-    directions = [adam_all[i][2] + WEIGHT_DECAY * weights[i] for i in range(4)]
-    squared = lambda v: jnp.sum(v * v, axis=tuple(range(1, v.ndim)))
-    sums = jnp.concatenate([squared(v) for v in weights[:4]] + [squared(v) for v in directions])
-    tile = jnp.broadcast_to(jnp.pad(sums, (0, LANES - sums.shape[0]))[None], (8, LANES))
-    LO, DN, GG, TILE = last_exchange(S, PN, layer_part, dnorm_part, gg, tile, rowdot)
-
+        gx, MORE, gtap, gch, GG, w_x, moment_x, square_x, average_x,
+        w_dt, moment_dt, square_dt, channel, moment_channel, square_channel, average_channel,
+        gain, row(moment_gain), row(square_gain), row(average_gain), norm_in, norm_out,
+    )
+    TILE = norms_over_all(S, PN, tile)
     totals = jnp.sum(TILE[:, 0, : 8 * M], axis=0).reshape(2, 4, M)
-    along = jnp.sum(TILE[:, 1, :], axis=0)[:, None]
-    adam_all.append(adam_parts(jnp.sum(GG[:, 0, :], axis=0), moment_gain, square_gain))
+    scales = MATRIX_RATE * (jnp.sqrt(totals[0]) / jnp.sqrt(totals[1]))
+    nw_in, na_in = final_rows(scales[0], flat_in, dir_in, to_rows(average_in, S), 2)
+    nw_out, na_out = final_rows(scales[3], w_out, dir_out, average_out, 1)
+    nw_x = w_x - scales[1][:, None, None] * dir_x
+    nw_dt = w_dt - scales[2][:, None, None] * dir_dt
+    na_x = AVERAGE_KEEP * average_x + (1.0 - AVERAGE_KEEP) * nw_x
+    na_dt = AVERAGE_KEEP * average_dt + (1.0 - AVERAGE_KEEP) * nw_dt
 
     def columns(blocks):
         b = jnp.sum(blocks.reshape(S // PN, PN, TL, width).astype(F32), axis=1)
         return jnp.concatenate([b[h] for h in range(S // PN)], axis=1)
 
+    along = jnp.sum(ROW[:, 0, :], axis=0)[:, None]
     out_width = out_grad.shape[1]
     mine = lax.dynamic_slice_in_dim(tokens, p * out_width, out_width, 1).astype(F32)
     inv = INV[:, 0:1]
     layer_out = mine + columns(LO)
     tokens_grad = out_grad.astype(F32) + inv * (columns(DN) - mine * inv * (along / D))
-    trust = jnp.sqrt(totals[0]) / jnp.sqrt(totals[1])
-    new_weights, new_averages = [], []
-    for i in range(6):
-        w = weights[i]
-        if i < 4:
-            scale = MATRIX_RATE * trust[i].reshape((M,) + (1,) * (w.ndim - 1))
-            new = w - scale * directions[i]
-        else:
-            new = w - (CHANNEL_RATE if i == 4 else GAIN_RATE) * adam_all[i][2]
-        new_weights.append(new)
-        new_averages.append(AVERAGE_KEEP * averages[i] + (1.0 - AVERAGE_KEEP) * new)
+    back = lambda v: from_rows(v, S, w_in.shape)
     return (
-        layer_out,
-        tokens_grad,
-        *new_weights,
-        *[a[0] for a in adam_all],
-        *[a[1] for a in adam_all],
-        *new_averages,
+        layer_out, tokens_grad,
+        back(nw_in), nw_x, nw_dt, nw_out, nw_ch, nw_g[0],
+        back(nm_in), nm_x, nm_dt, nm_out, nm_ch, nm_g[0],
+        back(ns_in), ns_x, ns_dt, ns_out, ns_ch, ns_g[0],
+        back(na_in), na_x, na_dt, na_out, na_ch, na_g[0],
     )
 
 
 def channels_fit(mesh):
     S, PN = mesh.shape["seq"], mesh.shape["tp"]
     n = S * PN
-    return PN == 4 and S % 4 == 0 and (2 * N) % n == 0 and (D * 2 // n) % LANES == 0
+    return PN == 4 and S % 4 == 0 and (2 * N) % n == 0 and D * 2 // n == LANES
 
 
 def solution(mesh):

time: 635 us -> 481 us (0.76)
  other arithmetic: 93.3 us -> 9.23 us
  Pallas kernels: 380 us -> 456 us
  local copies, waits for them, and re-layouts: 82.8 us -> 13.7 us
  starting transfers between devices: 47.8 us -> 0 us
  waiting for transfers between devices: 22.9 us -> 0 us
    pallas_call x7 -> x8, Pallas kernels: 380 us -> 456 us  [the longest x1 379 us: block_call(): pl.pallas_call(functools.partial(block_kernel, S, PN), out_shape=out, in_...]
    reduce_sum x7 -> x1, other arithmetic: 55 us -> 0.95 us  [local(): along = jnp.sum(ROW[:, 0, :], axis=0)[:, None]]
    ppermute x21 -> x0, starting transfers between devices: 47.8 us -> none  [the longest x9 34.6 us: row_gather(): lax.ppermute(block, 'seq', [(i, (i + 2 * k) % S) for i in range(S)])]
    unnamed x111 -> x36, local copies, waits for them, and re-layouts: 40.4 us -> 7.19 us
    ppermute x21 -> x0, waiting for transfers between devices: 22.9 us -> none  [the longest x12 16.7 us: row_gather(): out += [blk, lax.ppermute(blk, 'seq', across)]]
    add x6 -> x2, other arithmetic: 23.6 us -> 0.98 us  [the longest x1 0.84 us: local(): na_dt = AVERAGE_KEEP * average_dt + (1.0 - AVERAGE_KEEP) * nw_dt]
    another operation x7 -> x1, local copies, waits for them, and re-layouts: 14.6 us -> 0.01 us  [the longest x2 11.8 us: local(): jnp.stack([gin0, gin1]).reshape(2, M, width, inner_width)]
  transfers between devices with their start and end apart: 21 -> 0, of which waited for: 6 -> 0; matrix products, arithmetic and copies ran while one was open for 10% -> 0% of each run, Pallas kernels for 20% -> 0%
where the time goes in v2:
time: 481 us; the launch traced here: 480 us
  Pallas kernels  456 us (95%)
  local copies, waits for them, and re-layouts  13.7 us (3%)
  other arithmetic  9.23 us (2%)
    pallas_call x1, Pallas kernels, block_call(): pl.pallas_call(functools.partial(block_kernel, S, PN), out_shape=out, in_...  379 us
    pallas_call x1, Pallas kernels, adam_in(): pl.pallas_call(adam_in_kernel, out_shape=(sds(w.shape), sds(w.shape), sds...  22.1 us
    pallas_call x2, Pallas kernels, final_rows(): pl.pallas_call(final_rows_kernel, out_shape=(sds(rows(w).shape), sds(rows...  19.5 us
    pallas_call x1, Pallas kernels, adam_out(): pl.pallas_call(adam_out_kernel, out_shape=(sds(w.shape), sds(w.shape), sd...  14.2 us
    pallas_call x1, Pallas kernels, norms_over_all(): remote_call(functools.partial(norms_kernel, S, PN), sds((n,) + tile.shape...  9.73 us

profile of v2, /device:TPU:0, one launch (start us, length us, event | category | flops | bytes accessed | tf_op | source)
XLA Modules:
  0.0 480.3 jit_solution(7859505099137219075)
XLA Ops:
  0.7 0.7 convert_element_type.31
  1.3 0.6 broadcast_in_dim.27.refs_2_
  1.9 1.6 convert_element_type.32.refs_3_
  3.5 1.3 broadcast_in_dim.28.refs_4_
  4.8 7.9 %shard_map.467 = (bf16[8,256,384]{2,1,0:T(8,128)(2,1)}, bf16[8,256,384]{2,1,0:T(8,128)(2,1)}, bf16[8,384,256]{2,1,0:T(8,128)(2,1)}) custom-call(f32[12288,128]{1,0:T(8,128)} %bitcast.77, f32[3,1024,256]{2,1,0:T(8,128)} %w.3), custom_call_target="tpu_custom_call" | custom-call | tf_op jit(solution)/shard_map/pallas_call | solution.py:1266
  12.7 0.1 fusion.7
  12.8 0.1 stack.32
  12.8 1.0 copy.99.refs_8_
  13.8 0.0 copy-done.2
  13.9 0.8 copy.97
  14.6 0.6 copy_bitcast_fusion.refs_11_
  15.2 0.7 convert_bitcast_fusion.refs_12_
  15.9 379.3 %shard_map.468 = (bf16[8,128,256]{2,1,0:T(8,128)(2,1)}, bf16[8,128,256]{2,1,0:T(8,128)(2,1)}, f32[4,8,256]{2,1,0:T(8,128)}, f32[32,8,128]{2,1,0:T(8,128)}, f32[8...) custom-call(bf16[128,2048]{1,0:T(8,128)(2,1)} %refs_0_.1, ...), custom_call_target="tpu_custom_call" | custom-call | tf_op jit(solution)/shard_map/pallas_call | solution.py:1242
  395.1 0.0 copy-start.8
  395.2 0.0 copy-start.9
  395.2 0.0 copy-start.10
  395.2 1.5 convert_reduce_fusion
  396.7 1.0 slice_reduce_fusion.2
  397.7 0.9 slice_reduce_fusion
  398.7 1.8 fusion.3
  400.4 0.9 copy.102.wx
  401.3 0.0 copy-done.8
  401.3 0.9 copy.103.mx
  402.3 0.0 copy-done.9
  402.3 0.9 copy.104.sx
  403.2 0.0 copy-done.10
  403.2 0.9 copy.105.ax
  404.1 22.1 %shard_map.469 = (f32[12288,128]{1,0:T(8,128)}, f32[12288,128]{1,0:T(8,128)}, f32[12288,128]{1,0:T(8,128)}, f32[3,2,8,128]{3,2,1,0:T(8,128)}) custom-call(bf16[1024,256]{1,0:T(8,128)(2,1)} %get-tuple-element.82.NR, f32[1024,8]{1,0:T(8,128)} %get-tuple-element.83.aux, bf16[8,1024,256]{2,1,0:T(8,128)(2,1)} %get-tuple-element.84.dall, f32[12288,128]{1,0:T(8,128)} %bitcast.78, ...), custom_call_target="tpu_custom_call" | custom-call | tf_op jit(solution)/shard_map/pallas_call | solution.py:1349
  426.3 14.2 %shard_map.470 = (f32[3,1024,256]{2,1,0:T(8,128)}, f32[3,1024,256]{2,1,0:T(8,128)}, f32[3,1024,256]{2,1,0:T(8,128)}, f32[3,2,8,256]{3,2,1,0:T(8,128)}) custom-call(bf16[8,1024,128]{2,1,0:T(8,128)(2,1)} %get-tuple-element.86.gall, bf16[1024,256]{1,0:T(8,128)(2,1)} %get-tuple-element.87.G, f32[1024,8]{1,0:T(8,128)} %get-tuple-element.83.aux, ...), custom_call_target="tpu_custom_call" | custom-call | tf_op jit(solution)/shard_map/pallas_call | solution.py:1387
  440.5 3.7 shard_map.471
  444.2 9.7 %shard_map.472 = f32[32,8,128]{2,1,0:T(8,128)} custom-call(f32[8,128]{1,0:T(8,128)} %get-tuple-element.89.tile), custom_call_target="tpu_custom_call" | custom-call | tf_op jit(solution)/shard_map/pallas_call | solution.py:1486
  454.0 1.0 slice_reduce_fusion.1
  454.9 0.1 multiply_multiply_fusion
  455.0 0.6 fusion.10
  455.6 0.1 broadcast_in_dim.33
  455.7 0.6 reshape.159.scale
  456.3 0.0 copy-start.11
  456.3 0.0 copy-start.12
  456.3 12.2 %shard_map.473 = (f32[6,2048,128]{2,1,0:T(8,128)}, f32[6,2048,128]{2,1,0:T(8,128)}) custom-call(f32[6]{0:T(128)} %reshape.159.scale, f32[6,2048,128]{2,1,0:T(8,128)} %bitcast.79, f32[6,2048,128]{2,1,0:T(8,128)} %bitcast.83, f32[6,2048,128]{2,1,0:T(8,128)} %bitcast.82), custom_call_target="tpu_custom_call" | custom-call | tf_op jit(solution)/shard_map/pallas_call | solution.py:1502
  468.4 0.0 copy-done.7
  468.5 0.1 multiply_add_fusion
  468.6 0.9 copy.113
  469.5 0.8 multiply_add_fusion.1
  470.3 7.3 %shard_map.474 = (f32[3,1024,256]{2,1,0:T(8,128)}, f32[3,1024,256]{2,1,0:T(8,128)}) custom-call(f32[3]{0:T(128)} %get-tuple-element.205.scale, f32[3,1024,256]{2,1,0:T(8,128)} %w.3, f32[3,1024,256]{2,1,0:T(8,128)} %get-tuple-element.94.dr, f32[3,1024,256]{2,1,0:T(8,128)} %avg.1), custom_call_target="tpu_custom_call" | custom-call | tf_op jit(solution)/shard_map/pallas_call | solution.py:1502
  477.7 0.0 copy-done.6
  477.7 0.9 copy.114
  478.5 0.9 copy.115
  479.4 0.9 copy.116
  (24 shorter events, 0.1 us)
Async XLA Ops:
  4.8 7.9 %copy-start.13 = (s32[1024]{0:T(1024)S(1)}, s32[1024]{0:T(1024)}, u32[]{:S(2)}) copy-start(s32[1024]{0:T(1024)} %param.31) | copy-start | bytes 12292
  4.8 9.0 %copy-start.2 = (f32[3,128,160]{1,2,0:T(8,128)S(1)}, f32[3,128,160]{1,2,0:T(8,128)}, u32[]{:S(2)}) copy-start(f32[3,128,160]{1,2,0:T(8,128)} %param.33) | copy-start | bytes 737284
  15.9 382.8 %copy-start.4 = (bf16[128,512]{1,0:T(8,128)(2,1)S(1)}, bf16[128,512]{1,0:T(8,128)(2,1)}, u32[]{:S(2)}) copy-start(bf16[128,512]{1,0:T(8,128)(2,1)} %refs_1_.1) | copy-start | bytes 393220
  395.1 6.2 %copy-start.8 = (f32[3,128,160]{1,2,0:T(8,128)S(1)}, f32[3,128,160]{1,2,0:T(8,128)}, u32[]{:S(2)}) copy-start(f32[3,128,160]{1,2,0:T(8,128)} %param.39) | copy-start | bytes 737284
  395.2 7.1 %copy-start.9 = (f32[3,128,160]{1,2,0:T(8,128)S(1)}, f32[3,128,160]{1,2,0:T(8,128)}, u32[]{:S(2)}) copy-start(f32[3,128,160]{1,2,0:T(8,128)} %param.45) | copy-start | bytes 737284
  395.2 8.0 %copy-start.10 = (f32[3,128,160]{1,2,0:T(8,128)S(1)}, f32[3,128,160]{1,2,0:T(8,128)}, u32[]{:S(2)}) copy-start(f32[3,128,160]{1,2,0:T(8,128)} %param.51) | copy-start | bytes 737284
  456.3 12.2 %copy-start = (f32[3,128,160]{2,1,0:T(8,128)S(1)}, f32[3,128,160]{2,1,0:T(8,128)}, u32[]{:S(2)}) copy-start(f32[3,128,160]{2,1,0:T(8,128)} %copy.102.wx) | copy-start | bytes 737284
  456.3 12.2 %copy-start.1 = (f32[3,128,160]{2,1,0:T(8,128)S(1)}, f32[3,128,160]{2,1,0:T(8,128)}, u32[]{:S(2)}) copy-start(f32[3,128,160]{2,1,0:T(8,128)} %copy.105.ax) | copy-start | bytes 737284
  456.3 12.2 %copy-start.7 = (f32[3,128,160]{2,1,0:T(8,128)S(1)}, f32[3,128,160]{2,1,0:T(8,128)}, u32[]{:S(2)}) copy-start(f32[3,128,160]{2,1,0:T(8,128)} %get-tuple-element.92) | copy-start | bytes 737284
  456.3 13.2 %copy-start.3 = (f32[3,16,1024]{2,1,0:T(8,128)S(1)}, f32[3,16,1024]{2,1,0:T(8,128)}, u32[]{:S(2)}) copy-start(f32[3,16,1024]{2,1,0:T(8,128)} %wd.1) | copy-start | bytes 589828
  456.3 13.2 %copy-start.11 = (f32[3,16,1024]{2,1,0:T(8,128)S(1)}, f32[3,16,1024]{2,1,0:T(8,128)}, u32[]{:S(2)}) copy-start(f32[3,16,1024]{2,1,0:T(8,128)} %param.52) | copy-start | bytes 589828
  456.3 13.2 %copy-start.12 = (f32[3,16,1024]{2,1,0:T(8,128)S(1)}, f32[3,16,1024]{2,1,0:T(8,128)}, u32[]{:S(2)}) copy-start(f32[3,16,1024]{2,1,0:T(8,128)} %get-tuple-element.93) | copy-start | bytes 589828
  470.3 7.3 %copy-start.6 = (f32[3,128,160]{2,1,0:T(8,128)S(1)}, f32[3,128,160]{2,1,0:T(8,128)}, u32[]{:S(2)}) copy-start(f32[3,128,160]{2,1,0:T(8,128)} %get-tuple-element.175) | copy-start | bytes 737284
  470.3 8.2 %copy-start.5 = (f32[3,128,160]{2,1,0:T(8,128)S(1)}, f32[3,128,160]{2,1,0:T(8,128)}, u32[]{:S(2)}) copy-start(f32[3,128,160]{2,1,0:T(8,128)} %get-tuple-element.181) | copy-start | bytes 737284

commit v3 on v2

--- a/solution.py
+++ b/solution.py
@@ -371,7 +371,7 @@
 
 
 MESH = pl.DeviceIdType.MESH
-VMEM_LIMIT = 60 * 1024 * 1024
+VMEM_LIMIT = 62 * 1024 * 1024
 LANES = 128
 F32 = jnp.float32
 BF16 = jnp.bfloat16
@@ -523,22 +523,47 @@
     return out
 
 
-def sum_over_all(S, PN, lr, bct, LR, BCT, got_l, got_b, ssl, rsl, ssb, rsb, sgl, rgl, sgb, rgb):
-    n = S * PN
+def sum_over_all(
+    S, PN, lr, bct, LR, BCT, got_l, got_b, core_l, core_b,
+    c1s, c1r, ssl, rsl, ssb, rsb, sgl, rgl, sgb, rgb, c2s, c2r, between=(),
+):
+    n = S * PN // 2
     s, p = lax.axis_index("seq"), lax.axis_index("tp")
-    me = s * PN + p
-    rows = lr.shape[0] // n
-    per = n // bct.shape[0]
+    y, c = lax.div(p, 2), lax.rem(p, 2)
+    me = s * (PN // 2) + y
+    T = lr.shape[0]
+    half, rows = T // 2, T // 2 // n
+    chunks = bct.shape[0]
+    per = n // (chunks // 2)
     high = bct.shape[1] // per
+    twin = {"tp": p + 1 - 2 * c}
 
     def device(j):
-        return {"seq": lax.div(j, PN), "tp": lax.rem(j, PN)}
+        return {"seq": lax.div(j, PN // 2), "tp": 2 * lax.rem(j, PN // 2) + c}
+
+    def half_l(k):
+        return pl.ds(pl.multiple_of(k * half, half), half)
+
+    def half_b(k):
+        return pl.ds(k * (chunks // 2), chunks // 2)
 
     def rows_of(j):
-        return pl.ds(pl.multiple_of(j * rows, 16), rows)
+        return pl.ds(pl.multiple_of(c * half + j * rows, rows), rows)
 
     def slab(ref, j):
-        return ref.at[lax.div(j, per), pl.ds(pl.multiple_of(lax.rem(j, per) * high, 8), high)]
+        at = c * (chunks // 2) + lax.div(j, per)
+        return ref.at[at, pl.ds(pl.multiple_of(lax.rem(j, per) * high, 8), high)]
+
+    swap = [
+        seq_copy(lr.at[half_l(1 - c)], core_l, c1s.at[0], c1r.at[0], twin),
+        seq_copy(bct.at[half_b(1 - c)], core_b, c1s.at[1], c1r.at[1], twin),
+    ]
+    for cp in swap:
+        cp.start()
+    for cp in swap:
+        cp.wait()
+    lr[half_l(c), :] = lr[half_l(c), :] + core_l[...]
+    bct[half_b(c)] = bct[half_b(c)] + core_b[...]
 
     def first(k):
         j = lax.rem(me + k, n)
@@ -566,20 +591,37 @@
         return 0
 
     lax.fori_loop(1, n, lambda k, _: start(first, k), 0)
+    for cp in between[0:1]:
+        cp()
     got_l[0] = lr[rows_of(me), :]
     got_b[0] = slab(bct, me)[...]
     lax.fori_loop(1, n, lambda k, _: wait(first, k), 0)
     LR[rows_of(me), :] = jnp.sum(got_l[...], axis=0).astype(LR.dtype)
     slab(BCT, me)[...] = jnp.sum(got_b[...], axis=0)
     lax.fori_loop(1, n, lambda k, _: start(second, k), 0)
+    for cp in between[1:2]:
+        cp()
     lax.fori_loop(1, n, lambda k, _: wait(second, k), 0)
+    swap = [
+        seq_copy(LR.at[half_l(c)], LR.at[half_l(c)], c2s.at[0], c2r.at[0], twin),
+        seq_copy(BCT.at[half_b(c)], BCT.at[half_b(c)], c2s.at[1], c2r.at[1], twin),
+    ]
+    for cp in swap:
+        cp.start()
+    for cp in swap:
+        cp.wait()
 
 
 def sum_scratch(S, PN, T):
-    n = S * PN
+    n = S * PN // 2
     dma = pltpu.SemaphoreType.DMA
-    slabs = (T // LANES) * 2 * N // n
-    return [pltpu.VMEM((n, T // n, R), F32), pltpu.VMEM((n, slabs, LANES), F32)] + [dma((n,))] * 8
+    chunks = T // LANES
+    slabs = chunks * N // n
+    return (
+        [pltpu.VMEM((n, T // 2 // n, R), F32), pltpu.VMEM((n, slabs, LANES), F32)]
+        + [pltpu.VMEM((T // 2, R), F32), pltpu.VMEM((chunks // 2, 2 * N, LANES), F32)]
+        + [dma((2,))] * 2 + [dma((n,))] * 8 + [dma((2,))] * 2
+    )
 
 
 class RowGather:
@@ -600,16 +642,25 @@
             for k in range(zn)
         ]
 
-    def start(self):
-        self.local.start()
-        for cp in self.z:
-            cp.start()
-        self.x[0].start()
-
-    def forward(self):
-        for k in range(1, self.zn):
+    def start(self, *which):
+        for k in which:
+            if k == 0:
+                self.local.start()
+                self.x[0].start()
+            elif k < self.zn:
+                self.z[k - 1].start()
+
+    def start_from(self, first):
+        self.start(*range(first, self.zn))
+
+    def forward(self, k):
+        if k < self.zn:
             self.z[k - 1].wait_recv()
             self.x[k].start()
+
+    def forward_from(self, first):
+        for k in range(first, self.zn):
+            self.forward(k)
 
     def finish(self):
         self.local.wait()
@@ -624,6 +675,13 @@
         return [dma((S // 2,))] * 4 + [dma]
 
 
+def adam_terms(g, m, s):
+    new_m = BETA_ONE * m + (1.0 - BETA_ONE) * g
+    new_s = BETA_TWO * s + (1.0 - BETA_TWO) * (g * g)
+    root = jnp.sqrt(new_s * (1.0 / (1.0 - BETA_TWO**STEP))) + ADAM_EPSILON
+    return new_m, new_s, (new_m * (1.0 / (1.0 - BETA_ONE**STEP))) / root
+
+
 def softplus(v):
     u = jnp.exp(-jnp.abs(v))
     w = 1.0 + u
@@ -641,20 +699,24 @@
 def block_kernel(S, PN, *refs):
     rest = list(refs)
     take = lambda k: [rest.pop(0) for _ in range(k)]
-    tok, og, modrow, wdt_mine, gain_mine, wi, wg, wo, segs, ch, wlr, wbc, wxT = take(13)
-    LO, DN, GG, ROW, MORE, gx, gtap, gch, NR, G, AUXC, dall_out, gall_out, INV = take(14)
+    tok, og, modrow, gain, segs, ch, w_x, m_x, s_x, w_dt, m_dt, s_dt = take(12)
+    w_in, m_in, s_in, w_out, m_out, s_out = take(6)
+    LO, DN, GG, ROW, MORE, gx, gtap, gch, INV, SCALE, g_in, g_out = take(12)
     tile, toks, ogs, nrm, Wi, Wg, Wo, AUX, GAIN, WD = take(10)
     step, drive, keep, Y, pad, act3, lr, bcp = take(8)
     act, conv, inner, low, bct, pre, H, gated, dgate, dmix, aux, X = take(12)
     gall, dall, DS, DB, dst3, low3, dst, dlow, dbct, dact, gdt = take(11)
-    LR2, BCT2, tail, dpar, dinner, part, rowdot, ggs = take(8)
+    LR2, BCT2, tail, dpar, dinner, part, rowdot, ggs, wdt = take(9)
+    wi, wg, wo, wdt_mine, gain_mine, wlr, wbc, wxT, NR, G = take(10)
+    gdt_mine, turned, sums_ref, TILE, total_tile = take(5)
+    stage, load, store, pair, swaps = take(5)
     ag1, ag2 = take(9), take(9)
     ws = take(12)
     ls = take(1)[0]
-    sums = take(10)
+    sums = take(16)
     rows_g, rows_d, rows_i = take(5), take(5), take(5)
     mx, mr, ml = take(3)
-    last = take(8)
+    last = take(10)
     s, p, z, x = place(S, PN)
     TL, DD = tok.shape
     T = S * TL
@@ -663,12 +725,16 @@
     C = act.shape[1]
     rows = 128
 
+    load_in = pltpu.make_async_copy(w_in, H.at[0 : w_in.shape[0]], stage.at[0])
+    load_in.start()
     wide = tok[...].astype(F32)
     inv = lax.rsqrt(jnp.mean(wide * wide, axis=1, keepdims=True) + EPSILON)
     row = jnp.transpose(jnp.broadcast_to(inv, (TL, LANES)))[0:8]
     tile[...] = jnp.where(
         lax.broadcasted_iota(jnp.int32, row.shape, 0) == 0, modrow[...], row
     )
+    gain_mine[...] = jnp.broadcast_to(gain[...], gain_mine.shape)
+    wdt_mine[...] = w_dt[...].astype(BF16)
     greet_all(S, PN)
     chans = lambda d: pl.ds(pl.multiple_of(d * C, LANES), C)
     block = lambda d: pl.ds(pl.multiple_of(d * width, width), width)
@@ -687,18 +753,45 @@
     for cp in small:
         cp.start()
     tokens.start()
-    for cp in inners:
+    load_in.wait()
+    stride = 2 * S
+    for m in range(M):
+        for b in range(S):
+            r = pl.ds(m * width * stride + 2 * b, width, stride=stride)
+            wi[b, :, m * C : (m + 1) * C] = H[r, :].astype(BF16)
+    for cp in inners + dts:
         cp.start()
+    for m in range(M):
+        for b in range(S):
+            r = pl.ds(m * width * stride + 2 * b + 1, width, stride=stride)
+            wg[b, :, m * C : (m + 1) * C] = H[r, :].astype(BF16)
+    load_out = pltpu.make_async_copy(w_out, H.at[0 : w_out.shape[0]], stage.at[1])
+    load_out.start()
     own = [
         pltpu.make_async_copy(tile, AUX.at[s], ls.at[0]),
         pltpu.make_async_copy(gain_mine, GAIN.at[s], ls.at[1]),
         pltpu.make_async_copy(wdt_mine.at[:, :, chans(s)], WD.at[s], ls.at[2]),
         pltpu.make_async_copy(wi.at[s], Wi.at[block(s)], ls.at[3]),
         pltpu.make_async_copy(wg.at[s], Wg.at[block(s)], ls.at[4]),
-        pltpu.make_async_copy(wo.at[s], Wo.at[s], ls.at[5]),
     ]
     for cp in own:
         cp.start()
+    for m in range(M):
+        wlr[m * C : (m + 1) * C, :] = jnp.transpose(w_x[m, 0:R, :]).astype(BF16)
+        wbc[:, m * C : (m + 1) * C] = w_x[m, R : R + 2 * N, :].astype(BF16)
+        wxT[m] = w_x[m].astype(BF16)
+    load_out.wait()
+    tiles = width // LANES
+    for m in range(M):
+        for b in range(S):
+            rows_b = H[(m * S + b) * C * tiles : (m * S + b + 1) * C * tiles, :]
+            pieces = rows_b.reshape(C // 8, tiles, 8, LANES)
+            for t in range(tiles):
+                wo[b, m * C : (m + 1) * C, t * LANES : (t + 1) * LANES] = (
+                    pieces[:, t].reshape(C, LANES).astype(BF16)
+                )
+    own.append(pltpu.make_async_copy(wo.at[s], Wo.at[s], ls.at[5]))
+    own[-1].start()
     for cp in own:
         cp.wait()
     tokens.forward()
@@ -733,7 +826,7 @@
     lax.fori_loop(0, S, norm, 0)
     for cp in inners:
         cp.wait()
-    for cp in gates + dts:
+    for cp in gates[0:1]:
         cp.start()
 
     big = 256
@@ -766,12 +859,25 @@
         return 0
 
     lax.fori_loop(0, T // rows, convolve, 0)
-    sum_over_all(S, PN, lr, bcp, low, bct, *sums)
+    def start_all(copies):
+        for cp in copies:
+            cp.start()
+
+    sum_over_all(
+        S, PN, lr, bcp, low, bct, *sums,
+        between=(lambda: start_all(gates[1:3]), lambda: start_all(gates[3:5])),
+    )
+    start_all(gates[5:])
     for cp in dts:
         cp.wait()
     cotangent.start()
     for cp in outs:
         cp.start()
+
+    for m in range(M):
+        for t in range(S):
+            h = R // S
+            wdt[m * R + t * h : m * R + (t + 1) * h, :] = WD[t, m]
 
     def prepare(i, _):
         r = pl.ds(pl.multiple_of(i * rows, rows), rows)
@@ -781,9 +887,8 @@
             mask = aux[r, m : m + 1]
             masked = (low_wide * mask).astype(BF16)
             bias = bias + mask * ch[K + 2 + m : K + 3 + m, :]
-            for t in range(S):
-                h = R // S
-                bias = bias + dot(masked[:, t * h : (t + 1) * h], WD[t, m])
+            low3[r, m * R : (m + 1) * R] = masked
+        bias = bias + dot(low3[r, :], wdt[...])
         pre[r, :] = bias
         st = softplus(bias)
         step[r, :] = st
@@ -830,13 +935,13 @@
         return 0
 
     lax.fori_loop(0, T // rows, finish, 0)
+    half = lambda t, k: pl.ds(pl.multiple_of((2 * t + k) * C, LANES), C)
     gathers = [
-        RowGather(S, gated, lambda t: gall.at[t], *rows_g),
-        RowGather(S, dgate, lambda t: dall.at[t, :, C : 2 * C], *rows_d),
-        RowGather(S, dinner, lambda t: dall.at[t, :, 0:C], *rows_i),
+        RowGather(S, gated, lambda t: gall.at[:, chans(t)], *rows_g),
+        RowGather(S, dgate, lambda t: dall.at[:, half(t, 1)], *rows_d),
+        RowGather(S, dinner, lambda t: dall.at[:, half(t, 0)], *rows_i),
     ]
-    gathers[0].start()
-    gathers[1].start()
+    gathers[0].start(0, 1, 2)
     mine = pl.ds(pl.multiple_of(lax.rem(s, per) * width, width), width)
     NR[...] = nrm[:, pl.ds(pl.multiple_of(s * width, width), width)]
 
@@ -851,80 +956,113 @@
     lax.fori_loop(0, S, own_features, 0)
     INV[...] = jnp.broadcast_to(inv, INV.shape)
     scan_backward(
-        pre, H, dmix, act, bct, aux, ch, WD, low,
+        pre, H, dmix, act, bct, aux, ch, wdt, low,
         dlow, dbct, gdt, gch, dact, step, drive, keep, DS, DB, dst3, low3, dst,
-        [(T // LANES // 2, gathers[0].forward)],
-    )
-    gathers[1].forward()
+        [],
+    )
     h = R // S
     part_dt = lambda d: gdt.at[:, pl.ds(pl.multiple_of(d * h, 8), h), :]
     more = row_copies(S, part_dt, lambda t: MORE.at[t], mx, mr)
     more_own = pltpu.make_async_copy(part_dt(s), MORE.at[s], ml)
     for cp in more + [more_own]:
         cp.start()
-    sum_over_all(S, PN, dlow, dbct, LR2, BCT2, *sums)
+    sum_over_all(
+        S, PN, dlow, dbct, LR2, BCT2, *sums,
+        between=(lambda: gathers[0].start_from(3), lambda: gathers[1].start(0, 1)),
+    )
+    gathers[1].start(2)
+    gathers[0].forward(1)
+    gathers[0].forward(2)
     convolve_backward(
         LR2, BCT2, act, conv, aux, ch, wxT, dact, dinner, gx, gtap, pad, tail, act3, dpar
     )
-    gathers[2].start()
+    gathers[1].start_from(3)
+    gathers[2].start_from(0)
     for cp in more + [more_own]:
         cp.wait()
+    gathers[0].forward_from(3)
+    gathers[1].forward(1)
     gathers[0].finish()
-    out_gall = pltpu.make_async_copy(gall, gall_out, ls.at[0])
-    out_gall.start()
+
+    large = 512
 
     def layer(i, _):
-        r = pl.ds(pl.multiple_of(i * big, big), big)
-
-        def add(b, total):
-            wide = gall[b, r, :].astype(F32)
-            for m in range(M):
-                total = total + dot(
-                    (wide * aux[r, m : m + 1]).astype(BF16), wo[b, m * C : (m + 1) * C, :]
-                )
-            return total
-
-        total = lax.fori_loop(0, S, add, jnp.zeros((big, width), F32))
+        r = pl.ds(pl.multiple_of(i * large, large), large)
+
+        total = jnp.zeros((large, width), F32)
+        for m in range(M):
+            w = jnp.concatenate([wo[b, m * C : (m + 1) * C, :] for b in range(S)], axis=0)
+            total = total + dot(gall[r, :], w) * aux[r, m : m + 1]
         part[0, r, :] = total.astype(BF16)
         return 0
 
-    lax.fori_loop(0, T // big, layer, 0)
-    to_out = LastBlocks(S, PN, part.at[0], LO, last[0], last[1], ls.at[1])
+    lax.fori_loop(0, T // large, layer, 0)
+    stream = Stream(H, load, (w_out, m_out, s_out), 6, sums_ref.at[1])
+    stream.start(0)
+
+    def out_gradient(i, rows_of):
+        m, k = i // 2, i % 2
+        wide = gall[:, k * (S // 2) * C : (k + 1) * (S // 2) * C].astype(F32)
+        turned[...] = jnp.transpose((wide * aux[0:T, m : m + 1]).astype(BF16))
+        g = dot(turned[...], G[...])
+        parts = [
+            g[:, t * LANES : (t + 1) * LANES].reshape(-1, 8, LANES) for t in range(tiles)
+        ]
+        H[rows_of, :] = jnp.stack(parts, axis=1).reshape(-1, LANES)
+
+    to_out = LastBlocks(
+        S, PN, part.at[0], LO, pair.at[0], pair.at[1], last[0], last[1], swaps.at[0], ls.at[1]
+    )
     to_out.start()
-    gathers[2].forward()
+    gathers[1].forward(2)
+    stores = [None, None]
+    for i in range(6):
+        k = i % 2
+        if stores[k] is not None:
+            stores[k].wait()
+        rows_of = pl.ds((6 + k) * 1024, 1024)
+        out_gradient(i, rows_of)
+        stores[k] = pltpu.make_async_copy(
+            H.at[rows_of], g_out.at[i * 1024 : (i + 1) * 1024], store.at[k]
+        )
+        stores[k].start()
+        stream.norms(i, i // 2, (6 + k) * 1024)
+        if i == 1:
+            gathers[1].forward_from(3)
+        elif i == 3:
+            gathers[2].forward(1)
+        elif i == 4:
+            gathers[2].forward(2)
+    gathers[2].forward_from(3)
+    for cp in stores:
+        cp.wait()
+    stream = Stream(H, load, (w_in, m_in, s_in), 12, sums_ref.at[0])
+    stream.start(0)
     gathers[1].finish()
     gathers[2].finish()
-    out_dall = pltpu.make_async_copy(dall, dall_out, ls.at[2])
-    out_dall.start()
 
     def normed_back(i, total):
-        r = pl.ds(pl.multiple_of(i * big, big), big)
-
-        def add(b, accs):
-            d0, d1 = dall[b, r, 0:C], dall[b, r, C : 2 * C]
-            return tuple(
-                accs[m]
-                + dot(d0, wi[b, :, m * C : (m + 1) * C], NT)
-                + dot(d1, wg[b, :, m * C : (m + 1) * C], NT)
-                for m in range(M)
-            )
-
-        accs = lax.fori_loop(0, S, add, (jnp.zeros((big, width), F32),) * M)
-        d = accs[0] * aux[r, 0:1]
-        for m in range(1, M):
-            d = d + accs[m] * aux[r, m : m + 1]
+        r = pl.ds(pl.multiple_of(i * large, large), large)
+
+        d = jnp.zeros((large, width), F32)
+        for m in range(M):
+            cols = slice(m * C, (m + 1) * C)
+            w = jnp.concatenate([v[b, :, cols] for b in range(S) for v in (wi, wg)], axis=1)
+            d = d + dot(dall[r, :], w, NT) * aux[r, m : m + 1]
         scaled = X[r, :].astype(F32) * aux[r, 7:8]
         gained = d * gain_mine[0:1, :]
         part[1, r, :] = gained.astype(BF16)
         along = jnp.sum(gained * scaled, axis=1, keepdims=True)
-        for j in range(big // TL):
+        for j in range(large // TL):
             turned = jnp.transpose(jnp.broadcast_to(along[j * TL : (j + 1) * TL], (TL, LANES)))
-            rowdot[i * (big // TL) + j] = turned[0:8]
+            rowdot[i * (large // TL) + j] = turned[0:8]
         return total + jnp.sum(d * scaled, axis=0, keepdims=True)
 
-    total = lax.fori_loop(0, T // big, normed_back, jnp.zeros((1, width), F32))
+    total = lax.fori_loop(0, T // large, normed_back, jnp.zeros((1, width), F32))
     ggs[...] = jnp.broadcast_to(total, ggs.shape)
-    to_in = LastBlocks(S, PN, part.at[1], DN, last[2], last[3], ls.at[3])
+    to_in = LastBlocks(
+        S, PN, part.at[1], DN, pair.at[2], pair.at[3], last[2], last[3], swaps.at[1], ls.at[3]
+    )
     to_in.start()
     gains = [
         seq_copy(ggs, GG.at[k], last[4].at[k], last[5].at[k], {"tp": lax.rem(p + k, PN)})
@@ -935,63 +1073,171 @@
     n = S * PN
     me = s * PN + p
 
-    def tile_copy(k):
-        j = lax.rem(me + k, n)
-        device = {"seq": lax.div(j, PN), "tp": lax.rem(j, PN)}
-        return seq_copy(
-            rowdot.at[lax.div(j, PN)], ROW.at[k], last[6].at[k], last[7].at[k], device
+    def to_all(src, dst, send, recv):
+        def copy(k):
+            j = lax.rem(me + k, n)
+            device = {"seq": lax.div(j, PN), "tp": lax.rem(j, PN)}
+            return seq_copy(src(lax.div(j, PN)), dst.at[k], send.at[k], recv.at[k], device)
+
+        def start(k, _):
+            copy(k).start()
+            return 0
+
+        def wait(k, _):
+            copy(k).wait()
+            return 0
+
+        return (
+            lambda: lax.fori_loop(1, n, start, 0),
+            lambda: lax.fori_loop(1, n, wait, 0),
         )
 
-    def send_tile(k, _):
-        tile_copy(k).start()
-        return 0
-
-    def wait_tile(k, _):
-        tile_copy(k).wait()
-        return 0
-
-    lax.fori_loop(1, n, send_tile, 0)
+    send_row, wait_row = to_all(lambda t: rowdot.at[t], ROW, last[6], last[7])
+    send_row()
     GG[0] = ggs[...]
     ROW[0] = rowdot[s]
-    AUXC[...] = aux[0:T, :]
+
+    stores = [None, None]
+    per_m = width * stride
+    for m in range(M):
+        k = m % 2
+        if stores[k] is not None:
+            stores[k].wait()
+        first_row = 6 * 1024 + k * per_m
+        turned[0:width, :] = jnp.transpose(
+            (NR[...].astype(F32) * aux[0:T, m : m + 1]).astype(BF16)
+        )
+        for b in range(S):
+            g = dot(turned[0:width, :], dall[:, 2 * b * C : 2 * (b + 1) * C])
+            H[pl.ds(first_row + 2 * b, width, stride=stride), :] = g[:, 0:C]
+            H[pl.ds(first_row + 2 * b + 1, width, stride=stride), :] = g[:, C : 2 * C]
+        stores[k] = pltpu.make_async_copy(
+            H.at[first_row : first_row + per_m], g_in.at[m * per_m : (m + 1) * per_m], store.at[k]
+        )
+        stores[k].start()
+        for q in range(per_m // 1024):
+            stream.norms(m * (per_m // 1024) + q, m, first_row + q * 1024)
+    lane = lax.broadcasted_iota(jnp.int32, (8, LANES), 1)
+    total = jnp.zeros((8, LANES), F32)
+    square = lambda v: jnp.sum(v * v)
+    for t in range(S):
+        gdt_mine[:, :, t * C : (t + 1) * C] = MORE[t]
+    for m in range(M):
+        x = adam_terms(gx[m], m_x[m], s_x[m])[2] + WEIGHT_DECAY * w_x[m]
+        d = adam_terms(gdt_mine[m], m_dt[m], s_dt[m])[2] + WEIGHT_DECAY * w_dt[m]
+        for k, value in enumerate((
+            jnp.sum(sums_ref[0, m, 0]), square(w_x[m]), square(w_dt[m]), jnp.sum(sums_ref[1, m, 0]),
+            jnp.sum(sums_ref[0, m, 1]), square(x), square(d), jnp.sum(sums_ref[1, m, 1]),
+        )):
+            total = jnp.where(lane == k * M + m, value, total)
+    total_tile[...] = total
+    send_tile, wait_tile = to_all(lambda t: total_tile, TILE, last[8], last[9])
+    send_tile()
+    TILE[0] = total
     for cp in gains:
         cp.wait()
-    lax.fori_loop(1, n, wait_tile, 0)
+    wait_row()
+    wait_tile()
+    total = jnp.sum(TILE[...], axis=0)
+    below = pltpu.roll(total, LANES - 4 * M, 1)
+    SCALE[...] = MATRIX_RATE * (jnp.sqrt(total) / jnp.sqrt(below))
+    for cp in stores:
+        cp.wait()
     to_out.finish()
     to_in.finish()
-    out_gall.wait()
-    out_dall.wait()
+
+
+class Stream:
+    def __init__(self, H, sems, refs, steps, sums):
+        self.H, self.sems, self.refs, self.steps, self.sums = H, sems, refs, steps, sums
+        sums[...] = jnp.zeros(sums.shape, F32)
+
+    def copies(self, i):
+        k = i % 2
+        return [
+            pltpu.make_async_copy(
+                ref.at[i * 1024 : (i + 1) * 1024],
+                self.H.at[pl.ds((3 * k + a) * 1024, 1024)],
+                self.sems.at[k, a],
+            )
+            for a, ref in enumerate(self.refs)
+        ]
+
+    def start(self, i):
+        for cp in self.copies(i):
+            cp.start()
+
+    def norms(self, i, m, g_row):
+        for cp in self.copies(i):
+            cp.wait()
+        if i + 1 < self.steps:
+            self.start(i + 1)
+        H, k, rows = self.H, i % 2, 128
+
+        def body(t, sums):
+            at = lambda first: pl.ds(pl.multiple_of(first + t * rows, rows), rows)
+            weight = H[at(3 * k * 1024), :]
+            ratio = adam_terms(
+                H[at(g_row), :], H[at((3 * k + 1) * 1024), :], H[at((3 * k + 2) * 1024), :]
+            )[2]
+            direction = ratio + WEIGHT_DECAY * weight
+            fold = lambda v: jnp.sum((v * v).reshape(rows // 8, 8, LANES), axis=0)
+            return sums[0] + fold(weight), sums[1] + fold(direction)
+
+        a, b = lax.fori_loop(0, 1024 // rows, body, (self.sums[m, 0], self.sums[m, 1]))
+        self.sums[m, 0] = a
+        self.sums[m, 1] = b
 
 
 class LastBlocks:
-    def __init__(self, S, PN, part, out, send, recv, ls):
+    def __init__(self, S, PN, part, out, other, both, send, recv, swap, ls):
         s, p = lax.axis_index("seq"), lax.axis_index("tp")
         ratio = S // PN
         self.S, self.PN, self.ratio = S, PN, ratio
         self.s, self.p, self.home = s, p, lax.div(s, ratio)
-        self.slot = lax.rem(s, ratio) * PN + p
-        self.part, self.out, self.send, self.recv, self.ls = part, out, send, recv, ls
+        self.y, self.c = lax.div(p, 2), lax.rem(p, 2)
+        self.slot = lax.rem(s, ratio) * (PN // 2) + self.y
+        self.part, self.out, self.other, self.both = part, out, other, both
+        self.send, self.recv, self.ls = send, recv, ls
+        self.half = part.shape[0] // 2
         self.TL = part.shape[0] // S
+        self.swap = seq_copy(
+            part.at[self.rows(1 - self.c)],
+            other,
+            swap.at[0],
+            swap.at[1],
+            {"tp": p + 1 - 2 * self.c},
+        )
+
+    def rows(self, c):
+        return pl.ds(pl.multiple_of(c * self.half, self.half), self.half)
+
+    def seq(self, k):
+        return self.c * (self.S // 2) + k
 
     def away(self, k):
-        return jnp.logical_or(self.s != k, self.home != self.p)
+        return jnp.logical_or(self.s != self.seq(k), self.home != self.p)
 
     def copy(self, k):
         return seq_copy(
-            self.part.at[pl.ds(k * self.TL, self.TL)],
+            self.both.at[k * self.TL : (k + 1) * self.TL],
             self.out.at[self.slot],
             self.send.at[k],
             self.recv.at[self.slot],
-            {"seq": k, "tp": self.home},
+            {"seq": self.seq(k), "tp": self.home},
         )
 
     def own(self, k):
         return pltpu.make_async_copy(
-            self.part.at[pl.ds(k * self.TL, self.TL)], self.out.at[self.slot], self.ls
+            self.both.at[k * self.TL : (k + 1) * self.TL], self.out.at[self.slot], self.ls
         )
 
     def start(self):
-        for k in range(self.S):
+        self.swap.start()
+        self.swap.wait()
+        mine = self.part[self.rows(self.c), :].astype(F32)
+        self.both[...] = (mine + self.other[...].astype(F32)).astype(BF16)
+        for k in range(self.S // 2):
 
             @pl.when(self.away(k))
             def _():
@@ -1002,7 +1248,7 @@
                 self.own(k).start()
 
     def finish(self):
-        for k in range(self.S):
+        for k in range(self.S // 2):
 
             @pl.when(self.away(k))
             def _():
@@ -1012,15 +1258,16 @@
             def _():
                 self.own(k).wait()
 
+        core = lax.div(self.s, self.S // 2)
         for h in range(self.ratio):
-            for q in range(self.PN):
-                t = self.ratio * self.p + h
-                i = h * self.PN + q
+            for y in range(self.PN // 2):
+                t, q = self.ratio * self.p + h, 2 * y + core
+                i = h * (self.PN // 2) + y
 
                 @pl.when(jnp.logical_or(t != self.s, self.p != q))
                 def _():
                     seq_copy(
-                        self.part.at[0 : self.TL],
+                        self.both.at[0 : self.TL],
                         self.out.at[i],
                         self.send.at[0],
                         self.recv.at[i],
@@ -1030,32 +1277,37 @@
 
 def scan_forward(T, C, bct, ch, step, drive, keep, H, Y):
     base = -jnp.exp(ch[K + 2 + M : K + 2 + M + N, :])
-    H[0] = jnp.zeros((N, C), F32)
+    H[0:N, :] = jnp.zeros((N, C), F32)
 
     def chunk(c, h):
-        bc = bct[c]
-
-        def eight(i, h):
-            cols = pltpu.roll(bc, lax.rem(LANES - 8 * i, LANES), 1)
-            t0 = pl.multiple_of(c * LANES + i * 8, 8)
+        cols = bct[c]
+        for i in range(LANES // 8):
+            t0 = pl.multiple_of(c * LANES + 8 * i, 8)
             r = pl.ds(t0, 8)
             st, dr, kp = step[r, :], drive[r, :], keep[r, :]
             ys = []
             for j in range(8):
+                k = 8 * i + j
                 rate = jnp.exp(st[j : j + 1] * base) * kp[j : j + 1]
-                h = rate * h + dr[j : j + 1] * cols[0:N, j : j + 1]
-                H[t0 + j + 1] = h
-                ys.append(jnp.sum(cols[N : 2 * N, j : j + 1] * h, axis=0, keepdims=True))
+                h = rate * h + dr[j : j + 1] * cols[0:N, k : k + 1]
+                H[pl.ds(pl.multiple_of((t0 + j + 1) * N, N), N), :] = h
+                ys.append(jnp.sum(cols[N : 2 * N, k : k + 1] * h, axis=0, keepdims=True))
             Y[r, :] = jnp.concatenate(ys, axis=0)
-            return h
-
-        return lax.fori_loop(0, LANES // 8, eight, h)
+        return h
 
     lax.fori_loop(0, T // LANES, chunk, jnp.zeros((N, C), F32))
 
 
+def lane_sums(values):
+    v = jnp.concatenate(values, axis=0)
+    high = v.astype(BF16)
+    low = (v - high.astype(F32)).astype(BF16)
+    sums = dot(jnp.concatenate([high, low], axis=1), jnp.ones((2 * v.shape[1], LANES), BF16))
+    return [sums[k * N : (k + 1) * N] for k in range(len(values))]
+
+
 def scan_backward(
-    pre, H, dmix, act, bct, aux, ch, WD, low,
+    pre, H, dmix, act, bct, aux, ch, wdt, low,
     dlow, dbct, gdt, gch, dact, step, drive, keep, DS, DB, dst3, low3, dst, hooks,
 ):
     T, C = act.shape
@@ -1068,47 +1320,39 @@
 
     def chunk(cc, carry):
         c = chunks - 1 - cc
-        bc = bct[c]
-
-        def eight(ii, carry):
-            flow, hcur, gacc, accb, accc = carry
-            i = LANES // 8 - 1 - ii
-            cols = pltpu.roll(bc, lax.rem(LANES - 8 * i, LANES), 1)
-            t0 = pl.multiple_of(c * LANES + i * 8, 8)
+        cols = bct[c]
+        flow, hcur, gacc = carry
+        accb = accc = jnp.zeros((N, LANES), F32)
+        for i in reversed(range(LANES // 8)):
+            t0 = pl.multiple_of(c * LANES + 8 * i, 8)
             r = pl.ds(t0, 8)
             st, dr, kp, dm = step[r, :], drive[r, :], keep[r, :], dmix[r, :]
-            ds, db = [None] * 8, [None] * 8
+            ds, db, ub, uc = [None] * 8, [None] * 8, [None] * 8, [None] * 8
             for j in reversed(range(8)):
-                bcol, ccol = cols[0:N, j : j + 1], cols[N : 2 * N, j : j + 1]
-                back = ccol * dm[j : j + 1] + flow
+                k = 8 * i + j
+                back = cols[N : 2 * N, k : k + 1] * dm[j : j + 1] + flow
                 rate = jnp.exp(st[j : j + 1] * base) * kp[j : j + 1]
-                hprev = H[t0 + j]
-                here = lane == 8 * i + j
-                accc = jnp.where(
-                    here, jnp.sum(dm[j : j + 1] * hcur, axis=1, keepdims=True), accc
-                )
-                accb = jnp.where(
-                    here, jnp.sum(back * dr[j : j + 1], axis=1, keepdims=True), accb
-                )
+                hprev = H[pl.ds(pl.multiple_of((t0 + j) * N, N), N), :]
+                uc[j] = dm[j : j + 1] * hcur
+                ub[j] = back * dr[j : j + 1]
                 flow = rate * back
                 dlog = flow * hprev
                 gacc = gacc + dlog * st[j : j + 1]
                 ds[j] = jnp.sum(dlog * base, axis=0, keepdims=True)
-                db[j] = jnp.sum(back * bcol, axis=0, keepdims=True)
+                db[j] = jnp.sum(back * cols[0:N, k : k + 1], axis=0, keepdims=True)
                 hcur = hprev
             DS[r, :] = jnp.concatenate(ds, axis=0)
             DB[r, :] = jnp.concatenate(db, axis=0)
-            return flow, hcur, gacc, accb, accc
-
-        blank = jnp.zeros((N, LANES), F32)
-        flow, hcur, gacc, accb, accc = lax.fori_loop(
-            0, LANES // 8, eight, carry + (blank, blank)
-        )
+            sb, sc = lane_sums(ub), lane_sums(uc)
+            for j in range(8):
+                here = lane == 8 * i + j
+                accb = jnp.where(here, sb[j], accb)
+                accc = jnp.where(here, sc[j], accc)
         dbct[c, 0:N, :] = accb
         dbct[c, N : 2 * N, :] = accc
         return flow, hcur, gacc
 
-    carry, done = (nothing, H[T], nothing), 0
+    carry, done = (nothing, H[T * N : (T + 1) * N, :], nothing), 0
     for upto, call in hooks + [(chunks, None)]:
         carry = lax.fori_loop(done, upto, chunk, carry)
         done = upto
@@ -1125,20 +1369,16 @@
         d = (grad / (1.0 + jnp.exp(-pre[r, :]))).astype(BF16)
         dst[r, :] = d
         wide = d.astype(F32)
-        low_wide = low[r, :].astype(F32)
         sums = []
         for m in range(M):
             mask = aux[r, m : m + 1]
             masked = wide * mask
             sums.append(jnp.sum(masked, axis=0, keepdims=True))
             dst3[r, m * C : (m + 1) * C] = masked.astype(BF16)
-            low3[r, m * R : (m + 1) * R] = (low_wide * mask).astype(BF16)
-        h = R // WD.shape[0]
-        for t in range(WD.shape[0]):
-            total = dot(dst3[r, 0:C], WD[t, 0], NT)
-            for m in range(1, M):
-                total = total + dot(dst3[r, m * C : (m + 1) * C], WD[t, m], NT)
-            dlow[r, t * h : (t + 1) * h] = total
+        total = dot(dst3[r, 0:C], wdt[0:R, :], NT)
+        for m in range(1, M):
+            total = total + dot(dst3[r, m * C : (m + 1) * C], wdt[m * R : (m + 1) * R, :], NT)
+        dlow[r, :] = total
         dact[r, :] = dmix[r, :] * ch[K + 1 : K + 2, :] + step[r, :] * back_b
         skip = skip + jnp.sum(dmix[r, :] * a, axis=0, keepdims=True)
         return skip, bias + jnp.concatenate(sums, axis=0)
@@ -1201,7 +1441,7 @@
 
     gtap[0 : K + 1, :] = lax.fori_loop(0, T // rows, body, jnp.zeros((K + 1, C), F32))
     for m in range(M):
-        gx[m] = dot(act3[:, m * C : (m + 1) * C], dpar[...], TN)
+        gx[m] = dot(dpar[...], act3[:, m * C : (m + 1) * C], TN)
 
 
 def block_call(S, PN, args, T, C, width):
@@ -1214,9 +1454,9 @@
     vb = lambda *shape: pltpu.VMEM(shape, BF16)
     n = S * PN
     out = (
-        b(S, TL, width), b(S, TL, width), f(PN, 8, width), f(n, 8, LANES),
-        f(S, M, R // S, C), f(M, C, R + 2 * N), f(8, C), f(1 + M + N, C),
-        b(T, width), b(T, width), f(T, 8), b(S, T, 2 * C), b(S, T, C), f(TL, LANES),
+        b(S // 2, TL, width), b(S // 2, TL, width), f(PN, 8, width), f(n, 8, LANES),
+        f(S, M, R // S, C), f(M, R + 2 * N, C), f(8, C), f(1 + M + N, C),
+        f(TL, LANES), f(8, LANES), f(M * width * 2 * S, C), f(M * S * width, C),
     )
     scratch = (
         [vf(8, TL), vb(PN, S, TL, DD // PN), vb(PN, S, TL, DD // PN), vb(T, DD)]
@@ -1225,25 +1465,30 @@
         + [vf(T, C)] * 4
         + [vf(T + 8, C), vb(T, M * C), vf(T, R), vf(chunks, 2 * N, LANES)]
         + [vb(T, C), vf(T, C), vb(T, C), vb(T, R), vf(chunks, 2 * N, LANES), vf(T, C)]
-        + [vf(T + 1, N, C), vb(T, C), vb(T, C), vf(T, C), vf(T + 8, 8), vb(T, width)]
-        + [vb(S, T, C), vb(S, T, 2 * C), vf(T, C), vf(T, C), vb(T, M * C), vb(T, M * R)]
+        + [vf((T + 1) * N, C), vb(T, C), vb(T, C), vf(T, C), vf(T + 8, 8), vb(T, width)]
+        + [vb(T, S * C), vb(T, 2 * S * C), vf(T, C), vf(T, C), vb(T, M * C), vb(T, M * R)]
         + [vb(T, C), vf(T, R), vf(chunks, 2 * N, LANES), vf(T, C), vf(M, R, C)]
         + [vb(T, R), vf(chunks, 2 * N, LANES), vf(T + 8, C), vb(T, R + 2 * N), vb(T, C)]
-        + [vb(2, T, width), vf(S, 8, LANES), vf(8, width)]
+        + [vb(2, T, width), vf(S, 8, LANES), vf(8, width), vb(M * R, C)]
+        + [vb(S, width, M * C), vb(S, width, M * C), vb(S, M * C, width), vb(M, R // S, S * C)]
+        + [vf(8, width), vb(M * C, R), vb(2 * N, M * C), vb(M, R + 2 * N, C), vb(T, width)]
+        + [vb(T, width), vf(M, R // S, S * C), vb(S * C // 2, T), vf(2, M, 2, 8, LANES)]
+        + [vf(n, 8, LANES), vf(8, LANES), dma((2,)), dma((2, 3)), dma((2,))]
+        + [vb(4, T // 2, width), dma((2, 2))]
         + Spread.semaphores(S) * 2
         + [dma((S,))] * 12
         + [dma((6,))]
         + sum_scratch(S, PN, T)
         + RowGather.semaphores(S) * 3
         + [dma((S,)), dma((S,)), dma]
-        + [dma((S,))] * 4 + [dma((PN,))] * 2 + [dma((n,))] * 2
+        + [dma((S,))] * 4 + [dma((PN,))] * 2 + [dma((n,))] * 4
     )
     vm, hb = pl.BlockSpec(memory_space=pltpu.VMEM), pl.BlockSpec(memory_space=pl.ANY)
     return pl.pallas_call(
         functools.partial(block_kernel, S, PN),
         out_shape=out,
-        in_specs=[vm] * len(args),
-        out_specs=[hb if i in (11, 12) else vm for i in range(len(out))],
+        in_specs=[vm] * (len(args) - 6) + [hb] * 6,
+        out_specs=[vm] * (len(out) - 2) + [hb] * 2,
         scratch_shapes=scratch,
         compiler_params=pltpu.CompilerParams(
             collective_id=0, has_side_effects=True, vmem_limit_bytes=VMEM_LIMIT
@@ -1251,192 +1496,89 @@
     )(*args)
 
 
-def cast_kernel(w_in, w_out, wi, wg, wo):
-    S, width, C = wi.shape
-    stride = 2 * S
-    for b in range(S):
-        wi[b] = w_in[pl.ds(2 * b, width, stride=stride), :].astype(BF16)
-        wg[b] = w_in[pl.ds(2 * b + 1, width, stride=stride), :].astype(BF16)
-        wo[b] = w_out[0, b * C : (b + 1) * C, :].astype(BF16)
-
-
-def cast_weights(S, flat, w_out):
-    _, inner_width, width = w_out.shape
-    C = inner_width // S
-    return pl.pallas_call(
-        cast_kernel,
-        out_shape=(
-            sds((S, width, M * C), BF16),
-            sds((S, width, M * C), BF16),
-            sds((S, M * C, width), BF16),
-        ),
-        grid=(M,),
-        in_specs=[
-            pl.BlockSpec((width * 2 * S, C), lambda m: (m, 0)),
-            pl.BlockSpec((1, inner_width, width), lambda m: (m, 0, 0)),
-        ],
-        out_specs=[
-            pl.BlockSpec((S, width, C), lambda m: (0, 0, m)),
-            pl.BlockSpec((S, width, C), lambda m: (0, 0, m)),
-            pl.BlockSpec((S, C, width), lambda m: (0, m, 0)),
-        ],
-        compiler_params=pltpu.CompilerParams(vmem_limit_bytes=VMEM_LIMIT),
-    )(flat, w_out)
-
-
-def to_rows(w, S):
-    m, width, two, channels = w.shape
-    c = channels // S
-    return w.reshape(m, width, two, S, c).transpose(0, 1, 3, 2, 4).reshape(-1, c)
-
-
-def from_rows(rows, S, shape):
-    m, width, two, channels = shape
-    c = channels // S
-    return rows.reshape(m, width, S, two, c).transpose(0, 1, 3, 2, 4).reshape(shape)
-
-
-def adam_terms(g, m, s):
-    new_m = BETA_ONE * m + (1.0 - BETA_ONE) * g
-    new_s = BETA_TWO * s + (1.0 - BETA_TWO) * (g * g)
-    root = jnp.sqrt(new_s * (1.0 / (1.0 - BETA_TWO**STEP))) + ADAM_EPSILON
-    return new_m, new_s, (new_m * (1.0 / (1.0 - BETA_ONE**STEP))) / root
-
-
-def corner(shape, row, value):
-    at = lambda k: lax.broadcasted_iota(jnp.int32, shape, k)
-    return jnp.where(jnp.logical_and(at(0) == row, at(1) == 0), value, 0.0)
-
-
-def adam_in_kernel(NR, aux, dall, w, m, s, nm, ns, dr, norms, turned, gs):
-    i = pl.program_id(0)
-    T, width = NR.shape
-    S = dall.shape[0]
-    C = dall.shape[2] // 2
-    mask = aux[:, 0:1]
-    for k in range(1, M):
-        mask = jnp.where(i == k, aux[:, k : k + 1], mask)
-    turned[...] = jnp.transpose((NR[...].astype(F32) * mask).astype(BF16))
-    for b in range(S):
-        g = dot(turned[...], dall[b])
-        gs[pl.ds(2 * b, width, stride=2 * S), :] = g[:, 0:C]
-        gs[pl.ds(2 * b + 1, width, stride=2 * S), :] = g[:, C : 2 * C]
+def update_kernel(steps, scale, g, w, m, s, avg, nw, nm, ns, na, which):
+    k = lax.div(pl.program_id(0), steps)
+    factor = scale[0:1, M * which : M * which + 1]
+    for i in range(1, M):
+        lane = M * which + i
+        factor = jnp.where(k == i, scale[0:1, lane : lane + 1], factor)
     rows = 256
 
-    def body(k, sums):
-        r = pl.ds(pl.multiple_of(k * rows, rows), rows)
+    def body(t, _):
+        r = pl.ds(pl.multiple_of(t * rows, rows), rows)
         weight = w[r, :]
-        new_m, new_s, ratio = adam_terms(gs[r, :], m[r, :], s[r, :])
-        direction = ratio + WEIGHT_DECAY * weight
+        new_m, new_s, ratio = adam_terms(g[r, :], m[r, :], s[r, :])
+        new = weight - factor * (ratio + WEIGHT_DECAY * weight)
+        nw[r, :] = new
         nm[r, :] = new_m
         ns[r, :] = new_s
-        dr[r, :] = direction
-        fold = lambda v: jnp.sum((v * v).reshape(rows // 8, 8, C), axis=0)
-        return sums[0] + fold(weight), sums[1] + fold(direction)
-
-    zero = jnp.zeros((8, C), F32)
-    a, b = lax.fori_loop(0, w.shape[0] // rows, body, (zero, zero))
-    norms[0, 0] = a
-    norms[0, 1] = b
-
-
-def adam_in(NR, aux, dall, w, m, s):
-    T, width = NR.shape
-    S, _, two = dall.shape
-    C = two // 2
-    piece = pl.BlockSpec((width * 2 * S, C), lambda i: (i, 0))
-    whole = lambda shape: pl.BlockSpec(shape, lambda i: (0,) * len(shape))
+        na[r, :] = AVERAGE_KEEP * avg[r, :] + (1.0 - AVERAGE_KEEP) * new
+        return 0
+
+    lax.fori_loop(0, w.shape[0] // rows, body, 0)
+
+
+def update(which, rows, scale, *arrays):
+    total, C = arrays[0].shape
+    block = pl.BlockSpec((rows, C), lambda i: (i, 0))
+
+    def kernel(*refs):
+        update_kernel(total // M // rows, *refs, which)
+
     return pl.pallas_call(
-        adam_in_kernel,
-        out_shape=(sds(w.shape), sds(w.shape), sds(w.shape), sds((M, 2, 8, C))),
-        grid=(M,),
-        in_specs=[whole((T, width)), whole((T, 8)), whole(dall.shape), piece, piece, piece],
-        out_specs=[piece, piece, piece, pl.BlockSpec((1, 2, 8, C), lambda i: (i, 0, 0, 0))],
-        scratch_shapes=[pltpu.VMEM((width, T), BF16), pltpu.VMEM((width * 2 * S, C), F32)],
+        kernel,
+        out_shape=(sds((total, C)),) * 4,
+        grid=(total // rows,),
+        in_specs=[pl.BlockSpec((8, LANES), lambda i: (0, 0))] + [block] * 5,
+        out_specs=[block] * 4,
         compiler_params=pltpu.CompilerParams(vmem_limit_bytes=VMEM_LIMIT),
-    )(NR, aux, dall, w, m, s)
-
-
-def adam_out_kernel(gall, G, aux, w, m, s, nm, ns, dr, norms, turned):
-    i = pl.program_id(0)
-    T, C = gall.shape[1:]
-    wide = gall[0].astype(F32)
-
-    @pl.when(i == 0)
-    def _():
-        norms[...] = jnp.zeros(norms.shape, F32)
-
-    for k in range(M):
-        turned[...] = jnp.transpose((wide * aux[:, k : k + 1]).astype(BF16))
-        weight = w[k]
-        new_m, new_s, ratio = adam_terms(dot(turned[...], G[...]), m[k], s[k])
-        direction = ratio + WEIGHT_DECAY * weight
-        nm[k] = new_m
-        ns[k] = new_s
-        dr[k] = direction
-        fold = lambda v: jnp.sum((v * v).reshape(C // 8, 8, v.shape[1]), axis=0)
-        norms[k, 0] += fold(weight)
-        norms[k, 1] += fold(direction)
-
-
-def adam_out(gall, G, aux, w, m, s):
-    S, T, C = gall.shape
-    width = G.shape[1]
-    piece = pl.BlockSpec((M, C, width), lambda i: (0, i, 0))
-    whole = lambda shape: pl.BlockSpec(shape, lambda i: (0,) * len(shape))
-    return pl.pallas_call(
-        adam_out_kernel,
-        out_shape=(sds(w.shape), sds(w.shape), sds(w.shape), sds((M, 2, 8, width))),
-        grid=(S,),
-        in_specs=[
-            pl.BlockSpec((1, T, C), lambda i: (i, 0, 0)),
-            whole((T, width)),
-            whole((T, 8)),
-            piece,
-            piece,
-            piece,
-        ],
-        out_specs=[piece, piece, piece, whole((M, 2, 8, width))],
-        scratch_shapes=[pltpu.VMEM((C, T), BF16)],
-        compiler_params=pltpu.CompilerParams(vmem_limit_bytes=VMEM_LIMIT),
-    )(gall, G, aux, w, m, s)
-
-
-def adam_small_kernel(
-    gx, more, gtap, gch, GG, wx, mx, sx, ax, wd, md, sd, ch, mc, sc, ac, gn, mg, sg, ag, nin, nout,
-    nmx, nsx, dx, nmd, nsd, dd, nwc, nmc, nsc, nac, nwg, nmg, nsg, nag, tile, gc, gd,
+    )(scale, *arrays)
+
+
+def rest_kernel(
+    S, PN, tok, og, LO, DN, ROW, INV, scale, gx, more, gtap, gch, GG, wx, mx, sx, ax, wd, md, sd, ad,
+    ch, mc, sc, ac, gn, mg, sg, ag,
+    layer, grad, nwx, nmx, nsx, nax, nwd, nmd, nsd, nad, nwc, nmc, nsc, nac, nwg, nmg, nsg, nag, gc, gd,
 ):
-    S = more.shape[0]
+    p = lax.axis_index("tp")
     C = more.shape[3]
-    total = jnp.zeros((8, LANES), F32)
-    lane = lax.broadcasted_iota(jnp.int32, total.shape, 1)
-
-    def put(total, k, value):
-        return jnp.where(lane == k, value, total)
-
-    square = lambda v: jnp.sum(v * v)
+    width = LO.shape[2]
+    out_width = og.shape[1]
+
+    def average(old, new):
+        return AVERAGE_KEEP * old + (1.0 - AVERAGE_KEEP) * new
+
+    along = ROW[0, 0:1, :]
+    for k in range(1, ROW.shape[0]):
+        along = along + ROW[k, 0:1, :]
+    column = jnp.transpose(jnp.broadcast_to(along, (LANES, LANES)))[:, 0:1]
+    inv = INV[:, 0:1]
+    for h in range(out_width // width):
+        cols = pl.ds(pl.multiple_of(p * out_width + h * width, LANES), width)
+        here = slice(h * width, (h + 1) * width)
+        mine = tok[:, cols].astype(F32)
+        chips = PN // 2
+        total = LO[h * chips].astype(F32)
+        back = DN[h * chips].astype(F32)
+        for q in range(1, chips):
+            total = total + LO[h * chips + q].astype(F32)
+            back = back + DN[h * chips + q].astype(F32)
+        layer[:, here] = mine + total
+        grad[:, here] = og[:, here].astype(F32) + inv * (back - mine * inv * (column / D))
     for t in range(S):
         gd[:, :, t * C : (t + 1) * C] = more[t]
     for m in range(M):
-        total = put(total, m, jnp.sum(nin[m, 0]))
-        total = put(total, 4 * M + m, jnp.sum(nin[m, 1]))
-        total = put(total, 3 * M + m, jnp.sum(nout[m, 0]))
-        total = put(total, 7 * M + m, jnp.sum(nout[m, 1]))
-        new_m, new_s, ratio = adam_terms(gx[m], mx[m], sx[m])
-        direction = ratio + WEIGHT_DECAY * wx[m]
-        nmx[m] = new_m
-        nsx[m] = new_s
-        dx[m] = direction
-        total = put(total, M + m, square(wx[m]))
-        total = put(total, 5 * M + m, square(direction))
-        new_m, new_s, ratio = adam_terms(gd[m], md[m], sd[m])
-        direction = ratio + WEIGHT_DECAY * wd[m]
-        nmd[m] = new_m
-        nsd[m] = new_s
-        dd[m] = direction
-        total = put(total, 2 * M + m, square(wd[m]))
-        total = put(total, 6 * M + m, square(direction))
-    tile[...] = total
+        for k, g, w, mo, sq, av, nw, nm, ns, na in (
+            (1, gx, wx, mx, sx, ax, nwx, nmx, nsx, nax),
+            (2, gd, wd, md, sd, ad, nwd, nmd, nsd, nad),
+        ):
+            factor = scale[0:1, M * k + m : M * k + m + 1]
+            new_m, new_s, ratio = adam_terms(g[m], mo[m], sq[m])
+            new = w[m] - factor * (ratio + WEIGHT_DECAY * w[m])
+            nw[m] = new
+            nm[m] = new_m
+            ns[m] = new_s
+            na[m] = average(av[m], new)
     gc[0 : K + 1, :] = gtap[0 : K + 1, :]
     gc[K + 1 :, :] = gch[...]
     new_m, new_s, ratio = adam_terms(gc[...], mc[...], sc[...])
@@ -1444,70 +1586,42 @@
     nwc[...] = new
     nmc[...] = new_m
     nsc[...] = new_s
-    nac[...] = AVERAGE_KEEP * ac[...] + (1.0 - AVERAGE_KEEP) * new
+    nac[...] = average(ac[...], new)
     g = GG[0, 0:1, :]
-    for q in range(1, GG.shape[0]):
+    for q in range(1, PN):
         g = g + GG[q, 0:1, :]
     new_m, new_s, ratio = adam_terms(g, mg[...], sg[...])
     new = gn[...] - GAIN_RATE * ratio
     nwg[...] = new
     nmg[...] = new_m
     nsg[...] = new_s
-    nag[...] = AVERAGE_KEEP * ag[...] + (1.0 - AVERAGE_KEEP) * new
-
-
-def norms_kernel(S, PN, tile, TILE, ts, tr):
-    greet_all(S, PN)
-    s, p = lax.axis_index("seq"), lax.axis_index("tp")
-    n = S * PN
-    me = s * PN + p
-
-    def copy(k):
-        j = lax.rem(me + k, n)
-        device = {"seq": lax.div(j, PN), "tp": lax.rem(j, PN)}
-        return seq_copy(tile, TILE.at[k], ts.at[k], tr.at[k], device)
-
-    def send(k, _):
-        copy(k).start()
-        return 0
-
-    def wait(k, _):
-        copy(k).wait()
-        return 0
-
-    lax.fori_loop(1, n, send, 0)
-    TILE[0] = tile[...]
-    lax.fori_loop(1, n, wait, 0)
-
-
-def norms_over_all(S, PN, tile):
-    n = S * PN
-    dma = pltpu.SemaphoreType.DMA
-    return remote_call(
-        functools.partial(norms_kernel, S, PN), sds((n,) + tile.shape), 1, [dma((n,))] * 2, 1
-    )(tile)
-
-
-def final_rows_kernel(scale, w, dr, avg, nw, na):
-    k = scale[pl.program_id(0)]
-    new = w[...] - k * dr[...]
-    nw[...] = new
-    na[...] = AVERAGE_KEEP * avg[...] + (1.0 - AVERAGE_KEEP) * new
-
-
-def final_rows(scale, w, dr, avg, pieces):
-    shape = w.shape
-    rows = lambda v: v.reshape(M * pieces, -1, shape[-1])
-    block = pl.BlockSpec((1, w.size // shape[-1] // M // pieces, shape[-1]), lambda i: (i, 0, 0))
-    nw, na = pl.pallas_call(
-        final_rows_kernel,
-        out_shape=(sds(rows(w).shape), sds(rows(w).shape)),
-        grid=(M * pieces,),
-        in_specs=[pl.BlockSpec(memory_space=pltpu.SMEM), block, block, block],
-        out_specs=[block, block],
-        compiler_params=pltpu.CompilerParams(vmem_limit_bytes=VMEM_LIMIT),
-    )(jnp.repeat(scale, pieces), rows(w), rows(dr), rows(avg))
-    return nw.reshape(shape), na.reshape(shape)
+    nag[...] = average(ag[...], new)
+
+
+def to_rows(w, S):
+    m, width, two, channels = w.shape
+    c = channels // S
+    return w.reshape(m, width, two, S, c).transpose(0, 1, 3, 2, 4).reshape(-1, c)
+
+
+def from_rows(rows, S, shape):
+    m, width, two, channels = shape
+    c = channels // S
+    return rows.reshape(m, width, S, two, c).transpose(0, 1, 3, 2, 4).reshape(shape)
+
+
+def to_tiles(w):
+    m, rows, columns = w.shape
+    return w.reshape(m, rows // 8, 8, columns // LANES, LANES).transpose(0, 1, 3, 2, 4).reshape(
+        -1, LANES
+    )
+
+
+def from_tiles(flat, shape):
+    m, rows, columns = shape
+    return flat.reshape(m, rows // 8, columns // LANES, 8, LANES).transpose(0, 1, 3, 2, 4).reshape(
+        shape
+    )
 
 
 def local(
@@ -1518,81 +1632,49 @@
     average_in, average_x, average_dt, average_out, average_channel, average_gain,
 ):
     S, PN = lax.axis_size("seq"), lax.axis_size("tp")
-    p = lax.axis_index("tp")
     TL = tokens.shape[0]
     T = S * TL
     width = D // S
     inner_width = w_out.shape[1]
     C = inner_width // S
-    flat_in = to_rows(w_in, S)
-    wi, wg, wo = cast_weights(S, flat_in, w_out)
-    wx = w_x.astype(BF16)
-    wlr = wx[:, :, :R].reshape(M * C, R)
-    wbc = jnp.transpose(wx[:, :, R:], (2, 0, 1)).reshape(2 * N, M * C)
+    ins = [to_rows(v, S) for v in (w_in, moment_in, square_in, average_in)]
+    outs = [to_tiles(v) for v in (w_out, moment_out, square_out, average_out)]
     modrow = jnp.broadcast_to(modality.astype(F32)[None], (8, TL))
     ahead = jnp.concatenate([jnp.full((K - 1,), -1, jnp.int32), segment])
     same = [(ahead[k : k + T] == segment).astype(F32) for k in range(K - 1)]
     zero = jnp.zeros((T,), F32)
     segs = jnp.stack([zero] * M + same + [same[K - 2], zero], axis=1)
-    gain = norm_gain[None, :]
-    LO, DN, GG, ROW, MORE, gx, gtap, gch, NR, G, aux, dall, gall, INV = block_call(
+    row = lambda v: v[None, :]
+    xs = [jnp.transpose(v, (0, 2, 1)) for v in (w_x, moment_x, square_x, average_x)]
+    LO, DN, GG, ROW, MORE, gx, gtap, gch, INV, scale, g_in, g_out = block_call(
         S,
         PN,
         (
-            tokens, out_grad, modrow, w_dt.astype(BF16), jnp.broadcast_to(gain, (8, width)),
-            wi, wg, wo, segs, channel, wlr, wbc, jnp.transpose(wx, (0, 2, 1)),
+            tokens, out_grad, modrow, row(norm_gain), segs, channel,
+            *xs[:3], w_dt, moment_dt, square_dt, *ins[:3], *outs[:3],
         ),
         T, C, width,
     )
-    nm_in, ns_in, dir_in, norm_in = adam_in(
-        NR, aux, dall, flat_in, to_rows(moment_in, S), to_rows(square_in, S)
-    )
-    nm_out, ns_out, dir_out, norm_out = adam_out(gall, G, aux, w_out, moment_out, square_out)
+    new_in = [from_rows(v, S, w_in.shape) for v in update(0, 4096, scale, g_in, *ins)]
+    new_out = [from_tiles(v, w_out.shape) for v in update(3, 1024, scale, g_out, *outs)]
     like = lambda v: sds(v.shape)
-    row = lambda v: v[None, :]
     vec = sds((1, width))
-    (
-        nm_x, ns_x, dir_x, nm_dt, ns_dt, dir_dt, nw_ch, nm_ch, ns_ch, na_ch,
-        nw_g, nm_g, ns_g, na_g, tile,
-    ) = local_call(
-        adam_small_kernel,
-        (like(w_x),) * 3 + (like(w_dt),) * 3 + (like(channel),) * 4 + (vec,) * 4
-        + (sds((8, LANES)),),
-        22,
+    rest = local_call(
+        functools.partial(rest_kernel, S, PN),
+        (sds(out_grad.shape),) * 2 + (like(xs[0]),) * 4 + (like(w_dt),) * 4 + (like(channel),) * 4
+        + (vec,) * 4,
+        28,
         [pltpu.VMEM(channel.shape, F32), pltpu.VMEM(w_dt.shape, F32)],
     )(
-        gx, MORE, gtap, gch, GG, w_x, moment_x, square_x, average_x,
-        w_dt, moment_dt, square_dt, channel, moment_channel, square_channel, average_channel,
-        gain, row(moment_gain), row(square_gain), row(average_gain), norm_in, norm_out,
-    )
-    TILE = norms_over_all(S, PN, tile)
-    totals = jnp.sum(TILE[:, 0, : 8 * M], axis=0).reshape(2, 4, M)
-    scales = MATRIX_RATE * (jnp.sqrt(totals[0]) / jnp.sqrt(totals[1]))
-    nw_in, na_in = final_rows(scales[0], flat_in, dir_in, to_rows(average_in, S), 2)
-    nw_out, na_out = final_rows(scales[3], w_out, dir_out, average_out, 1)
-    nw_x = w_x - scales[1][:, None, None] * dir_x
-    nw_dt = w_dt - scales[2][:, None, None] * dir_dt
-    na_x = AVERAGE_KEEP * average_x + (1.0 - AVERAGE_KEEP) * nw_x
-    na_dt = AVERAGE_KEEP * average_dt + (1.0 - AVERAGE_KEEP) * nw_dt
-
-    def columns(blocks):
-        b = jnp.sum(blocks.reshape(S // PN, PN, TL, width).astype(F32), axis=1)
-        return jnp.concatenate([b[h] for h in range(S // PN)], axis=1)
-
-    along = jnp.sum(ROW[:, 0, :], axis=0)[:, None]
-    out_width = out_grad.shape[1]
-    mine = lax.dynamic_slice_in_dim(tokens, p * out_width, out_width, 1).astype(F32)
-    inv = INV[:, 0:1]
-    layer_out = mine + columns(LO)
-    tokens_grad = out_grad.astype(F32) + inv * (columns(DN) - mine * inv * (along / D))
-    back = lambda v: from_rows(v, S, w_in.shape)
-    return (
-        layer_out, tokens_grad,
-        back(nw_in), nw_x, nw_dt, nw_out, nw_ch, nw_g[0],
-        back(nm_in), nm_x, nm_dt, nm_out, nm_ch, nm_g[0],
-        back(ns_in), ns_x, ns_dt, ns_out, ns_ch, ns_g[0],
-        back(na_in), na_x, na_dt, na_out, na_ch, na_g[0],
-    )
+        tokens, out_grad, LO, DN, ROW, INV, scale, gx, MORE, gtap, gch, GG,
+        *xs, w_dt, moment_dt, square_dt, average_dt,
+        channel, moment_channel, square_channel, average_channel,
+        row(norm_gain), row(moment_gain), row(square_gain), row(average_gain),
+    )
+    new_x, new_dt, new_ch, new_g = [rest[2 + 4 * k : 6 + 4 * k] for k in range(4)]
+    new_x = [jnp.transpose(v, (0, 2, 1)) for v in new_x]
+    groups = [(new_in[k], new_x[k], new_dt[k], new_out[k], new_ch[k], new_g[k][0]) for k in range(4)]
+    return (*rest[:2], *groups[0], *groups[1], *groups[2], *groups[3])
 
 
 def channels_fit(mesh):

time: 481 us -> 365 us (0.76)
  Pallas kernels: 456 us -> 361 us
  local copies, waits for them, and re-layouts: 13.7 us -> 1.66 us
  other arithmetic: 9.23 us -> 1.57 us
    pallas_call x1, Pallas kernels: 379 us -> 318 us  [block_call(): pl.pallas_call(functools.partial(block_kernel, S, PN), out_shape=out, in_...]
    pallas_call x7 -> x3, Pallas kernels: 77.2 us -> 42.2 us  [the longest x2 38.2 us: update(): pl.pallas_call(kernel, out_shape=(sds((total, C)),) * 4, grid=(total // r...]
    unnamed x36 -> x0, local copies, waits for them, and re-layouts: 7.19 us -> none
where the time goes in v3:
time: 365 us; the launch traced here: 364 us
  Pallas kernels  361 us (99%)
    pallas_call x1, Pallas kernels, block_call(): pl.pallas_call(functools.partial(block_kernel, S, PN), out_shape=out, in_...  318 us
    pallas_call x2, Pallas kernels, update(): pl.pallas_call(kernel, out_shape=(sds((total, C)),) * 4, grid=(total // r...  38.2 us

profile of v3, /device:TPU:0, one launch (start us, length us, event | category | flops | bytes accessed | tf_op | source)
XLA Modules:
  0.0 364.5 jit_solution(11221052347551626855)
XLA Ops:
  0.7 0.9 fusion.3
  1.6 0.1 stack.32
  1.6 1.0 copy.77.refs_4_
  2.6 0.7 convert_element_type.2
  3.3 0.6 broadcast_in_dim.19.refs_2_
  3.9 318.3 %shard_map.467 = (bf16[4,128,256]{2,1,0:T(8,128)(2,1)}, bf16[4,128,256]{2,1,0:T(8,128)(2,1)}, f32[4,8,256]{2,1,0:T(8,128)}, f32[32,8,128]{2,1,0:T(8,128)}, f32[8...) custom-call(bf16[128,2048]{1,0:T(8,128)(2,1)} %tok.1, ...), custom_call_target="tpu_custom_call" | custom-call | tf_op jit(solution)/shard_map/pallas_call | solution.py:1487
  322.2 4.1 %shard_map.468 = (f32[128,512]{1,0:T(8,128)}, f32[128,512]{1,0:T(8,128)}, f32[3,160,128]{2,1,0:T(8,128)}, f32[3,160,128]{2,1,0:T(8,128)}, f32[3,160,128]{2,1,0:T...) custom-call(bf16[128,2048]{1,0:T(8,128)(2,1)} %tok.1, ...), custom_call_target="tpu_custom_call" | custom-call | tf_op jit(solution)/shard_map/pallas_call | solution.py:1662
  326.3 24.9 %shard_map.469 = (f32[12288,128]{1,0:T(8,128)}, f32[12288,128]{1,0:T(8,128)}, f32[12288,128]{1,0:T(8,128)}, f32[12288,128]{1,0:T(8,128)}) custom-call(f32[8,128]{1,0:T(8,128)} %get-tuple-element.68.scale.refs_0_, f32[12288,128]{1,0:T(8,128)} %get-tuple-element.76.refs_1_, f32[12288,128]{1,0:T(8,128)} %bitcast.100, f32[12288,128]{1,0:T(8,128)} %bitcast.102, ...), custom_call_target="tpu_custom_call" | custom-call | tf_op jit(solution)/shard_map/pallas_call | solution.py:1528
  351.2 13.3 %shard_map.470 = (f32[6144,128]{1,0:T(8,128)}, f32[6144,128]{1,0:T(8,128)}, f32[6144,128]{1,0:T(8,128)}, f32[6144,128]{1,0:T(8,128)}) custom-call(f32[8,128]{1,0:T(8,128)} %get-tuple-element.68.scale.refs_0_, f32[6144,128]{1,0:T(8,128)} %get-tuple-element.80.refs_1_, f32[6144,128]{1,0:T(8,128)} %bitcast.106, f32[6144,128]{1,0:T(8,128)} %bitcast.108, ...), custom_call_target="tpu_custom_call" | custom-call | tf_op jit(solution)/shard_map/pallas_call | solution.py:1528
  (2 shorter events, 0.0 us)

commit v4 on v3

--- a/solution.py
+++ b/solution.py
@@ -624,55 +624,174 @@
     )
 
 
-class RowGather:
-    def __init__(self, S, own, place_of, zs, zr, xs, xr, ls):
-        s, p, z, x = place(S, 1)
+class FeatureGather:
+    def __init__(self, S, PN, own, buf, s1, r1, s2, r2, cs, cr, ys, yr, ls):
+        s, p, z, x = place(S, PN)
         self.zn = zn = S // 2
-        other = {"seq": 2 * z + 1 - x}
-        at = lambda k: 2 * lax.rem(z - k + zn, zn) + x
-        self.local = pltpu.make_async_copy(own, place_of(s), ls)
-        self.z = [
-            seq_copy(own, place_of(s), zs.at[k], zr.at[k], {"seq": 2 * lax.rem(z + k, zn) + x})
-            for k in range(1, zn)
+        self.root = p == z
+        self.relay = lax.rem(p + 2, PN) == z
+        self.twin_of_root = p + 1 - 2 * lax.rem(p, 2) == z
+        self.z = z
+        self.moves = z != p
+        self.local = pltpu.make_async_copy(own, buf.at[z, x], ls)
+        self.first = seq_copy(own, buf.at[z, x], s1, r1.at[z], {"seq": 2 * p + x})
+        self.arrive = [
+            seq_copy(own, buf.at[t, x], s1, r1.at[t], {"seq": 2 * lax.rem(z + 1, zn) + x})
+            for t in range(zn)
         ]
-        self.x = [
-            seq_copy(
-                own if k == 0 else place_of(at(k)), place_of(at(k)), xs.at[k], xr.at[k], other
-            )
-            for k in range(zn)
-        ]
-
-    def start(self, *which):
-        for k in which:
-            if k == 0:
-                self.local.start()
-                self.x[0].start()
-            elif k < self.zn:
-                self.z[k - 1].start()
-
-    def start_from(self, first):
-        self.start(*range(first, self.zn))
-
-    def forward(self, k):
-        if k < self.zn:
-            self.z[k - 1].wait_recv()
-            self.x[k].start()
-
-    def forward_from(self, first):
-        for k in range(first, self.zn):
-            self.forward(k)
+        halves = [buf.at[:, x], buf.at[:, 1 - x]]
+        twin = {"tp": p + 1 - 2 * lax.rem(p, 2)}
+        far = {"tp": lax.rem(p + 2, PN)}
+        self.across = seq_copy(halves[0], halves[0], s2, r2, {"seq": 2 * z + 1 - x})
+        self.core = [seq_copy(h, h, cs.at[j], cr.at[j], twin) for j, h in enumerate(halves)]
+        self.y = [seq_copy(h, h, ys.at[j], yr.at[j], far) for j, h in enumerate(halves)]
+
+    def start(self):
+        @pl.when(self.moves)
+        def _():
+            self.first.start()
+
+        @pl.when(jnp.logical_not(self.moves))
+        def _():
+            self.local.start()
+            self.local.wait()
+
+    def near(self):
+        @pl.when(self.root)
+        def _():
+            for t in range(self.zn):
+
+                @pl.when(self.z != t)
+                def _():
+                    self.arrive[t].wait_recv()
+
+            self.across.start()
+            self.core[0].start()
+            self.y[0].start()
+
+    def far(self):
+        @pl.when(self.root)
+        def _():
+            self.across.wait_recv()
+            self.core[1].start()
+            self.y[1].start()
+
+        self.pass_on(0)
+
+    def pass_on(self, j):
+        @pl.when(self.relay)
+        def _():
+            self.y[j].wait_recv()
+            self.core[j].start()
 
     def finish(self):
-        self.local.wait()
-        for cp in self.z:
-            cp.wait_send()
-        for cp in self.x:
-            cp.wait()
+        self.pass_on(1)
+
+        @pl.when(self.moves)
+        def _():
+            self.first.wait_send()
+
+        @pl.when(self.root)
+        def _():
+            self.across.wait_send()
+            for cp in self.core + self.y:
+                cp.wait_send()
+
+        @pl.when(self.relay)
+        def _():
+            for cp in self.core:
+                cp.wait_send()
+
+        @pl.when(jnp.logical_not(jnp.logical_or(self.root, self.relay)))
+        def _():
+            for cp in self.core:
+                cp.wait_recv()
 
     @staticmethod
     def semaphores(S):
         dma = pltpu.SemaphoreType.DMA
-        return [dma((S // 2,))] * 4 + [dma]
+        return [dma, dma((S // 2,)), dma, dma] + [dma((2,))] * 4 + [dma]
+
+
+class RowGather:
+    PARTS = 2
+
+    def __init__(self, S, own, place_of, us, ur, ds, dr, xs, xr, ls):
+        s, p, z, x = place(S, 1)
+        self.zn, self.z, self.x, self.own, self.place_of = S // 2, z, x, own, place_of
+        self.up_sems, self.down_sems, self.x_sems = (us, ur), (ds, dr), (xs, xr)
+        self.every = pl.ds(0, own.shape[0])
+        self.local = pltpu.make_async_copy(own, place_of(self.every, s), ls)
+
+    def hop(self, t, d, h, up, toward=1):
+        size = self.own.shape[0] // self.PARTS
+        r = pl.ds(h * size, size)
+        there = self.place_of(r, 2 * t + self.x)
+        send, recv = self.up_sems if up else self.down_sems
+        chip = self.z + (toward if up else -toward)
+        src = self.own.at[r] if d == 1 else there
+        return seq_copy(src, there, send.at[d, h], recv.at[d, h], {"seq": 2 * chip + self.x})
+
+    def across(self, t):
+        block = self.place_of(self.every, 2 * t + self.x)
+        send, recv = self.x_sems
+        other = {"seq": 2 * self.z + 1 - self.x}
+        return seq_copy(block, block, send.at[t], recv.at[t], other)
+
+    def can(self, d, up):
+        z, last = self.z, self.zn - 1
+        if up:
+            return jnp.logical_and(z >= d - 1, z < last)
+        return jnp.logical_and(z + d - 1 <= last, z > 0)
+
+    def start(self):
+        self.local.start()
+        for h in range(self.PARTS):
+            for up in (True, False):
+
+                @pl.when(self.can(1, up))
+                def _():
+                    self.hop(self.z, 1, h, up).start()
+
+        self.local.wait()
+        self.across(self.z).start()
+
+    def step(self, d):
+        if d >= self.zn:
+            return
+        for up in (True, False):
+            t = self.z - d if up else self.z + d
+            there = self.z >= d if up else self.z + d < self.zn
+
+            @pl.when(there)
+            def _():
+                for h in range(self.PARTS):
+                    self.hop(t, d, h, up, -1).wait_recv()
+                    if d + 1 < self.zn:
+
+                        @pl.when(self.can(d + 1, up))
+                        def _():
+                            self.hop(t, d + 1, h, up).start()
+
+                self.across(t).start()
+
+    def finish(self):
+        for d in range(1, self.zn):
+            for h in range(self.PARTS):
+                for up in (True, False):
+
+                    @pl.when(self.can(d, up))
+                    def _():
+                        t = self.z - (d - 1) if up else self.z + (d - 1)
+                        self.hop(t, d, h, up).wait_send()
+
+        for t in range(self.zn):
+            self.across(t).wait()
+
+    @staticmethod
+    def semaphores(S):
+        dma = pltpu.SemaphoreType.DMA
+        return [dma((S // 2, RowGather.PARTS))] * 4 + [dma((S // 2,))] * 2 + [dma]
 
 
 def adam_terms(g, m, s):
@@ -702,7 +821,8 @@
     tok, og, modrow, gain, segs, ch, w_x, m_x, s_x, w_dt, m_dt, s_dt = take(12)
     w_in, m_in, s_in, w_out, m_out, s_out = take(6)
     LO, DN, GG, ROW, MORE, gx, gtap, gch, INV, SCALE, g_in, g_out = take(12)
-    tile, toks, ogs, nrm, Wi, Wg, Wo, AUX, GAIN, WD = take(10)
+    tile, toks, ogz, nrm, Wi, Wg, Wo, AUX, GAIN, WD = take(10)
+    gsend, grecv, osend, orecv = take(4)
     step, drive, keep, Y, pad, act3, lr, bcp = take(8)
     act, conv, inner, low, bct, pre, H, gated, dgate, dmix, aux, X = take(12)
     gall, dall, DS, DB, dst3, low3, dst, dlow, dbct, dact, gdt = take(11)
@@ -711,10 +831,11 @@
     gdt_mine, turned, sums_ref, TILE, total_tile = take(5)
     stage, load, store, pair, swaps = take(5)
     ag1, ag2 = take(9), take(9)
+    parts_sems = take(4)
     ws = take(12)
     ls = take(1)[0]
     sums = take(16)
-    rows_g, rows_d, rows_i = take(5), take(5), take(5)
+    rows_g, rows_d, rows_i = take(7), take(7), take(7)
     mx, mr, ml = take(3)
     last = take(10)
     s, p, z, x = place(S, PN)
@@ -747,9 +868,26 @@
     )
     dts = row_copies(S, lambda d: wdt_mine.at[:, :, chans(d)], lambda t: WD.at[t], ws[4], ws[5])
     inners = row_copies(S, lambda d: wi.at[d], lambda t: Wi.at[block(t)], ws[6], ws[7])
-    gates = row_copies(S, lambda d: wg.at[d], lambda t: Wg.at[block(t)], ws[8], ws[9])
-    outs = row_copies(S, lambda d: wo.at[d], lambda t: Wo.at[t], ws[10], ws[11])
-    cotangent = Spread(S, PN, og, ogs, *ag2)
+    zn = S // 2
+    across = {"seq": 2 * z + 1 - x}
+    pair_rows = pl.ds(pl.multiple_of(x * width, width), width)
+    gate_swap = seq_copy(wg.at[:, 1 - x], Wg.at[:, pair_rows], ws[8].at[0], ws[9].at[0], across)
+    out_swap = seq_copy(
+        wo.at[:, 1 - x], Wo.at[:, :, pair_rows], ws[10].at[0], ws[11].at[0], across
+    )
+
+    def along(k, send, recv, sems):
+        return seq_copy(
+            send.at[k - 1],
+            recv.at[k - 1],
+            sems[0].at[k],
+            sems[1].at[k],
+            {"seq": 2 * lax.rem(z + k, zn) + x},
+        )
+
+    gates = [along(k, gsend, grecv, parts_sems[0:2]) for k in range(1, zn)]
+    backs = [along(k, osend, orecv, parts_sems[2:4]) for k in range(1, zn)]
+    cotangent = FeatureGather(S, PN, og, ogz, *ag2)
     for cp in small:
         cp.start()
     tokens.start()
@@ -761,10 +899,12 @@
             wi[b, :, m * C : (m + 1) * C] = H[r, :].astype(BF16)
     for cp in inners + dts:
         cp.start()
+    cotangent.start()
     for m in range(M):
         for b in range(S):
             r = pl.ds(m * width * stride + 2 * b + 1, width, stride=stride)
-            wg[b, :, m * C : (m + 1) * C] = H[r, :].astype(BF16)
+            wg[b // 2, b % 2, :, m * C : (m + 1) * C] = H[r, :].astype(BF16)
+    gate_swap.start()
     load_out = pltpu.make_async_copy(w_out, H.at[0 : w_out.shape[0]], stage.at[1])
     load_out.start()
     own = [
@@ -772,7 +912,7 @@
         pltpu.make_async_copy(gain_mine, GAIN.at[s], ls.at[1]),
         pltpu.make_async_copy(wdt_mine.at[:, :, chans(s)], WD.at[s], ls.at[2]),
         pltpu.make_async_copy(wi.at[s], Wi.at[block(s)], ls.at[3]),
-        pltpu.make_async_copy(wg.at[s], Wg.at[block(s)], ls.at[4]),
+        pltpu.make_async_copy(wg.at[:, x], Wg.at[:, pair_rows], ls.at[4]),
     ]
     for cp in own:
         cp.start()
@@ -787,14 +927,16 @@
             rows_b = H[(m * S + b) * C * tiles : (m * S + b + 1) * C * tiles, :]
             pieces = rows_b.reshape(C // 8, tiles, 8, LANES)
             for t in range(tiles):
-                wo[b, m * C : (m + 1) * C, t * LANES : (t + 1) * LANES] = (
+                wo[b // 2, b % 2, m * C : (m + 1) * C, t * LANES : (t + 1) * LANES] = (
                     pieces[:, t].reshape(C, LANES).astype(BF16)
                 )
-    own.append(pltpu.make_async_copy(wo.at[s], Wo.at[s], ls.at[5]))
+    out_swap.start()
+    own.append(pltpu.make_async_copy(wo.at[:, x], Wo.at[:, :, pair_rows], ls.at[5]))
     own[-1].start()
     for cp in own:
         cp.wait()
     tokens.forward()
+    cotangent.near()
     for cp in small:
         cp.wait()
     lane = lax.broadcasted_iota(jnp.int32, (TL, 8), 1)
@@ -826,10 +968,38 @@
     lax.fori_loop(0, S, norm, 0)
     for cp in inners:
         cp.wait()
-    for cp in gates[0:1]:
-        cp.start()
 
     big = 256
+    features = pl.ds(pl.multiple_of(z * 2 * width, 2 * width), 2 * width)
+
+    def gate_part(k):
+        def body(i, _):
+            r = pl.ds(pl.multiple_of(i * big, big), big)
+            w = Wg[lax.rem(z + k, zn)]
+            value = masked_sum(dot(nrm[r, features], w), aux, r, C)
+            if k == 0:
+                DS[r, :] = value
+            else:
+                gsend[k - 1, r, :] = value.astype(BF16)
+            return 0
+
+        lax.fori_loop(0, T // big, body, 0)
+
+    def back_part(k):
+        def body(i, _):
+            r = pl.ds(pl.multiple_of(i * big, big), big)
+            w = Wo[lax.rem(z + k, zn)]
+            chips = big // TL // 2
+            g = ogz[pl.ds(i * chips, chips)].reshape(big, 2 * width)
+            value = masked_sum(dot(g, w, NT), aux, r, C)
+            if k == 0:
+                DB[r, :] = value
+            else:
+                osend[k - 1, r, :] = value.astype(BF16)
+            return 0
+
+        lax.fori_loop(0, T // big, body, 0)
+
     pad[0:8, :] = jnp.zeros((8, C), F32)
 
     def first(i, _):
@@ -859,21 +1029,34 @@
         return 0
 
     lax.fori_loop(0, T // rows, convolve, 0)
-    def start_all(copies):
-        for cp in copies:
-            cp.start()
+    cotangent.far()
+
+    def during_first():
+        gate_swap.wait()
+        gate_part(1)
+        gates[0].start()
+        gate_part(2)
+        gates[1].start()
+        gate_part(3)
+        gate_part(0)
+
+    def during_second():
+        gates[2].start()
+        cotangent.finish()
+        out_swap.wait()
+        back_part(1)
+        backs[0].start()
 
     sum_over_all(
-        S, PN, lr, bcp, low, bct, *sums,
-        between=(lambda: start_all(gates[1:3]), lambda: start_all(gates[3:5])),
-    )
-    start_all(gates[5:])
+        S, PN, lr, bcp, low, bct, *sums, between=(during_first, during_second)
+    )
+    back_part(2)
+    backs[1].start()
+    back_part(3)
+    backs[2].start()
+    back_part(0)
     for cp in dts:
         cp.wait()
-    cotangent.start()
-    for cp in outs:
-        cp.start()
-
     for m in range(M):
         for t in range(S):
             h = R // S
@@ -898,36 +1081,16 @@
 
     lax.fori_loop(0, T // rows, prepare, 0)
     scan_forward(T, C, bct, ch, step, drive, keep, H, Y)
-    cotangent.forward()
-    for cp in gates:
+    for cp in gates + backs:
         cp.wait()
-
-    def gate(i, _):
-        r = pl.ds(pl.multiple_of(i * big, big), big)
-        drive[r, :] = masked_sum(dot(nrm[r, :], Wg[...]), aux, r, C)
-        return 0
-
-    lax.fori_loop(0, T // big, gate, 0)
-    cotangent.finish()
-    for cp in outs:
-        cp.wait()
-
-    def back(i, _):
-        r = pl.ds(pl.multiple_of(i * big, big), big)
-        acc = jnp.zeros((big, M * C), F32)
-        for q in range(PN):
-            g = ogs[q, pl.ds(i * (big // TL), big // TL)].reshape(big, quarter)
-            for j in range(per):
-                acc = acc + dot(g[:, j * width : (j + 1) * width], Wo[q * per + j], NT)
-        keep[r, :] = masked_sum(acc, aux, r, C)
-        return 0
-
-    lax.fori_loop(0, T // big, back, 0)
 
     def finish(i, _):
         r = pl.ds(pl.multiple_of(i * rows, rows), rows)
         mixed = Y[r, :] + ch[K + 1 : K + 2, :] * act[r, :].astype(F32)
-        g, d = drive[r, :], keep[r, :]
+        g, d = DS[r, :], DB[r, :]
+        for k in range(zn - 1):
+            g = g + grecv[k, r, :].astype(F32)
+            d = d + orecv[k, r, :].astype(F32)
         sig = 1.0 / (1.0 + jnp.exp(-g))
         gated[r, :] = (mixed * (g * sig)).astype(BF16)
         dmix[r, :] = d * (g * sig)
@@ -937,20 +1100,19 @@
     lax.fori_loop(0, T // rows, finish, 0)
     half = lambda t, k: pl.ds(pl.multiple_of((2 * t + k) * C, LANES), C)
     gathers = [
-        RowGather(S, gated, lambda t: gall.at[:, chans(t)], *rows_g),
-        RowGather(S, dgate, lambda t: dall.at[:, half(t, 1)], *rows_d),
-        RowGather(S, dinner, lambda t: dall.at[:, half(t, 0)], *rows_i),
+        RowGather(S, gated, lambda r, t: gall.at[r, chans(t)], *rows_g),
+        RowGather(S, dgate, lambda r, t: dall.at[r, half(t, 1)], *rows_d),
+        RowGather(S, dinner, lambda r, t: dall.at[r, half(t, 0)], *rows_i),
     ]
-    gathers[0].start(0, 1, 2)
+    gathers[0].start()
+    gathers[1].start()
     mine = pl.ds(pl.multiple_of(lax.rem(s, per) * width, width), width)
     NR[...] = nrm[:, pl.ds(pl.multiple_of(s * width, width), width)]
 
     def own_features(t, _):
         r = pl.ds(pl.multiple_of(t * TL, TL), TL)
         X[r, :] = toks[lax.div(s, per), t, :, mine]
-        G[r, :] = ogs[lax.div(s, per), t, :, mine]
-        drive[r, :] = step[r, :] * act[r, :].astype(F32)
-        keep[r, :] = jnp.broadcast_to(aux[r, 6:7], (TL, C))
+        G[r, :] = ogz[lax.div(t, 2), lax.rem(t, 2), :, mine]
         return 0
 
     lax.fori_loop(0, S, own_features, 0)
@@ -958,7 +1120,7 @@
     scan_backward(
         pre, H, dmix, act, bct, aux, ch, wdt, low,
         dlow, dbct, gdt, gch, dact, step, drive, keep, DS, DB, dst3, low3, dst,
-        [],
+        [(T // LANES * 3 // 4, lambda: gathers[0].step(1))],
     )
     h = R // S
     part_dt = lambda d: gdt.at[:, pl.ds(pl.multiple_of(d * h, 8), h), :]
@@ -966,22 +1128,20 @@
     more_own = pltpu.make_async_copy(part_dt(s), MORE.at[s], ml)
     for cp in more + [more_own]:
         cp.start()
+    def during_second_sum():
+        gathers[1].step(1)
+        gathers[0].step(3)
+
     sum_over_all(
         S, PN, dlow, dbct, LR2, BCT2, *sums,
-        between=(lambda: gathers[0].start_from(3), lambda: gathers[1].start(0, 1)),
-    )
-    gathers[1].start(2)
-    gathers[0].forward(1)
-    gathers[0].forward(2)
+        between=(lambda: gathers[0].step(2), during_second_sum),
+    )
     convolve_backward(
         LR2, BCT2, act, conv, aux, ch, wxT, dact, dinner, gx, gtap, pad, tail, act3, dpar
     )
-    gathers[1].start_from(3)
-    gathers[2].start_from(0)
+    gathers[2].start()
     for cp in more + [more_own]:
         cp.wait()
-    gathers[0].forward_from(3)
-    gathers[1].forward(1)
     gathers[0].finish()
 
     large = 512
@@ -991,7 +1151,9 @@
 
         total = jnp.zeros((large, width), F32)
         for m in range(M):
-            w = jnp.concatenate([wo[b, m * C : (m + 1) * C, :] for b in range(S)], axis=0)
+            w = jnp.concatenate(
+                [wo[b // 2, b % 2, m * C : (m + 1) * C, :] for b in range(S)], axis=0
+            )
             total = total + dot(gall[r, :], w) * aux[r, m : m + 1]
         part[0, r, :] = total.astype(BF16)
         return 0
@@ -1014,7 +1176,7 @@
         S, PN, part.at[0], LO, pair.at[0], pair.at[1], last[0], last[1], swaps.at[0], ls.at[1]
     )
     to_out.start()
-    gathers[1].forward(2)
+    gathers[1].step(2)
     stores = [None, None]
     for i in range(6):
         k = i % 2
@@ -1027,13 +1189,14 @@
         )
         stores[k].start()
         stream.norms(i, i // 2, (6 + k) * 1024)
-        if i == 1:
-            gathers[1].forward_from(3)
+        if i == 0:
+            gathers[2].step(1)
+        elif i == 1:
+            gathers[1].step(3)
         elif i == 3:
-            gathers[2].forward(1)
-        elif i == 4:
-            gathers[2].forward(2)
-    gathers[2].forward_from(3)
+            gathers[2].step(2)
+        elif i == 5:
+            gathers[2].step(3)
     for cp in stores:
         cp.wait()
     stream = Stream(H, load, (w_in, m_in, s_in), 12, sums_ref.at[0])
@@ -1047,7 +1210,9 @@
         d = jnp.zeros((large, width), F32)
         for m in range(M):
             cols = slice(m * C, (m + 1) * C)
-            w = jnp.concatenate([v[b, :, cols] for b in range(S) for v in (wi, wg)], axis=1)
+            w = jnp.concatenate(
+                [v for b in range(S) for v in (wi[b, :, cols], wg[b // 2, b % 2, :, cols])], axis=1
+            )
             d = d + dot(dall[r, :], w, NT) * aux[r, m : m + 1]
         scaled = X[r, :].astype(F32) * aux[r, 7:8]
         gained = d * gain_mine[0:1, :]
@@ -1448,6 +1613,7 @@
     dma = pltpu.SemaphoreType.DMA
     TL, DD = args[0].shape
     chunks = T // LANES
+    zn = S // 2
     f = lambda *shape: sds(shape)
     b = lambda *shape: sds(shape, BF16)
     vf = lambda *shape: pltpu.VMEM(shape, F32)
@@ -1459,9 +1625,11 @@
         f(TL, LANES), f(8, LANES), f(M * width * 2 * S, C), f(M * S * width, C),
     )
     scratch = (
-        [vf(8, TL), vb(PN, S, TL, DD // PN), vb(PN, S, TL, DD // PN), vb(T, DD)]
-        + [vb(DD, M * C), vb(DD, M * C), vb(S, M * C, width), vf(S, 8, TL), vf(S, 8, width)]
+        [vf(8, TL), vb(PN, S, TL, DD // PN), vb(zn, 2, TL, DD // PN), vb(T, DD)]
+        + [vb(DD, M * C), vb(zn, 2 * width, M * C), vb(zn, M * C, 2 * width)]
+        + [vf(S, 8, TL), vf(S, 8, width)]
         + [vb(S, M, R // S, C)]
+        + [vb(zn - 1, T, C)] * 4
         + [vf(T, C)] * 4
         + [vf(T + 8, C), vb(T, M * C), vf(T, R), vf(chunks, 2 * N, LANES)]
         + [vb(T, C), vf(T, C), vb(T, C), vb(T, R), vf(chunks, 2 * N, LANES), vf(T, C)]
@@ -1470,12 +1638,15 @@
         + [vb(T, C), vf(T, R), vf(chunks, 2 * N, LANES), vf(T, C), vf(M, R, C)]
         + [vb(T, R), vf(chunks, 2 * N, LANES), vf(T + 8, C), vb(T, R + 2 * N), vb(T, C)]
         + [vb(2, T, width), vf(S, 8, LANES), vf(8, width), vb(M * R, C)]
-        + [vb(S, width, M * C), vb(S, width, M * C), vb(S, M * C, width), vb(M, R // S, S * C)]
+        + [vb(S, width, M * C), vb(zn, 2, width, M * C), vb(zn, 2, M * C, width)]
+        + [vb(M, R // S, S * C)]
         + [vf(8, width), vb(M * C, R), vb(2 * N, M * C), vb(M, R + 2 * N, C), vb(T, width)]
         + [vb(T, width), vf(M, R // S, S * C), vb(S * C // 2, T), vf(2, M, 2, 8, LANES)]
         + [vf(n, 8, LANES), vf(8, LANES), dma((2,)), dma((2, 3)), dma((2,))]
         + [vb(4, T // 2, width), dma((2, 2))]
-        + Spread.semaphores(S) * 2
+        + Spread.semaphores(S)
+        + FeatureGather.semaphores(S)
+        + [dma((zn,))] * 4
         + [dma((S,))] * 12
         + [dma((6,))]
         + sum_scratch(S, PN, T)
@@ -1680,7 +1851,7 @@
 def channels_fit(mesh):
     S, PN = mesh.shape["seq"], mesh.shape["tp"]
     n = S * PN
-    return PN == 4 and S % 4 == 0 and (2 * N) % n == 0 and D * 2 // n == LANES
+    return PN == 4 and S == 2 * PN and (2 * N) % n == 0 and D * 2 // n == LANES
 
 
 def solution(mesh):

time: 365 us -> 319 us (0.87)
  Pallas kernels: 361 us -> 314 us
    pallas_call x1, Pallas kernels: 318 us -> 272 us  [block_call(): pl.pallas_call(functools.partial(block_kernel, S, PN), out_shape=out, in_...]
where the time goes in v4:
time: 319 us; the launch traced here: 318 us
  Pallas kernels  314 us (98%)
    pallas_call x1, Pallas kernels, block_call(): pl.pallas_call(functools.partial(block_kernel, S, PN), out_shape=out, in_...  272 us
    pallas_call x2, Pallas kernels, update(): pl.pallas_call(kernel, out_shape=(sds((total, C)),) * 4, grid=(total // r...  38.2 us

profile of v4, /device:TPU:0, one launch (start us, length us, event | category | flops | bytes accessed | tf_op | source)
XLA Modules:
  0.0 318.0 jit_solution(4329362316567345453)
XLA Ops:
  0.7 0.9 fusion.3
  1.6 0.1 stack.32
  1.6 1.0 copy.77.refs_4_
  2.6 0.7 convert_element_type.2
  3.3 0.6 broadcast_in_dim.19.refs_2_
  3.9 271.9 %shard_map.467 = (bf16[4,128,256]{2,1,0:T(8,128)(2,1)}, bf16[4,128,256]{2,1,0:T(8,128)(2,1)}, f32[4,8,256]{2,1,0:T(8,128)}, f32[32,8,128]{2,1,0:T(8,128)}, f32[8...) custom-call(bf16[128,2048]{1,0:T(8,128)(2,1)} %tok.1, ...), custom_call_target="tpu_custom_call" | custom-call | tf_op jit(solution)/shard_map/pallas_call | solution.py:1658
  275.8 4.1 %shard_map.468 = (f32[128,512]{1,0:T(8,128)}, f32[128,512]{1,0:T(8,128)}, f32[3,160,128]{2,1,0:T(8,128)}, f32[3,160,128]{2,1,0:T(8,128)}, f32[3,160,128]{2,1,0:T...) custom-call(bf16[128,2048]{1,0:T(8,128)(2,1)} %tok.1, ...), custom_call_target="tpu_custom_call" | custom-call | tf_op jit(solution)/shard_map/pallas_call | solution.py:1833
  279.9 24.9 %shard_map.469 = (f32[12288,128]{1,0:T(8,128)}, f32[12288,128]{1,0:T(8,128)}, f32[12288,128]{1,0:T(8,128)}, f32[12288,128]{1,0:T(8,128)}) custom-call(f32[8,128]{1,0:T(8,128)} %get-tuple-element.68.scale.refs_0_, f32[12288,128]{1,0:T(8,128)} %get-tuple-element.76.refs_1_, f32[12288,128]{1,0:T(8,128)} %bitcast.100, f32[12288,128]{1,0:T(8,128)} %bitcast.102, ...), custom_call_target="tpu_custom_call" | custom-call | tf_op jit(solution)/shard_map/pallas_call | solution.py:1699
  304.7 13.3 %shard_map.470 = (f32[6144,128]{1,0:T(8,128)}, f32[6144,128]{1,0:T(8,128)}, f32[6144,128]{1,0:T(8,128)}, f32[6144,128]{1,0:T(8,128)}) custom-call(f32[8,128]{1,0:T(8,128)} %get-tuple-element.68.scale.refs_0_, f32[6144,128]{1,0:T(8,128)} %get-tuple-element.80.refs_1_, f32[6144,128]{1,0:T(8,128)} %bitcast.106, f32[6144,128]{1,0:T(8,128)} %bitcast.108, ...), custom_call_target="tpu_custom_call" | custom-call | tf_op jit(solution)/shard_map/pallas_call | solution.py:1699
  (2 shorter events, 0.0 us)

commit v5 on v4

--- a/solution.py
+++ b/solution.py
@@ -966,9 +966,6 @@
         return 0
 
     lax.fori_loop(0, S, norm, 0)
-    for cp in inners:
-        cp.wait()
-
     big = 256
     features = pl.ds(pl.multiple_of(z * 2 * width, 2 * width), 2 * width)
 
@@ -999,6 +996,17 @@
             return 0
 
         lax.fori_loop(0, T // big, body, 0)
+
+    gate_swap.wait()
+    gate_part(1)
+    gates[0].start()
+    gate_part(2)
+    gates[1].start()
+    gate_part(3)
+    gates[2].start()
+    gate_part(0)
+    for cp in inners:
+        cp.wait()
 
     pad[0:8, :] = jnp.zeros((8, C), F32)
 
@@ -1032,29 +1040,21 @@
     cotangent.far()
 
     def during_first():
-        gate_swap.wait()
-        gate_part(1)
-        gates[0].start()
-        gate_part(2)
-        gates[1].start()
-        gate_part(3)
-        gate_part(0)
-
-    def during_second():
-        gates[2].start()
         cotangent.finish()
         out_swap.wait()
         back_part(1)
+        back_part(2)
+        back_part(3)
+
+    def during_second():
         backs[0].start()
+        backs[1].start()
+        back_part(0)
 
     sum_over_all(
         S, PN, lr, bcp, low, bct, *sums, between=(during_first, during_second)
     )
-    back_part(2)
-    backs[1].start()
-    back_part(3)
     backs[2].start()
-    back_part(0)
     for cp in dts:
         cp.wait()
     for m in range(M):
@@ -1202,18 +1202,41 @@
     stream = Stream(H, load, (w_in, m_in, s_in), 12, sums_ref.at[0])
     stream.start(0)
     gathers[1].finish()
+    spare = 6 * 1024 + 2 * width * stride
+
+    def half_product(r, h, m):
+        cols = slice(m * C, (m + 1) * C)
+        v = jnp.concatenate(
+            [dall[r, (2 * b + h) * C : (2 * b + h + 1) * C] for b in range(S)], axis=1
+        )
+        pieces = [wg[b // 2, b % 2, :, cols] if h else wi[b, :, cols] for b in range(S)]
+        return dot(v, jnp.concatenate(pieces, axis=1), NT)
+
+    def gate_back(i, _):
+        r = pl.ds(pl.multiple_of(i * large, large), large)
+        d = half_product(r, 1, 0) * aux[r, 0:1]
+        for m in range(1, M):
+            d = d + half_product(r, 1, m) * aux[r, m : m + 1]
+        for t in range(tiles):
+            at = pl.ds(pl.multiple_of(spare + t * T + i * large, large), large)
+            H[at, :] = d[:, t * LANES : (t + 1) * LANES]
+        return 0
+
+    lax.fori_loop(0, T // large, gate_back, 0)
     gathers[2].finish()
 
     def normed_back(i, total):
         r = pl.ds(pl.multiple_of(i * large, large), large)
 
-        d = jnp.zeros((large, width), F32)
+        d = jnp.concatenate(
+            [
+                H[pl.ds(pl.multiple_of(spare + t * T + i * large, large), large), :]
+                for t in range(tiles)
+            ],
+            axis=1,
+        )
         for m in range(M):
-            cols = slice(m * C, (m + 1) * C)
-            w = jnp.concatenate(
-                [v for b in range(S) for v in (wi[b, :, cols], wg[b // 2, b % 2, :, cols])], axis=1
-            )
-            d = d + dot(dall[r, :], w, NT) * aux[r, m : m + 1]
+            d = d + half_product(r, 0, m) * aux[r, m : m + 1]
         scaled = X[r, :].astype(F32) * aux[r, 7:8]
         gained = d * gain_mine[0:1, :]
         part[1, r, :] = gained.astype(BF16)
@@ -1667,13 +1690,12 @@
     )(*args)
 
 
-def update_kernel(steps, scale, g, w, m, s, avg, nw, nm, ns, na, which):
-    k = lax.div(pl.program_id(0), steps)
+def update_rows(scale, which, k, g, w, m, s, avg, nw, nm, ns, na):
     factor = scale[0:1, M * which : M * which + 1]
     for i in range(1, M):
         lane = M * which + i
         factor = jnp.where(k == i, scale[0:1, lane : lane + 1], factor)
-    rows = 256
+    rows = 128
 
     def body(t, _):
         r = pl.ds(pl.multiple_of(t * rows, rows), rows)
@@ -1689,21 +1711,39 @@
     lax.fori_loop(0, w.shape[0] // rows, body, 0)
 
 
-def update(which, rows, scale, *arrays):
-    total, C = arrays[0].shape
-    block = pl.BlockSpec((rows, C), lambda i: (i, 0))
-
-    def kernel(*refs):
-        update_kernel(total // M // rows, *refs, which)
-
+def update_kernel(S, PN, count, outs, *refs):
+    ins, outputs, scratch = refs[: 10 + count], refs[10 + count : 18 + count + outs], refs[18 + count + outs :]
+    scale = ins[10 + 6]
+    step = pl.program_id(0)
+    k = lax.div(step, pl.num_programs(0) // M)
+    update_rows(scale, 0, k, *ins[0:5], *outputs[0:4])
+    update_rows(scale, 3, k, *ins[5:10], *outputs[4:8])
+
+    @pl.when(step == 2)
+    def _():
+        rest_kernel(S, PN, *ins[10:], *outputs[8:], *scratch)
+
+
+def update_all(S, PN, in_rows, out_rows, rest, rest_out, scratch):
+    steps = 2 * M
+
+    def piece(v):
+        return pl.BlockSpec((v.shape[0] // steps, v.shape[1]), lambda i: (i, 0))
+
+    def whole(v):
+        return pl.BlockSpec(v.shape, lambda i: (0,) * len(v.shape))
+
+    arrays = (*in_rows, *out_rows)
+    new = (sds(in_rows[0].shape),) * 4 + (sds(out_rows[0].shape),) * 4
     return pl.pallas_call(
-        kernel,
-        out_shape=(sds((total, C)),) * 4,
-        grid=(total // rows,),
-        in_specs=[pl.BlockSpec((8, LANES), lambda i: (0, 0))] + [block] * 5,
-        out_specs=[block] * 4,
+        functools.partial(update_kernel, S, PN, len(rest), len(rest_out)),
+        out_shape=new + tuple(rest_out),
+        grid=(steps,),
+        in_specs=[piece(v) for v in arrays] + [whole(v) for v in rest],
+        out_specs=[piece(v) for v in new] + [whole(v) for v in rest_out],
+        scratch_shapes=scratch,
         compiler_params=pltpu.CompilerParams(vmem_limit_bytes=VMEM_LIMIT),
-    )(scale, *arrays)
+    )(*arrays, *rest)
 
 
 def rest_kernel(
@@ -1826,22 +1866,26 @@
         ),
         T, C, width,
     )
-    new_in = [from_rows(v, S, w_in.shape) for v in update(0, 4096, scale, g_in, *ins)]
-    new_out = [from_tiles(v, w_out.shape) for v in update(3, 1024, scale, g_out, *outs)]
     like = lambda v: sds(v.shape)
     vec = sds((1, width))
-    rest = local_call(
-        functools.partial(rest_kernel, S, PN),
+    everything = update_all(
+        S,
+        PN,
+        (g_in, *ins),
+        (g_out, *outs),
+        (
+            tokens, out_grad, LO, DN, ROW, INV, scale, gx, MORE, gtap, gch, GG,
+            *xs, w_dt, moment_dt, square_dt, average_dt,
+            channel, moment_channel, square_channel, average_channel,
+            row(norm_gain), row(moment_gain), row(square_gain), row(average_gain),
+        ),
         (sds(out_grad.shape),) * 2 + (like(xs[0]),) * 4 + (like(w_dt),) * 4 + (like(channel),) * 4
         + (vec,) * 4,
-        28,
         [pltpu.VMEM(channel.shape, F32), pltpu.VMEM(w_dt.shape, F32)],
-    )(
-        tokens, out_grad, LO, DN, ROW, INV, scale, gx, MORE, gtap, gch, GG,
-        *xs, w_dt, moment_dt, square_dt, average_dt,
-        channel, moment_channel, square_channel, average_channel,
-        row(norm_gain), row(moment_gain), row(square_gain), row(average_gain),
-    )
+    )
+    new_in = [from_rows(v, S, w_in.shape) for v in everything[0:4]]
+    new_out = [from_tiles(v, w_out.shape) for v in everything[4:8]]
+    rest = everything[8:]
     new_x, new_dt, new_ch, new_g = [rest[2 + 4 * k : 6 + 4 * k] for k in range(4)]
     new_x = [jnp.transpose(v, (0, 2, 1)) for v in new_x]
     groups = [(new_in[k], new_x[k], new_dt[k], new_out[k], new_ch[k], new_g[k][0]) for k in range(4)]

time: 319 us -> 308 us (0.966)
  Pallas kernels: 314 us -> 303 us
    pallas_call x1, Pallas kernels: 272 us -> 266 us  [block_call(): pl.pallas_call(functools.partial(block_kernel, S, PN), out_shape=out, in_...]
    pallas_call x3 -> x1, Pallas kernels: 42.2 us -> 37.9 us  [update_all(): pl.pallas_call(functools.partial(update_kernel, S, PN, len(rest), len(res...]
where the time goes in v5:
time: 308 us; the launch traced here: 307 us
  Pallas kernels  303 us (98%)
    pallas_call x1, Pallas kernels, block_call(): pl.pallas_call(functools.partial(block_kernel, S, PN), out_shape=out, in_...  266 us
    pallas_call x1, Pallas kernels, update_all(): pl.pallas_call(functools.partial(update_kernel, S, PN, len(rest), len(res...  37.9 us

profile of v5, /device:TPU:0, one launch (start us, length us, event | category | flops | bytes accessed | tf_op | source)
XLA Modules:
  0.0 307.5 jit_solution(2313406943295333340)
XLA Ops:
  0.7 0.7 convert_element_type.2
  1.3 0.6 broadcast_in_dim.19.refs_2_
  1.9 0.9 fusion.3
  2.8 0.1 stack.32
  2.9 1.0 copy.77.refs_4_
  3.9 265.5 %shard_map.467 = (bf16[4,128,256]{2,1,0:T(8,128)(2,1)}, bf16[4,128,256]{2,1,0:T(8,128)(2,1)}, f32[4,8,256]{2,1,0:T(8,128)}, f32[32,8,128]{2,1,0:T(8,128)}, f32[8...) custom-call(bf16[128,2048]{1,0:T(8,128)(2,1)} %refs_10_.3, ...), custom_call_target="tpu_custom_call" | custom-call | tf_op jit(solution)/shard_map/pallas_call | solution.py:1681
  269.4 37.9 %shard_map.468 = (f32[12288,128]{1,0:T(8,128)}, f32[12288,128]{1,0:T(8,128)}, f32[12288,128]{1,0:T(8,128)}, f32[12288,128]{1,0:T(8,128)}, f32[6144,128]{1,0:T(8,...) custom-call(f32[12288,128]{1,0:T(8,128)} %get-tuple-element.64.refs_, ...), custom_call_target="tpu_custom_call" | custom-call | tf_op jit(solution)/shard_map/pallas_call | solution.py:1738
  (2 shorter events, 0.0 us)

commit v6 on v5

--- a/solution.py
+++ b/solution.py
@@ -445,7 +445,7 @@
         return 0
 
     lax.fori_loop(1, n, greet, 0)
-    pl.semaphore_wait(bar, n - 1)
+    return lambda: pl.semaphore_wait(bar, n - 1)
 
 
 class Spread:
@@ -846,6 +846,7 @@
     C = act.shape[1]
     rows = 128
 
+    wait_for_all = greet_all(S, PN)
     load_in = pltpu.make_async_copy(w_in, H.at[0 : w_in.shape[0]], stage.at[0])
     load_in.start()
     wide = tok[...].astype(F32)
@@ -856,7 +857,6 @@
     )
     gain_mine[...] = jnp.broadcast_to(gain[...], gain_mine.shape)
     wdt_mine[...] = w_dt[...].astype(BF16)
-    greet_all(S, PN)
     chans = lambda d: pl.ds(pl.multiple_of(d * C, LANES), C)
     block = lambda d: pl.ds(pl.multiple_of(d * width, width), width)
     tokens = Spread(
@@ -888,6 +888,7 @@
     gates = [along(k, gsend, grecv, parts_sems[0:2]) for k in range(1, zn)]
     backs = [along(k, osend, orecv, parts_sems[2:4]) for k in range(1, zn)]
     cotangent = FeatureGather(S, PN, og, ogz, *ag2)
+    wait_for_all()
     for cp in small:
         cp.start()
     tokens.start()
@@ -897,7 +898,7 @@
         for b in range(S):
             r = pl.ds(m * width * stride + 2 * b, width, stride=stride)
             wi[b, :, m * C : (m + 1) * C] = H[r, :].astype(BF16)
-    for cp in inners + dts:
+    for cp in inners[::-1] + dts:
         cp.start()
     cotangent.start()
     for m in range(M):
@@ -966,7 +967,7 @@
         return 0
 
     lax.fori_loop(0, S, norm, 0)
-    big = 256
+    big = 512
     features = pl.ds(pl.multiple_of(z * 2 * width, 2 * width), 2 * width)
 
     def gate_part(k):

time: 308 us -> 307 us (level)
  no operation moved by 1% of the time
where the time goes in v6:
time: 307 us
  Pallas kernels  303 us (99%)
    pallas_call x1, Pallas kernels, block_call(): pl.pallas_call(functools.partial(block_kernel, S, PN), out_shape=out, in_...  265 us
    pallas_call x1, Pallas kernels, update_all(): pl.pallas_call(functools.partial(update_kernel, S, PN, len(rest), len(res...  37.9 us

profile of v6, /device:TPU:0, one launch (start us, length us, event | category | flops | bytes accessed | tf_op | source)
XLA Modules:
  0.0 306.8 jit_solution(7511462456919861472)
XLA Ops:
  0.7 0.7 convert_element_type.2
  1.3 0.6 broadcast_in_dim.19.refs_2_
  1.9 0.9 fusion.3
  2.8 0.1 stack.32
  2.9 1.0 copy.77.refs_4_
  3.9 264.8 %shard_map.467 = (bf16[4,128,256]{2,1,0:T(8,128)(2,1)}, bf16[4,128,256]{2,1,0:T(8,128)(2,1)}, f32[4,8,256]{2,1,0:T(8,128)}, f32[32,8,128]{2,1,0:T(8,128)}, f32[8...) custom-call(bf16[128,2048]{1,0:T(8,128)(2,1)} %refs_10_.3, ...), custom_call_target="tpu_custom_call" | custom-call | tf_op jit(solution)/shard_map/pallas_call | solution.py:1682
  268.8 37.9 %shard_map.468 = (f32[12288,128]{1,0:T(8,128)}, f32[12288,128]{1,0:T(8,128)}, f32[12288,128]{1,0:T(8,128)}, f32[12288,128]{1,0:T(8,128)}, f32[6144,128]{1,0:T(8,...) custom-call(f32[12288,128]{1,0:T(8,128)} %get-tuple-element.64.refs_, ...), custom_call_target="tpu_custom_call" | custom-call | tf_op jit(solution)/shard_map/pallas_call | solution.py:1739
  (2 shorter events, 0.0 us)
